TPU v7x, 256 devices: a whole 4x4x8 slice. The times are simulated.
256 devices in a mesh: grp: 8 (over y, x_lo), afd: 32 (over x_hi, z, core).
Axes of the slice: x: 4 (x_hi: 2, x_lo: 2; x = x_hi * 2 + x_lo), y: 4, z: 8, core: 2. Of those that a mesh axis runs over, the one named last changes fastest.
Arguments:
- queries: bfloat16 [4096, 8192], P(('grp', 'afd')), parts along dimension 0, may hold values from -500 to 500
- key_cache: bfloat16 [4096, 128, 256], P(('grp', 'afd')), parts along dimension 0, may hold values from -4.05 to 4.05
- value_cache: bfloat16 [4096, 128, 256], P(('grp', 'afd')), parts along dimension 0, may hold values from -4 to 4
- lengths: int32 [4096], P(('grp', 'afd')), parts along dimension 0, may hold values from 2 to 128, as said below
- out_proj: bfloat16 [8192, 7168], P('afd'), may hold values from -0.375 to 0.375
- residual: bfloat16 [4096, 7168], P(('grp', 'afd')), parts along dimension 0, may hold values from -6 to 6
- routes: int32 [4096, 3], P(('grp', 'afd')), parts along dimension 0, may hold values from 0 to 47, as said below
- route_weight: float32 [4096, 3], P(('grp', 'afd')), parts along dimension 0, may hold values from 0.25 to 1
- w_gate: bfloat16 [5120, 7168], P('afd'), may hold values from -0.0625 to 0.0625
- w_up: bfloat16 [5120, 7168], P('afd'), may hold values from -0.0625 to 0.0625
- w_down: bfloat16 [5120, 7168], P('afd'), may hold values from -0.078125 to 0.078125
Outputs:
- layer_out: bfloat16 [4096, 7168], P(('grp', 'afd')), parts along dimension 0
There are 8 independent parts, one for each index of `grp`. A program takes and returns all parts, laid end to end along the dimension named above; an argument that names none is the same for every part. Nothing has to cross between parts.
Inputs may be any that keep to these rules, and one draw needn't show every extreme that they name: `routes`: each row names 3 different experts. Within the 16 rows of one device, expert 0 is named by 1 to 8 rows, and by exactly 8 rows on some device. `lengths`: some request has all 128 positions valid.
All inputs are finite; a program needn't handle non-finite values.
Results may differ from a plain program's by a relative error of at most 0.02.
Values may be sent and summed in bfloat16 or wider, within the bound.
No kernel may reach another device: no remote copies, remote signals or barrier semaphores. Data moves between devices by JAX's collectives and lax.ppermute only.
A program may use at most 128 MiB of HBM per device.

v0:
```python
import functools
import math

import jax
import jax.numpy as jnp
from jax import lax
from jax.experimental import pallas as pl
from jax.experimental.pallas import tpu as pltpu
from jax.sharding import Mesh
from jax.sharding import PartitionSpec as P

D = 7168
HS = 256
CAP = 8
NX = 2
NZ = 8
CHIPS = NX * NZ
ROWS = 16
AXES = ("y", "xlo", "xhi", "z", "core")
RING = ("xhi", "z")
VMEM_LIMIT = 16 * 1024 * 1024


def attend(queries, key_cache, value_cache, lengths):
    count_rows = queries.shape[0]
    cache_len = key_cache.shape[1]
    head_size = key_cache.shape[2]
    num_heads = queries.shape[1] // head_size
    grouped = queries.reshape(count_rows, num_heads, head_size)
    scores = jnp.einsum(
        "rhd,rld->rhl", grouped, key_cache, preferred_element_type=jnp.float32
    ) / math.sqrt(head_size)
    positions = lax.broadcasted_iota(jnp.int32, (1, 1, cache_len), 2)
    scores = jnp.where(positions < lengths[:, None, None], scores, -1e30)
    largest = jnp.max(scores, axis=2, keepdims=True)
    expo = jnp.exp(scores - largest)
    weights = (expo / jnp.sum(expo, axis=2, keepdims=True)).astype(jnp.bfloat16)
    mixed = jnp.einsum("rhl,rld->rhd", weights, value_cache, preferred_element_type=jnp.float32)
    return mixed.astype(jnp.bfloat16).reshape(count_rows, num_heads * head_size)


def swap_cores(a):
    return lax.ppermute(a, "core", [(0, 1), (1, 0)])


def swap_x(a):
    return lax.ppermute(a, "xhi", [(0, 1), (1, 0)])


def shift(a, by):
    return lax.ppermute(a, "z", [(i, (i + by) % NZ) for i in range(NZ)])


def add(*terms):
    total = terms[0].astype(jnp.float32)
    for term in terms[1:]:
        total = total + term.astype(jnp.float32)
    return total


def add16(*terms):
    return add(*terms).astype(jnp.bfloat16)


def sum_z(part):
    half = part[0].shape[-1] // 2
    up, down = shift(part[3], 1), shift(part[5], -1)
    far_up, far_down = shift(part[4][..., :half], 2), shift(part[4][..., half:], -2)
    up = shift(add_part(part[2], up, far_up, 0), 1)
    down = shift(add_part(part[6], down, far_down, half), -1)
    up = shift(add16(part[1], up), 1)
    down = shift(add16(part[7], down), -1)
    return part[0], up, down


def add_part(whole, other, piece, at):
    size = piece.shape[-1]
    rest = whole.shape[-1] - size - at
    piece = jnp.pad(piece, ((0, 0), (at, rest)))
    return add16(whole, other, piece)


def sum_z_x(part):
    rows = part.shape[0] // CHIPS
    both = NX * rows
    got = add16(*sum_z([part[k * both : (k + 1) * both] for k in range(NZ)]))
    return add(got[:rows], swap_x(got[rows:]))


def gather_z(mine):
    half = mine.shape[-1] // 2
    a1, b1 = shift(mine, 1), shift(mine, -1)
    a2, b2 = shift(a1, 1), shift(b1, -1)
    a3, b3 = shift(a2, 1), shift(b2, -1)
    a4, b4 = shift(a3[..., :half], 1), shift(b3[..., half:], -1)
    return [mine, b1, b2, b3, a4, b4, a3, a2, a1]


def project_kernel(tile, place, a_own, a_oth, w_own, w_oth, out, own, oth):
    for rz in range(NZ):
        for rx in range(NX):
            x = lax.rem(place[0] + rx, NX)
            z = lax.rem(place[1] + rz, NZ)
            chip = x * NZ + z
            own[rz * NX + rx] = a_own[chip].astype(jnp.float32)
            oth[rz * NX + rx] = a_oth[chip].astype(jnp.float32)
    rows = out.shape[0]
    first = own[...].reshape(rows, own.shape[2]).astype(jnp.bfloat16)
    second = oth[...].reshape(rows, oth.shape[2]).astype(jnp.bfloat16)

    @pl.loop(0, D // tile)
    def _(i):
        at = pl.ds(pl.multiple_of(i * tile, tile), tile)
        total = jnp.dot(first, w_own[:, at], preferred_element_type=jnp.float32)
        total += jnp.dot(second, w_oth[:, at], preferred_element_type=jnp.float32)
        out[:, at] = total.astype(jnp.bfloat16)


def project(place, attended, w_own, w_oth, tile=512):
    chips, count, _ = attended.shape
    depth = w_own.shape[0]
    whole = pl.BlockSpec(memory_space=pltpu.VMEM)
    return pl.pallas_call(
        functools.partial(project_kernel, tile),
        out_shape=jax.ShapeDtypeStruct((chips * count, D), jnp.bfloat16),
        grid_spec=pltpu.PrefetchScalarGridSpec(
            num_scalar_prefetch=1,
            grid=(1,),
            in_specs=[
                pl.BlockSpec((chips, count, depth), lambda i, s: (0, 0, s[2])),
                pl.BlockSpec((chips, count, depth), lambda i, s: (0, 0, 1 - s[2])),
                whole,
                whole,
            ],
            out_specs=whole,
            scratch_shapes=[
                pltpu.VMEM((chips, count, depth), jnp.float32),
                pltpu.VMEM((chips, count, depth), jnp.float32),
            ],
        ),
        compiler_params=pltpu.CompilerParams(vmem_limit_bytes=VMEM_LIMIT),
        name="project",
    )(place, attended, attended, w_own, w_oth)


def expert_kernel(tile, *refs):
    pieces, (g_own, g_oth, u_own, u_oth, d_own, d_oth, out) = refs[:9], refs[9:]
    steps, units = D // tile, g_own.shape[0]
    dims = (((1,), (1,)), ((), ()))
    rows = out.shape[0]
    gate = jnp.zeros((rows, 2 * units), jnp.float32)
    up = jnp.zeros((rows, 2 * units), jnp.float32)
    for i in range(steps):
        at = slice(i * tile, (i + 1) * tile)
        if i < steps // 2:
            far = pieces[4][:, at]
        else:
            far = pieces[5][:, i * tile - D // 2 : (i + 1) * tile - D // 2]
        near = [p[:, at] for p in pieces[:4]]
        back = [p[:, at] for p in pieces[6:]]
        piece = jnp.concatenate(near + [far] + back, axis=0)
        g = jnp.concatenate([g_own[:, at], g_oth[:, at]], axis=0)
        u = jnp.concatenate([u_own[:, at], u_oth[:, at]], axis=0)
        gate += lax.dot_general(piece, g, dims, preferred_element_type=jnp.float32)
        up += lax.dot_general(piece, u, dims, preferred_element_type=jnp.float32)
    act = (gate / (1.0 + jnp.exp(-gate)) * up).astype(jnp.bfloat16)

    @pl.loop(0, steps)
    def _(i):
        at = pl.ds(pl.multiple_of(i * tile, tile), tile)
        d = jnp.concatenate([d_own[:, at], d_oth[:, at]], axis=0)
        out[:, at] = jnp.dot(act, d, preferred_element_type=jnp.float32).astype(jnp.bfloat16)


def expert(pieces, weights, tile=896):
    whole = pl.BlockSpec(memory_space=pltpu.VMEM)
    return pl.pallas_call(
        functools.partial(expert_kernel, tile),
        out_shape=jax.ShapeDtypeStruct((CHIPS * CAP, D), jnp.bfloat16),
        in_specs=[whole] * (len(pieces) + len(weights)),
        out_specs=whole,
        compiler_params=pltpu.CompilerParams(vmem_limit_bytes=VMEM_LIMIT),
        name="expert",
    )(*pieces, *weights)


def slots(routes):
    named = jnp.any(routes == 0, axis=1)
    row = jnp.arange(ROWS)
    before = row[:, None] < row[None, :]
    n_named = jnp.sum(named)
    rank_named = jnp.sum((before & named[:, None]).astype(jnp.int32), axis=0)
    slot = jnp.where(named, rank_named, n_named + row - rank_named)
    return row[:, None] == slot[None, :]


def body(
    queries,
    key_cache,
    value_cache,
    lengths,
    out_proj,
    residual,
    routes,
    route_weight,
    w_gate,
    w_up,
    w_down,
):
    place = jnp.stack([lax.axis_index(a) for a in ("xhi", "z", "core")]).astype(jnp.int32)
    o_oth = swap_cores(out_proj)
    g_oth, u_oth, d_oth = swap_cores(w_gate), swap_cores(w_up), swap_cores(w_down)

    order = slots(routes)
    order16 = order.astype(jnp.bfloat16)
    share = jnp.sum(jnp.where(routes == 0, route_weight, 0.0), axis=1)
    share = jnp.sum(jnp.where(order, share[None, :], 0.0), axis=1)

    attended = attend(queries, key_cache, value_cache, lengths)
    attended = jnp.dot(order16, attended, preferred_element_type=jnp.float32).astype(jnp.bfloat16)
    by_heads = lax.all_to_all(
        attended.reshape(2, CAP, CHIPS, 2 * HS), RING, split_axis=2, concat_axis=1
    )
    by_heads, o_oth, g_oth, u_oth, d_oth = lax.optimization_barrier(
        (by_heads, o_oth, g_oth, u_oth, d_oth)
    )
    res = jnp.dot(order16, residual, preferred_element_type=jnp.float32)

    chosen_part = project(place, by_heads[0], out_proj, o_oth)
    fixed = place * jnp.array([1, 0, 1], jnp.int32)
    other_part = project(fixed, by_heads[1], out_proj, o_oth)
    other_part = lax.psum_scatter(other_part, "z", scatter_dimension=0, tiled=True)

    chosen = res[:CAP] + sum_z_x(chosen_part)
    normed = (
        chosen * lax.rsqrt(jnp.mean(chosen * chosen, axis=1, keepdims=True) + 1e-06)
    ).astype(jnp.bfloat16)
    pieces = gather_z(jnp.concatenate([normed, swap_x(normed)], axis=0))
    rows = expert(pieces, (w_gate, g_oth, w_up, u_oth, w_down, d_oth))
    expert_rows = sum_z_x(rows)
    others = res[CAP:] + add(other_part[:CAP], swap_x(other_part[CAP:]))
    done = jnp.concatenate(
        [chosen + share[:CAP, None] * expert_rows, others], axis=0
    ).astype(jnp.bfloat16)
    return jnp.dot(order16.T, done, preferred_element_type=jnp.float32).astype(jnp.bfloat16)


def solution(mesh):
    fine = Mesh(mesh.devices.reshape(4, 2, NX, NZ, 2), AXES)
    rows, weights = P(AXES, None), P(("xhi", "z", "core"), None)
    placed = (
        rows,
        P(AXES, None, None),
        P(AXES, None, None),
        P(AXES),
        weights,
        rows,
        rows,
        rows,
        weights,
        weights,
        weights,
    )
    return jax.shard_map(body, mesh=fine, in_specs=placed, out_specs=rows, check_vma=False)
```

profile of v0, /device:TPU:24, one launch (start us, length us, event | category | flops | bytes accessed | tf_op | source)
XLA Modules:
  0.0 224.1 jit_solution(3850966772243666728)
XLA Ops:
  7.6 1.0 copy.17
  9.3 1.7 fusion.3
  12.0 2.7 %convolution_convert_fusion.2 = bf16[16,32,256]{2,1,0:T(8,128)(2,1)} fusion(bf16[16,128,256]{2,1,0:T(8,128)(2,1)S(1)} %copy-done, f32[16,32]{1,0:T(8,128)S(1)} %fusion.21, f32[16,32,128]{2,1,0:T(8,128)} %copy-done.10), kind=kOutput, calls=%fused_computation.4 | convolution fusion | flops 33882752 | bytes 1574912 | tf_op jit(solution)/shard_map/rhl,rld->rhd/dot_general | solution.py:38
  14.7 1.8 copy.18
  18.0 1.2 convolution_convert_fusion
  19.9 11.1 %all-to-all-start = ((bf16[2,1,8,16,512]{4,2,0,1,3:T(8,128)(2,1)}), bf16[2,1,8,16,512]{4,2,0,1,3:T(8,128)(2,1)}, u32[]{:S(2)}, u32[]{:S(2)}) async-start(bf16[2,1,8,16,512]{4,2,0,1,3:T(8,128)(2,1)} %copy.15), calls=%async_computation | async-start | bytes 524288 | tf_op jit(solution)/shard_map/all_to_all | solution.py:221
  31.1 11.7 %all-to-all-done = bf16[2,1,8,16,512]{4,2,0,1,3:T(8,128)(2,1)} async-done(((bf16[2,1,8,16,512]{4,2,0,1,3:T(8,128)(2,1)}), bf16[2,1,8,16,512]{4,2,0,1,3:T(8,128)(2,1)}, u32[]{:S(2)}, u32[]{:S(2)}) %all-to-all-start) | async-done | bytes 262176 | tf_op jit(solution)/shard_map/all_to_all | solution.py:221
  42.8 1.0 copy.20
  43.8 2.8 %copy-done.1 = bf16[256,7168]{1,0:T(8,128)(2,1)S(1)} copy-done((bf16[256,7168]{1,0:T(8,128)(2,1)S(1)}, bf16[256,7168]{1,0:T(8,128)(2,1)}, u32[]{:S(2)}) %copy-start.1) | copy-done | bytes 3670040
  46.6 5.9 %project.2 = bf16[128,7168]{1,0:T(8,128)(2,1)S(1)} custom-call(s32[3]{0:T(128)S(1)} %get-tuple-element.18.place, bf16[16,8,512]{2,1,0:T(8,128)(2,1)S(1)} %get-tuple-element.33.a_own.a_oth, bf16[16,8,512]{2,1,0:T(8,128)(2,1)S(1)} %get-tuple-element.33.a_own.a_oth, bf16[256,7168]{1,0:T(8,128)(2,1)S(1)} %copy-done.1, bf16[256,7168]{1,0:T(8,128)(2,1)} %collective-permute-done.w_oth), custom_call_target="tpu_custom_call" | custom-call | tf_op jit(solution)/shard_map/project/pallas_call | solution.py:123
  52.6 1.9 collective-permute-start.4
  54.6 1.2 collective-permute-start.5
  55.8 2.5 %collective-permute-start.8 = (bf16[16,7168]{1,0:T(8,128)(2,1)S(1)}, bf16[16,7168]{1,0:T(8,128)(2,1)S(1)}, u32[]{:S(2)}, u32[]{:S(2)}) collective-permute-start(bf16[16,7168]{1,0:T(8,128)(2,1)S(1)} %get-tuple-element.30), channel_id=1, source_target_pairs={{0,14},{2,0},{4,2},{6,4},{8,6},{10,8},{12,10},{14,12},{1,15},{3,1}... | collective-permute-start | bytes 688136 | tf_op jit(solution)/shard_map/ppermute | solution.py:51
  58.3 8.4 %collective-permute-done.5 = bf16[16,3584]{1,0:T(8,128)(2,1)S(1)} collective-permute-done((bf16[16,3584]{1,0:T(8,128)(2,1)S(1)}, bf16[16,3584]{1,0:T(8,128)(2,1)S(1)}, u32[]{:S(2)}, u32[]{:S(2)}) %collective-permute-start.5) | collective-permute-done | bytes 114720 | tf_op jit(solution)/shard_map/ppermute | solution.py:51
  67.4 7.5 %collective-permute-done.9 = bf16[16,3584]{1,0:T(8,128)(2,1)S(1)} collective-permute-done((bf16[16,3584]{1,0:T(8,128)(2,1)S(1)}, bf16[16,3584]{1,0:T(8,128)(2,1)S(1)}, u32[]{:S(2)}, u32[]{:S(2)}) %collective-permute-start.9) | collective-permute-done | bytes 114720 | tf_op jit(solution)/shard_map/ppermute | solution.py:51
  75.0 4.1 %collective-permute-start.10 = (bf16[16,7168]{1,0:T(8,128)(2,1)S(1)}, bf16[16,7168]{1,0:T(8,128)(2,1)S(1)}, u32[]{:S(2)}, u32[]{:S(2)}) collective-permute-start(bf16[16,7168]{1,0:T(8,128)(2,1)S(1)} %get-tuple-element.26), channel_id=1, source_target_pairs={{0,14},{2,0},{4,2},{6,4},{8,6},{10,8},{12,10},{14,12},{1,15},{3,1}... | collective-permute-start | bytes 688136 | tf_op jit(solution)/shard_map/ppermute | solution.py:51
  79.1 5.0 %collective-permute-done.10 = bf16[16,7168]{1,0:T(8,128)(2,1)S(1)} collective-permute-done((bf16[16,7168]{1,0:T(8,128)(2,1)S(1)}, bf16[16,7168]{1,0:T(8,128)(2,1)S(1)}, u32[]{:S(2)}, u32[]{:S(2)}) %collective-permute-start.10) | collective-permute-done | bytes 229408 | tf_op jit(solution)/shard_map/ppermute | solution.py:51
  84.1 3.8 %collective-permute-start.11 = (bf16[16,7168]{1,0:T(8,128)(2,1)S(1)}, bf16[16,7168]{1,0:T(8,128)(2,1)S(1)}, u32[]{:S(2)}, u32[]{:S(2)}) collective-permute-start(bf16[16,7168]{1,0:T(8,128)(2,1)S(1)} %add_convert_fusion.6), channel_id=1, source_target_pairs={{0,14},{2,0},{4,2},{6,4},{8,6},{10,8},{12,10},{14,12},{1,15},{3,1}... | collective-permute-start | bytes 688136 | tf_op jit(solution)/shard_map/ppermute | solution.py:51
  87.9 3.5 %collective-permute-done.11 = bf16[16,7168]{1,0:T(8,128)(2,1)S(1)} collective-permute-done((bf16[16,7168]{1,0:T(8,128)(2,1)S(1)}, bf16[16,7168]{1,0:T(8,128)(2,1)S(1)}, u32[]{:S(2)}, u32[]{:S(2)}) %collective-permute-start.11) | collective-permute-done | bytes 229408 | tf_op jit(solution)/shard_map/ppermute | solution.py:51
  92.1 5.9 %collective-permute-done.12 = bf16[8,7168]{1,0:T(8,128)(2,1)S(1)} collective-permute-done((bf16[8,7168]{1,0:T(8,128)(2,1)S(1)}, bf16[8,7168]{1,0:T(8,128)(2,1)S(1)}, u32[]{:S(2)}, u32[]{:S(2)}) %collective-permute-start.12) | collective-permute-done | bytes 114720 | tf_op jit(solution)/shard_map/ppermute | solution.py:47
  98.7 6.1 %collective-permute-done.13 = bf16[8,7168]{1,0:T(8,128)(2,1)S(1)} collective-permute-done((bf16[8,7168]{1,0:T(8,128)(2,1)S(1)}, bf16[8,7168]{1,0:T(8,128)(2,1)S(1)}, u32[]{:S(2)}, u32[]{:S(2)}) %collective-permute-start.13) | collective-permute-done | bytes 114720 | tf_op jit(solution)/shard_map/ppermute | solution.py:47
  104.9 3.8 %collective-permute-start.14 = (bf16[16,7168]{1,0:T(8,128)(2,1)S(1)}, bf16[16,7168]{1,0:T(8,128)(2,1)S(1)}, u32[]{:S(2)}, u32[]{:S(2)}) collective-permute-start(bf16[16,7168]{1,0:T(8,128)(2,1)S(1)} %pad_maximum_fusion.refs_0_), channel_id=1, source_target_pairs={{0,14},{2,0},{4,2},{6,4},{8,6},{10,8},{12,10},{14,12},{1,15},{3,1}... | collective-permute-start | bytes 688136 | tf_op jit(solution)/shard_map/ppermute | solution.py:51
  108.7 5.5 %collective-permute-done.17.refs_8_ = bf16[16,7168]{1,0:T(8,128)(2,1)S(1)} collective-permute-done((bf16[16,7168]{1,0:T(8,128)(2,1)S(1)}, bf16[16,7168]{1,0:T(8,128)(2,1)S(1)}, u32[]{:S(2)}, u32[]{:S(2)}) %collective-permute-start.17) | collective-permute-done | bytes 229408 | tf_op jit(solution)/shard_map/ppermute | solution.py:51
  114.2 3.6 %collective-permute-start.15 = (bf16[16,7168]{1,0:T(8,128)(2,1)S(1)}, bf16[16,7168]{1,0:T(8,128)(2,1)S(1)}, u32[]{:S(2)}, u32[]{:S(2)}) collective-permute-start(bf16[16,7168]{1,0:T(8,128)(2,1)S(1)} %collective-permute-done.14.refs_1_), channel_id=1, source_target_pairs={{0,14},{2,0},{4,2},{6,4},{8,6},{10,8},{12,10},{14,12},{1,15},{3,1}... | collective-permute-start | bytes 688136 | tf_op jit(solution)/shard_map/ppermute | solution.py:51
  117.8 4.6 %collective-permute-done.18.refs_7_ = bf16[16,7168]{1,0:T(8,128)(2,1)S(1)} collective-permute-done((bf16[16,7168]{1,0:T(8,128)(2,1)S(1)}, bf16[16,7168]{1,0:T(8,128)(2,1)S(1)}, u32[]{:S(2)}, u32[]{:S(2)}) %collective-permute-start.18) | collective-permute-done | bytes 229408 | tf_op jit(solution)/shard_map/ppermute | solution.py:51
  122.4 3.3 %collective-permute-start.16 = (bf16[16,7168]{1,0:T(8,128)(2,1)S(1)}, bf16[16,7168]{1,0:T(8,128)(2,1)S(1)}, u32[]{:S(2)}, u32[]{:S(2)}) collective-permute-start(bf16[16,7168]{1,0:T(8,128)(2,1)S(1)} %collective-permute-done.15.refs_2_), channel_id=1, source_target_pairs={{0,14},{2,0},{4,2},{6,4},{8,6},{10,8},{12,10},{14,12},{1,15},{3,1}... | collective-permute-start | bytes 688136 | tf_op jit(solution)/shard_map/ppermute | solution.py:51
  125.8 3.9 %collective-permute-done.19.refs_6_ = bf16[16,7168]{1,0:T(8,128)(2,1)S(1)} collective-permute-done((bf16[16,7168]{1,0:T(8,128)(2,1)S(1)}, bf16[16,7168]{1,0:T(8,128)(2,1)S(1)}, u32[]{:S(2)}, u32[]{:S(2)}) %collective-permute-start.19) | collective-permute-done | bytes 229408 | tf_op jit(solution)/shard_map/ppermute | solution.py:51
  129.8 3.3 %collective-permute-start.21 = (bf16[16,3584]{1,0:T(8,128)(2,1)S(1)}, bf16[16,3584]{1,0:T(8,128)(2,1)S(1)}, u32[]{:S(2)}, u32[]{:S(2)}) collective-permute-start(bf16[16,3584]{1,0:T(8,128)(2,1)S(1)} %slice.143), channel_id=1, source_target_pairs={{0,14},{2,0},{4,2},{6,4},{8,6},{10,8},{12,10},{14,12},{1,15},{3,1}... | collective-permute-start | bytes 344072 | tf_op jit(solution)/shard_map/ppermute | solution.py:51
  133.1 3.1 %collective-permute-done.20.refs_4_ = bf16[16,3584]{1,0:T(8,128)(2,1)S(1)} collective-permute-done((bf16[16,3584]{1,0:T(8,128)(2,1)S(1)}, bf16[16,3584]{1,0:T(8,128)(2,1)S(1)}, u32[]{:S(2)}, u32[]{:S(2)}) %collective-permute-start.20) | collective-permute-done | bytes 114720 | tf_op jit(solution)/shard_map/ppermute | solution.py:51
  136.2 1.6 copy-done.8
  137.9 7.9 %expert.1 = bf16[128,7168]{1,0:T(8,128)(2,1)S(1)} custom-call(bf16[16,7168]{1,0:T(8,128)(2,1)S(1)} %pad_maximum_fusion.refs_0_, bf16[16,7168]{1,0:T(8,128)(2,1)S(1)} %collective-permute-done.14.refs_1_, bf16[16,7168]{1,0:T(8,128)(2,1)S(1)} %collective-permute-done.15.refs_2_, bf16[16,7168]{1,0:T(8,128)(2,1)S(1)} %collective-permute-done.16.refs_3_, ...), custom_call_target="tpu_custom_call" | custom-call | tf_op jit(solution)/shard_map/expert/pallas_call | solution.py:177
  147.2 3.0 %collective-permute-start.23 = (bf16[16,3584]{1,0:T(8,128)(2,1)S(1)}, bf16[16,3584]{1,0:T(8,128)(2,1)S(1)}, u32[]{:S(2)}, u32[]{:S(2)}) collective-permute-start(bf16[16,3584]{1,0:T(8,128)(2,1)S(1)} %get-tuple-element.21), channel_id=1, source_target_pairs={{0,4},{2,6},{4,8},{6,10},{8,12},{10,14},{12,0},{14,2},{1,5},{3,7},... | collective-permute-start | bytes 344072 | tf_op jit(solution)/shard_map/ppermute | solution.py:51
  150.4 6.9 %collective-permute-done.23 = bf16[16,3584]{1,0:T(8,128)(2,1)S(1)} collective-permute-done((bf16[16,3584]{1,0:T(8,128)(2,1)S(1)}, bf16[16,3584]{1,0:T(8,128)(2,1)S(1)}, u32[]{:S(2)}, u32[]{:S(2)}) %collective-permute-start.23) | collective-permute-done | bytes 114720 | tf_op jit(solution)/shard_map/ppermute | solution.py:51
  158.1 0.8 collective-permute-start.27
  158.9 5.9 %project.3 = bf16[128,7168]{1,0:T(8,128)(2,1)S(1)} custom-call(s32[3]{0:T(128)S(1)} %get-tuple-element.17.place, bf16[16,8,512]{2,1,0:T(8,128)(2,1)S(1)} %get-tuple-element.34.a_own.a_oth, bf16[16,8,512]{2,1,0:T(8,128)(2,1)S(1)} %get-tuple-element.34.a_own.a_oth, bf16[256,7168]{1,0:T(8,128)(2,1)S(1)} %copy-done.2, bf16[256,7168]{1,0:T(8,128)(2,1)} %collective-permute-done.w_oth), custom_call_target="tpu_custom_call" | custom-call | tf_op jit(solution)/shard_map/project/pallas_call | solution.py:123
  164.8 1.3 copy-done.3
  166.5 1.2 add_convert_fusion.3
  167.8 2.6 %collective-permute-start.28 = (bf16[16,7168]{1,0:T(8,128)(2,1)S(1)}, bf16[16,7168]{1,0:T(8,128)(2,1)S(1)}, u32[]{:S(2)}, u32[]{:S(2)}) collective-permute-start(bf16[16,7168]{1,0:T(8,128)(2,1)S(1)} %get-tuple-element.20), channel_id=1, source_target_pairs={{0,14},{2,0},{4,2},{6,4},{8,6},{10,8},{12,10},{14,12},{1,15},{3,1}... | collective-permute-start | bytes 688136 | tf_op jit(solution)/shard_map/ppermute | solution.py:51
  170.4 1.1 collective-permute-start.25
  171.5 3.9 %collective-permute-done.28 = bf16[16,7168]{1,0:T(8,128)(2,1)S(1)} collective-permute-done((bf16[16,7168]{1,0:T(8,128)(2,1)S(1)}, bf16[16,7168]{1,0:T(8,128)(2,1)S(1)}, u32[]{:S(2)}, u32[]{:S(2)}) %collective-permute-start.28) | collective-permute-done | bytes 229408 | tf_op jit(solution)/shard_map/ppermute | solution.py:51
  175.4 2.3 %collective-permute-start.29 = (bf16[16,7168]{1,0:T(8,128)(2,1)S(1)}, bf16[16,7168]{1,0:T(8,128)(2,1)S(1)}, u32[]{:S(2)}, u32[]{:S(2)}) collective-permute-start(bf16[16,7168]{1,0:T(8,128)(2,1)S(1)} %add_convert_fusion.1), channel_id=1, source_target_pairs={{0,14},{2,0},{4,2},{6,4},{8,6},{10,8},{12,10},{14,12},{1,15},{3,1}... | collective-permute-start | bytes 688136 | tf_op jit(solution)/shard_map/ppermute | solution.py:51
  177.7 7.1 %collective-permute-done.29 = bf16[16,7168]{1,0:T(8,128)(2,1)S(1)} collective-permute-done((bf16[16,7168]{1,0:T(8,128)(2,1)S(1)}, bf16[16,7168]{1,0:T(8,128)(2,1)S(1)}, u32[]{:S(2)}, u32[]{:S(2)}) %collective-permute-start.29) | collective-permute-done | bytes 229408 | tf_op jit(solution)/shard_map/ppermute | solution.py:51
  185.7 22.2 %reduce-scatter.2.cloned.1.call-done = bf16[16,7168]{1,0:T(8,128)(2,1)} async-done(((bf16[128,7168]{1,0:T(8,128)(2,1)}), bf16[16,7168]{1,0:T(8,128)(2,1)}) %reduce-scatter.2.cloned.1.call-update) | async-done | bytes 229392 | tf_op jit(solution)/shard_map/reduce_scatter | solution.py:232
  207.9 0.9 slice.157
  208.8 2.8 %collective-permute-start.31 = (bf16[8,7168]{1,0:T(8,128)(2,1)S(1)}, bf16[8,7168]{1,0:T(8,128)(2,1)S(1)}, u32[]{:S(2)}, u32[]{:S(2)}) collective-permute-start(bf16[8,7168]{1,0:T(8,128)(2,1)S(1)} %slice.157), channel_id=1, source_target_pairs={{0,16},{16,0},{1,17},{17,1},{2,18},{18,2},{3,19},{19,3},{4,20},{20... | collective-permute-start | bytes 344072 | tf_op jit(solution)/shard_map/ppermute | solution.py:47
  211.8 3.3 %collective-permute-done.31 = bf16[8,7168]{1,0:T(8,128)(2,1)S(1)} collective-permute-done((bf16[8,7168]{1,0:T(8,128)(2,1)S(1)}, bf16[8,7168]{1,0:T(8,128)(2,1)S(1)}, u32[]{:S(2)}, u32[]{:S(2)}) %collective-permute-start.31) | collective-permute-done | bytes 114720 | tf_op jit(solution)/shard_map/ppermute | solution.py:47
  215.1 1.1 add_convert_fusion.10
  216.3 1.0 convolution_convert_fusion.1
  (97 shorter events, 11.5 us)
Async XLA Ops:
  6.5 5.4 %copy-start = (bf16[16,128,256]{2,1,0:T(8,128)(2,1)S(1)}, bf16[16,128,256]{2,1,0:T(8,128)(2,1)}, u32[]{:S(2)}) copy-start(bf16[16,128,256]{2,1,0:T(8,128)(2,1)} %param.14) | copy-start | bytes 3145732
  6.5 37.3 %collective-permute-start = (bf16[256,7168]{1,0:T(8,128)(2,1)}, bf16[256,7168]{1,0:T(8,128)(2,1)}, u32[]{:S(2)}, u32[]{:S(2)}) collective-permute-start(bf16[256,7168]{1,0:T(8,128)(2,1)} %w_own.3), channel_id=1, source_target_pairs={{0,1},{1,0},{2,3},{3,2},{4,5},{5,4},{6,7},{7,6},{8,9},{9,8},{10,11... | collective-permute-start | bytes 11010056 | tf_op jit(solution)/shard_map/ppermute | solution.py:43
  6.5 37.2 %collective-permute-start.1 = (bf16[160,7168]{1,0:T(8,128)(2,1)}, bf16[160,7168]{1,0:T(8,128)(2,1)S(1)}, u32[]{:S(2)}, u32[]{:S(2)}) collective-permute-start(bf16[160,7168]{1,0:T(8,128)(2,1)} %refs_9_.1), channel_id=1, source_target_pairs={{0,1},{1,0},{2,3},{3,2},{4,5},{5,4},{6,7},{7,6},{8,9},{9,8},{10,11... | collective-permute-start | bytes 6881288 | tf_op jit(solution)/shard_map/ppermute | solution.py:43
  7.0 36.7 %collective-permute-start.2 = (bf16[160,7168]{1,0:T(8,128)(2,1)}, bf16[160,7168]{1,0:T(8,128)(2,1)}, u32[]{:S(2)}, u32[]{:S(2)}) collective-permute-start(bf16[160,7168]{1,0:T(8,128)(2,1)} %refs_11_.1), channel_id=1, source_target_pairs={{0,1},{1,0},{2,3},{3,2},{4,5},{5,4},{6,7},{7,6},{8,9},{9,8},{10,11... | collective-permute-start | bytes 6881288 | tf_op jit(solution)/shard_map/ppermute | solution.py:43
  7.1 36.7 %collective-permute-start.3 = (bf16[160,7168]{1,0:T(8,128)(2,1)}, bf16[160,7168]{1,0:T(8,128)(2,1)}, u32[]{:S(2)}, u32[]{:S(2)}) collective-permute-start(bf16[160,7168]{1,0:T(8,128)(2,1)} %refs_13_.1), channel_id=1, source_target_pairs={{0,1},{1,0},{2,3},{3,2},{4,5},{5,4},{6,7},{7,6},{8,9},{9,8},{10,11... | collective-permute-start | bytes 6881288 | tf_op jit(solution)/shard_map/ppermute | solution.py:43
  9.3 7.2 %copy-start.13 = (f32[16,3]{0,1:T(4,128)S(1)}, f32[16,3]{0,1:T(4,128)}, u32[]{:S(2)}) copy-start(f32[16,3]{0,1:T(4,128)} %param.19) | copy-start | bytes 580
  9.3 7.2 %copy-start.14 = (s32[16,3]{0,1:T(4,128)S(1)}, s32[16,3]{0,1:T(4,128)}, u32[]{:S(2)}) copy-start(s32[16,3]{0,1:T(4,128)} %param.18) | copy-start | bytes 580
  12.0 19.0 %copy-start.15 = (s32[3]{0:T(128)S(1)}, s32[3]{0:T(128)}, u32[]{:S(2)}) copy-start(s32[3]{0:T(128)} %constant.35.clone) | copy-start | bytes 40
  19.9 22.9 %all-to-all-start = ((bf16[2,1,8,16,512]{4,2,0,1,3:T(8,128)(2,1)}), bf16[2,1,8,16,512]{4,2,0,1,3:T(8,128)(2,1)}, u32[]{:S(2)}, u32[]{:S(2)}) async-start(bf16[2,1,8,16,512]{4,2,0,1,3:T(8,128)(2,1)} %copy.15), calls=%async_computation | async-start | bytes 524288 | tf_op jit(solution)/shard_map/all_to_all | solution.py:221
  31.0 177.0 %reduce-scatter.2.cloned.1.call-start = ((), (), s32[]{:S(2)}) async-start(), calls=%async_computation.2 | async-start | bytes 2064384 | tf_op jit(solution)/shard_map/reduce_scatter | solution.py:232
  43.8 8.8 %copy-start.7 = (bf16[160,7168]{1,0:T(8,128)(2,1)}, bf16[160,7168]{1,0:T(8,128)(2,1)S(1)}, u32[]{:S(2)}) copy-start(bf16[160,7168]{1,0:T(8,128)(2,1)S(1)} %collective-permute-done.1.refs_10_) | copy-start | bytes 6881284
  43.8 2.8 %copy-start.1 = (bf16[256,7168]{1,0:T(8,128)(2,1)S(1)}, bf16[256,7168]{1,0:T(8,128)(2,1)}, u32[]{:S(2)}) copy-start(bf16[256,7168]{1,0:T(8,128)(2,1)} %w_own.3) | copy-start | bytes 11010052
  52.6 14.0 %collective-permute-start.4 = (bf16[16,7168]{1,0:T(8,128)(2,1)S(1)}, bf16[16,7168]{1,0:T(8,128)(2,1)S(1)}, u32[]{:S(2)}, u32[]{:S(2)}) collective-permute-start(bf16[16,7168]{1,0:T(8,128)(2,1)S(1)} %get-tuple-element.29), channel_id=1, source_target_pairs={{0,2},{2,4},{4,6},{6,8},{8,10},{10,12},{12,14},{14,0},{1,3},{3,5},... | collective-permute-start | bytes 688136 | tf_op jit(solution)/shard_map/ppermute | solution.py:51
  54.5 81.7 %copy-start.6 = (bf16[160,7168]{1,0:T(8,128)(2,1)S(1)}, bf16[160,7168]{1,0:T(8,128)(2,1)}, u32[]{:S(2)}) copy-start(bf16[160,7168]{1,0:T(8,128)(2,1)} %refs_13_.1) | copy-start | bytes 6881284
  54.6 12.1 %collective-permute-start.5 = (bf16[16,3584]{1,0:T(8,128)(2,1)S(1)}, bf16[16,3584]{1,0:T(8,128)(2,1)S(1)}, u32[]{:S(2)}, u32[]{:S(2)}) collective-permute-start(bf16[16,3584]{1,0:T(8,128)(2,1)S(1)} %get-tuple-element.27), channel_id=1, source_target_pairs={{0,4},{2,6},{4,8},{6,10},{8,12},{10,14},{12,0},{14,2},{1,5},{3,7},... | collective-permute-start | bytes 344072 | tf_op jit(solution)/shard_map/ppermute | solution.py:51
  55.8 19.1 %collective-permute-start.8 = (bf16[16,7168]{1,0:T(8,128)(2,1)S(1)}, bf16[16,7168]{1,0:T(8,128)(2,1)S(1)}, u32[]{:S(2)}, u32[]{:S(2)}) collective-permute-start(bf16[16,7168]{1,0:T(8,128)(2,1)S(1)} %get-tuple-element.30), channel_id=1, source_target_pairs={{0,14},{2,0},{4,2},{6,4},{8,6},{10,8},{12,10},{14,12},{1,15},{3,1}... | collective-permute-start | bytes 688136 | tf_op jit(solution)/shard_map/ppermute | solution.py:51
  66.7 25.1 %copy-start.12 = (bf16[16,7168]{1,0:T(8,128)(2,1)S(1)}, bf16[16,7168]{1,0:T(8,128)(2,1)}, u32[]{:S(2)}) copy-start(bf16[16,7168]{1,0:T(8,128)(2,1)} %param.17) | copy-start | bytes 688132
  66.7 8.1 %collective-permute-start.6 = (bf16[16,7168]{1,0:T(8,128)(2,1)S(1)}, bf16[16,7168]{1,0:T(8,128)(2,1)S(1)}, u32[]{:S(2)}, u32[]{:S(2)}) collective-permute-start(bf16[16,7168]{1,0:T(8,128)(2,1)S(1)} %add_convert_fusion.9), channel_id=1, source_target_pairs={{0,2},{2,4},{4,6},{6,8},{8,10},{10,12},{12,14},{14,0},{1,3},{3,5},... | collective-permute-start | bytes 688136 | tf_op jit(solution)/shard_map/ppermute | solution.py:51
  66.8 8.0 %collective-permute-start.9 = (bf16[16,3584]{1,0:T(8,128)(2,1)S(1)}, bf16[16,3584]{1,0:T(8,128)(2,1)S(1)}, u32[]{:S(2)}, u32[]{:S(2)}) collective-permute-start(bf16[16,3584]{1,0:T(8,128)(2,1)S(1)} %get-tuple-element.28), channel_id=1, source_target_pairs={{0,12},{2,14},{4,0},{6,2},{8,4},{10,6},{12,8},{14,10},{1,13},{3,15... | collective-permute-start | bytes 344072 | tf_op jit(solution)/shard_map/ppermute | solution.py:51
  74.9 61.3 %copy-start.5 = (bf16[160,7168]{1,0:T(8,128)(2,1)S(1)}, bf16[160,7168]{1,0:T(8,128)(2,1)}, u32[]{:S(2)}) copy-start(bf16[160,7168]{1,0:T(8,128)(2,1)} %refs_11_.1) | copy-start | bytes 6881284
  75.0 9.0 %collective-permute-start.10 = (bf16[16,7168]{1,0:T(8,128)(2,1)S(1)}, bf16[16,7168]{1,0:T(8,128)(2,1)S(1)}, u32[]{:S(2)}, u32[]{:S(2)}) collective-permute-start(bf16[16,7168]{1,0:T(8,128)(2,1)S(1)} %get-tuple-element.26), channel_id=1, source_target_pairs={{0,14},{2,0},{4,2},{6,4},{8,6},{10,8},{12,10},{14,12},{1,15},{3,1}... | collective-permute-start | bytes 688136 | tf_op jit(solution)/shard_map/ppermute | solution.py:51
  79.1 8.8 %collective-permute-start.7 = (bf16[16,7168]{1,0:T(8,128)(2,1)S(1)}, bf16[16,7168]{1,0:T(8,128)(2,1)S(1)}, u32[]{:S(2)}, u32[]{:S(2)}) collective-permute-start(bf16[16,7168]{1,0:T(8,128)(2,1)S(1)} %get-tuple-element.25), channel_id=1, source_target_pairs={{0,2},{2,4},{4,6},{6,8},{8,10},{10,12},{12,14},{14,0},{1,3},{3,5},... | collective-permute-start | bytes 688136 | tf_op jit(solution)/shard_map/ppermute | solution.py:51
  84.1 52.1 %copy-start.4 = (bf16[160,7168]{1,0:T(8,128)(2,1)S(1)}, bf16[160,7168]{1,0:T(8,128)(2,1)}, u32[]{:S(2)}) copy-start(bf16[160,7168]{1,0:T(8,128)(2,1)} %refs_9_.1) | copy-start | bytes 6881284
  84.1 7.3 %collective-permute-start.11 = (bf16[16,7168]{1,0:T(8,128)(2,1)S(1)}, bf16[16,7168]{1,0:T(8,128)(2,1)S(1)}, u32[]{:S(2)}, u32[]{:S(2)}) collective-permute-start(bf16[16,7168]{1,0:T(8,128)(2,1)S(1)} %add_convert_fusion.6), channel_id=1, source_target_pairs={{0,14},{2,0},{4,2},{6,4},{8,6},{10,8},{12,10},{14,12},{1,15},{3,1}... | collective-permute-start | bytes 688136 | tf_op jit(solution)/shard_map/ppermute | solution.py:51
  91.5 44.7 %copy-start.9 = (bf16[16,7168]{1,0:T(8,128)(2,1)}, bf16[16,7168]{1,0:T(8,128)(2,1)S(1)}, u32[]{:S(2)}) copy-start(bf16[16,7168]{1,0:T(8,128)(2,1)S(1)} %add_convert_fusion.5) | copy-start | bytes 688132
  91.6 6.4 %collective-permute-start.12 = (bf16[8,7168]{1,0:T(8,128)(2,1)S(1)}, bf16[8,7168]{1,0:T(8,128)(2,1)S(1)}, u32[]{:S(2)}, u32[]{:S(2)}) collective-permute-start(bf16[8,7168]{1,0:T(8,128)(2,1)S(1)} %slice.141), channel_id=1, source_target_pairs={{0,16},{16,0},{1,17},{17,1},{2,18},{18,2},{3,19},{19,3},{4,20},{20... | collective-permute-start | bytes 344072 | tf_op jit(solution)/shard_map/ppermute | solution.py:47
  98.2 6.6 %collective-permute-start.13 = (bf16[8,7168]{1,0:T(8,128)(2,1)S(1)}, bf16[8,7168]{1,0:T(8,128)(2,1)S(1)}, u32[]{:S(2)}, u32[]{:S(2)}) collective-permute-start(bf16[8,7168]{1,0:T(8,128)(2,1)S(1)} %multiply_convert_fusion), channel_id=1, source_target_pairs={{0,16},{16,0},{1,17},{17,1},{2,18},{18,2},{3,19},{19,3},{4,20},{20... | collective-permute-start | bytes 344072 | tf_op jit(solution)/shard_map/ppermute | solution.py:47
  104.8 9.4 %collective-permute-start.17 = (bf16[16,7168]{1,0:T(8,128)(2,1)S(1)}, bf16[16,7168]{1,0:T(8,128)(2,1)S(1)}, u32[]{:S(2)}, u32[]{:S(2)}) collective-permute-start(bf16[16,7168]{1,0:T(8,128)(2,1)S(1)} %pad_maximum_fusion.refs_0_), channel_id=1, source_target_pairs={{0,2},{2,4},{4,6},{6,8},{8,10},{10,12},{12,14},{14,0},{1,3},{3,5},... | collective-permute-start | bytes 688136 | tf_op jit(solution)/shard_map/ppermute | solution.py:51
  104.9 9.3 %collective-permute-start.14 = (bf16[16,7168]{1,0:T(8,128)(2,1)S(1)}, bf16[16,7168]{1,0:T(8,128)(2,1)S(1)}, u32[]{:S(2)}, u32[]{:S(2)}) collective-permute-start(bf16[16,7168]{1,0:T(8,128)(2,1)S(1)} %pad_maximum_fusion.refs_0_), channel_id=1, source_target_pairs={{0,14},{2,0},{4,2},{6,4},{8,6},{10,8},{12,10},{14,12},{1,15},{3,1}... | collective-permute-start | bytes 688136 | tf_op jit(solution)/shard_map/ppermute | solution.py:51
  114.2 8.3 %collective-permute-start.18 = (bf16[16,7168]{1,0:T(8,128)(2,1)S(1)}, bf16[16,7168]{1,0:T(8,128)(2,1)S(1)}, u32[]{:S(2)}, u32[]{:S(2)}) collective-permute-start(bf16[16,7168]{1,0:T(8,128)(2,1)S(1)} %collective-permute-done.17.refs_8_), channel_id=1, source_target_pairs={{0,2},{2,4},{4,6},{6,8},{8,10},{10,12},{12,14},{14,0},{1,3},{3,5},... | collective-permute-start | bytes 688136 | tf_op jit(solution)/shard_map/ppermute | solution.py:51
  114.2 8.3 %collective-permute-start.15 = (bf16[16,7168]{1,0:T(8,128)(2,1)S(1)}, bf16[16,7168]{1,0:T(8,128)(2,1)S(1)}, u32[]{:S(2)}, u32[]{:S(2)}) collective-permute-start(bf16[16,7168]{1,0:T(8,128)(2,1)S(1)} %collective-permute-done.14.refs_1_), channel_id=1, source_target_pairs={{0,14},{2,0},{4,2},{6,4},{8,6},{10,8},{12,10},{14,12},{1,15},{3,1}... | collective-permute-start | bytes 688136 | tf_op jit(solution)/shard_map/ppermute | solution.py:51
  122.4 7.2 %collective-permute-start.19 = (bf16[16,7168]{1,0:T(8,128)(2,1)S(1)}, bf16[16,7168]{1,0:T(8,128)(2,1)S(1)}, u32[]{:S(2)}, u32[]{:S(2)}) collective-permute-start(bf16[16,7168]{1,0:T(8,128)(2,1)S(1)} %collective-permute-done.18.refs_7_), channel_id=1, source_target_pairs={{0,2},{2,4},{4,6},{6,8},{8,10},{10,12},{12,14},{14,0},{1,3},{3,5},... | collective-permute-start | bytes 688136 | tf_op jit(solution)/shard_map/ppermute | solution.py:51
  122.4 7.3 %collective-permute-start.16 = (bf16[16,7168]{1,0:T(8,128)(2,1)S(1)}, bf16[16,7168]{1,0:T(8,128)(2,1)S(1)}, u32[]{:S(2)}, u32[]{:S(2)}) collective-permute-start(bf16[16,7168]{1,0:T(8,128)(2,1)S(1)} %collective-permute-done.15.refs_2_), channel_id=1, source_target_pairs={{0,14},{2,0},{4,2},{6,4},{8,6},{10,8},{12,10},{14,12},{1,15},{3,1}... | collective-permute-start | bytes 688136 | tf_op jit(solution)/shard_map/ppermute | solution.py:51
  129.7 6.5 %collective-permute-start.20 = (bf16[16,3584]{1,0:T(8,128)(2,1)S(1)}, bf16[16,3584]{1,0:T(8,128)(2,1)S(1)}, u32[]{:S(2)}, u32[]{:S(2)}) collective-permute-start(bf16[16,3584]{1,0:T(8,128)(2,1)S(1)} %slice.142), channel_id=1, source_target_pairs={{0,2},{2,4},{4,6},{6,8},{8,10},{10,12},{12,14},{14,0},{1,3},{3,5},... | collective-permute-start | bytes 344072 | tf_op jit(solution)/shard_map/ppermute | solution.py:51
  129.8 6.4 %collective-permute-start.21 = (bf16[16,3584]{1,0:T(8,128)(2,1)S(1)}, bf16[16,3584]{1,0:T(8,128)(2,1)S(1)}, u32[]{:S(2)}, u32[]{:S(2)}) collective-permute-start(bf16[16,3584]{1,0:T(8,128)(2,1)S(1)} %slice.143), channel_id=1, source_target_pairs={{0,14},{2,0},{4,2},{6,4},{8,6},{10,8},{12,10},{14,12},{1,15},{3,1}... | collective-permute-start | bytes 344072 | tf_op jit(solution)/shard_map/ppermute | solution.py:51
  136.2 1.6 copy-start.8
  137.9 21.0 %copy-start.2 = (bf16[256,7168]{1,0:T(8,128)(2,1)S(1)}, bf16[256,7168]{1,0:T(8,128)(2,1)}, u32[]{:S(2)}) copy-start(bf16[256,7168]{1,0:T(8,128)(2,1)} %w_own.3) | copy-start | bytes 11010052
  146.5 10.8 %collective-permute-start.22 = (bf16[16,7168]{1,0:T(8,128)(2,1)S(1)}, bf16[16,7168]{1,0:T(8,128)(2,1)S(1)}, u32[]{:S(2)}, u32[]{:S(2)}) collective-permute-start(bf16[16,7168]{1,0:T(8,128)(2,1)S(1)} %get-tuple-element.23), channel_id=1, source_target_pairs={{0,2},{2,4},{4,6},{6,8},{8,10},{10,12},{12,14},{14,0},{1,3},{3,5},... | collective-permute-start | bytes 688136 | tf_op jit(solution)/shard_map/ppermute | solution.py:51
  147.2 10.2 %collective-permute-start.23 = (bf16[16,3584]{1,0:T(8,128)(2,1)S(1)}, bf16[16,3584]{1,0:T(8,128)(2,1)S(1)}, u32[]{:S(2)}, u32[]{:S(2)}) collective-permute-start(bf16[16,3584]{1,0:T(8,128)(2,1)S(1)} %get-tuple-element.21), channel_id=1, source_target_pairs={{0,4},{2,6},{4,8},{6,10},{8,12},{10,14},{12,0},{14,2},{1,5},{3,7},... | collective-permute-start | bytes 344072 | tf_op jit(solution)/shard_map/ppermute | solution.py:51
  150.2 16.3 %collective-permute-start.26 = (bf16[16,7168]{1,0:T(8,128)(2,1)}, bf16[16,7168]{1,0:T(8,128)(2,1)}, u32[]{:S(2)}, u32[]{:S(2)}) collective-permute-start(bf16[16,7168]{1,0:T(8,128)(2,1)} %get-tuple-element.24), channel_id=1, source_target_pairs={{0,14},{2,0},{4,2},{6,4},{8,6},{10,8},{12,10},{14,12},{1,15},{3,1}... | collective-permute-start | bytes 688136 | tf_op jit(solution)/shard_map/ppermute | solution.py:51
  158.1 8.4 %collective-permute-start.24 = (bf16[16,7168]{1,0:T(8,128)(2,1)}, bf16[16,7168]{1,0:T(8,128)(2,1)}, u32[]{:S(2)}, u32[]{:S(2)}) collective-permute-start(bf16[16,7168]{1,0:T(8,128)(2,1)} %add_convert_fusion.4), channel_id=1, source_target_pairs={{0,2},{2,4},{4,6},{6,8},{8,10},{10,12},{12,14},{14,0},{1,3},{3,5},... | collective-permute-start | bytes 688136 | tf_op jit(solution)/shard_map/ppermute | solution.py:51
  158.1 8.4 %collective-permute-start.27 = (bf16[16,3584]{1,0:T(8,128)(2,1)}, bf16[16,3584]{1,0:T(8,128)(2,1)}, u32[]{:S(2)}, u32[]{:S(2)}) collective-permute-start(bf16[16,3584]{1,0:T(8,128)(2,1)} %get-tuple-element.22), channel_id=1, source_target_pairs={{0,12},{2,14},{4,0},{6,2},{8,4},{10,6},{12,8},{14,10},{1,13},{3,15... | collective-permute-start | bytes 344072 | tf_op jit(solution)/shard_map/ppermute | solution.py:51
  164.8 1.3 copy-start.3
  167.8 7.6 %collective-permute-start.28 = (bf16[16,7168]{1,0:T(8,128)(2,1)S(1)}, bf16[16,7168]{1,0:T(8,128)(2,1)S(1)}, u32[]{:S(2)}, u32[]{:S(2)}) collective-permute-start(bf16[16,7168]{1,0:T(8,128)(2,1)S(1)} %get-tuple-element.20), channel_id=1, source_target_pairs={{0,14},{2,0},{4,2},{6,4},{8,6},{10,8},{12,10},{14,12},{1,15},{3,1}... | collective-permute-start | bytes 688136 | tf_op jit(solution)/shard_map/ppermute | solution.py:51
  170.4 7.4 %collective-permute-start.25 = (bf16[16,7168]{1,0:T(8,128)(2,1)S(1)}, bf16[16,7168]{1,0:T(8,128)(2,1)S(1)}, u32[]{:S(2)}, u32[]{:S(2)}) collective-permute-start(bf16[16,7168]{1,0:T(8,128)(2,1)S(1)} %get-tuple-element.19), channel_id=1, source_target_pairs={{0,2},{2,4},{4,6},{6,8},{8,10},{10,12},{12,14},{14,0},{1,3},{3,5},... | collective-permute-start | bytes 688136 | tf_op jit(solution)/shard_map/ppermute | solution.py:51
  175.4 9.4 %collective-permute-start.29 = (bf16[16,7168]{1,0:T(8,128)(2,1)S(1)}, bf16[16,7168]{1,0:T(8,128)(2,1)S(1)}, u32[]{:S(2)}, u32[]{:S(2)}) collective-permute-start(bf16[16,7168]{1,0:T(8,128)(2,1)S(1)} %add_convert_fusion.1), channel_id=1, source_target_pairs={{0,14},{2,0},{4,2},{6,4},{8,6},{10,8},{12,10},{14,12},{1,15},{3,1}... | collective-permute-start | bytes 688136 | tf_op jit(solution)/shard_map/ppermute | solution.py:51
  185.6 26.2 %collective-permute-start.30 = (bf16[8,7168]{1,0:T(8,128)(2,1)S(1)}, bf16[8,7168]{1,0:T(8,128)(2,1)S(1)}, u32[]{:S(2)}, u32[]{:S(2)}) collective-permute-start(bf16[8,7168]{1,0:T(8,128)(2,1)S(1)} %slice.154), channel_id=1, source_target_pairs={{0,16},{16,0},{1,17},{17,1},{2,18},{18,2},{3,19},{19,3},{4,20},{20... | collective-permute-start | bytes 344072 | tf_op jit(solution)/shard_map/ppermute | solution.py:47
  208.8 6.3 %collective-permute-start.31 = (bf16[8,7168]{1,0:T(8,128)(2,1)S(1)}, bf16[8,7168]{1,0:T(8,128)(2,1)S(1)}, u32[]{:S(2)}, u32[]{:S(2)}) collective-permute-start(bf16[8,7168]{1,0:T(8,128)(2,1)S(1)} %slice.157), channel_id=1, source_target_pairs={{0,16},{16,0},{1,17},{17,1},{2,18},{18,2},{3,19},{19,3},{4,20},{20... | collective-permute-start | bytes 344072 | tf_op jit(solution)/shard_map/ppermute | solution.py:47
  (2 other events, 1.4 us)
Sparse Core Ops, SparseCore 0:
  166.2 41.6 reduce-scatter.1
where the time goes:
time: 225 us; the launch traced here: 224 us
  waiting for transfers between devices  109 us (48%)
  starting transfers between devices  54.1 us (24%)
  Pallas kernels  19.8 us (9%)
  local copies, waits for them, and re-layouts  14.1 us (6%)
  between operations  13.8 us (6%)
  matrix products  6.72 us (3%)
  other arithmetic  6.48 us (3%)
    ppermute x24, waiting for transfers between devices, shift(): return lax.ppermute(a, 'z', [(i, (i + by) % NZ) for i in range(NZ)])  59.9 us
    ppermute x24, starting transfers between devices, shift(): return lax.ppermute(a, 'z', [(i, (i + by) % NZ) for i in range(NZ)])  38.3 us
    reduce_scatter x1, waiting for transfers between devices, body(): lax.psum_scatter(other_part, 'z', scatter_dimension=0, tiled=True)  22.2 us
    ppermute x4, waiting for transfers between devices, swap_x(): return lax.ppermute(a, 'xhi', [(0, 1), (1, 0)])  15.3 us
    pallas_call x2, Pallas kernels, project(): pl.pallas_call(functools.partial(project_kernel, tile), out_shape=jax.Sha...  11.8 us
    all_to_all x1, waiting for transfers between devices, body(): lax.all_to_all(attended.reshape(2, CAP, CHIPS, 2 * HS), RING, split_axis=...  11.7 us
    all_to_all x1, starting transfers between devices, body(): lax.all_to_all(attended.reshape(2, CAP, CHIPS, 2 * HS), RING, split_axis=...  11.1 us
    unnamed x34, local copies, waits for them, and re-layouts  9.98 us
  transfers between devices with their start and end apart: 34, of which 17 were waited for; matrix products, arithmetic and copies ran while one was open for 7% of the time, Pallas kernels for 3%

commit v1 on v0

v1 whole, which is shorter than its diff:
```python
import functools
import math

import jax
import jax.numpy as jnp
from jax import lax
from jax.experimental import pallas as pl
from jax.experimental.pallas import tpu as pltpu
from jax.sharding import Mesh
from jax.sharding import PartitionSpec as P

D = 7168
HS = 256
CAP = 8
NX = 2
NZ = 8
CHIPS = NX * NZ
ROWS = 16
AXES = ("y", "xlo", "xhi", "z", "core")
RING = ("xhi", "z")


def attend(queries, key_cache, value_cache, lengths):
    count_rows = queries.shape[0]
    cache_len = key_cache.shape[1]
    head_size = key_cache.shape[2]
    num_heads = queries.shape[1] // head_size
    grouped = queries.reshape(count_rows, num_heads, head_size)
    scores = jnp.einsum(
        "rhd,rld->rhl", grouped, key_cache, preferred_element_type=jnp.float32
    ) / math.sqrt(head_size)
    positions = lax.broadcasted_iota(jnp.int32, (1, 1, cache_len), 2)
    scores = jnp.where(positions < lengths[:, None, None], scores, -1e30)
    largest = jnp.max(scores, axis=2, keepdims=True)
    expo = jnp.exp(scores - largest)
    weights = (expo / jnp.sum(expo, axis=2, keepdims=True)).astype(jnp.bfloat16)
    mixed = jnp.einsum("rhl,rld->rhd", weights, value_cache, preferred_element_type=jnp.float32)
    return mixed.astype(jnp.bfloat16).reshape(count_rows, num_heads * head_size)


def swap_cores(a):
    return lax.ppermute(a, "core", [(0, 1), (1, 0)])


def swap_x(a):
    return lax.ppermute(a, "xhi", [(0, 1), (1, 0)])


def shift(a, by):
    return lax.ppermute(a, "z", [(i, (i + by) % NZ) for i in range(NZ)])


def add(*terms):
    total = terms[0].astype(jnp.float32)
    for term in terms[1:]:
        total = total + term.astype(jnp.float32)
    return total


def add16(*terms):
    return add(*terms).astype(jnp.bfloat16)


def sum_z(part):
    half = part[0].shape[-1] // 2
    up, down = shift(part[4][:, :half], 1), shift(part[4][:, half:], -1)
    up = shift(add_part(part[3], up, 0), 1)
    down = shift(add_part(part[5], down, half), -1)
    up = shift(add16(part[2], up), 1)
    down = shift(add16(part[6], down), -1)
    up = shift(add16(part[1], up), 1)
    down = shift(add16(part[7], down), -1)
    return add16(part[0], up, down)


def add_part(whole, piece, at):
    size = piece.shape[-1]
    added = add16(whole[:, at : at + size], piece)
    return jnp.concatenate([whole[:, :at], added, whole[:, at + size :]], axis=1)


def cut(part):
    both = part.shape[0] // NZ
    return [part[k * both : (k + 1) * both] for k in range(NZ)]


def gather_z(mine):
    half = mine.shape[-1] // 2
    a1, b1 = shift(mine, 1), shift(mine, -1)
    a2, b2 = shift(a1, 1), shift(b1, -1)
    a3, b3 = shift(a2, 1), shift(b2, -1)
    a4, b4 = shift(a3[..., :half], 1), shift(b3[..., half:], -1)
    return [mine, b1, b2, b3, a4, b4, a3, a2, a1]


def project_kernel(tile, place, a, w_own, w_oth, out):
    blocks = []
    for rz in range(NZ):
        for kind in range(a.shape[0]):
            for rx in range(NX):
                x = lax.rem(place[0] + rx, NX)
                z = lax.rem(place[1] + rz, NZ)
                blocks.append(a[kind, x * NZ + z].astype(jnp.float32))
    rows = jnp.concatenate(blocks, axis=0)
    depth = w_own.shape[0]
    first = place[2] == 0
    own = jnp.where(first, rows[:, :depth], rows[:, depth:]).astype(jnp.bfloat16)
    oth = jnp.where(first, rows[:, depth:], rows[:, :depth]).astype(jnp.bfloat16)
    for i in range(D // tile):
        at = slice(i * tile, (i + 1) * tile)
        total = jnp.dot(own, w_own[:, at], preferred_element_type=jnp.float32)
        total += jnp.dot(oth, w_oth[:, at], preferred_element_type=jnp.float32)
        out[:, at] = total.astype(jnp.bfloat16)


def project(place, attended, w_own, w_oth, tile=1024):
    rows = math.prod(attended.shape[:3])
    whole = pl.BlockSpec(memory_space=pltpu.VMEM)
    return pl.pallas_call(
        functools.partial(project_kernel, tile),
        out_shape=jax.ShapeDtypeStruct((rows, D), jnp.bfloat16),
        in_specs=[pl.BlockSpec(memory_space=pltpu.SMEM)] + [whole] * 3,
        out_specs=whole,
        compiler_params=pltpu.CompilerParams(vmem_limit_bytes=16 * 1024 * 1024),
        name="project",
    )(place, attended, w_own, w_oth)


def expert_kernel(tile, *refs):
    pieces, (g_own, g_oth, u_own, u_oth, d_own, d_oth, out, first, last, sems) = refs[:9], refs[9:]
    steps, units = D // tile, g_own.shape[0]
    dims = (((1,), (1,)), ((), ()))

    def copies(i):
        at = pl.ds(i * tile, tile)
        return [
            pltpu.make_async_copy(w.at[:, at], first.at[pl.ds(k * units, units), at], sems.at[i, k])
            for k, w in enumerate((g_own, g_oth, u_own, u_oth))
        ]

    down = [
        pltpu.make_async_copy(w, last.at[pl.ds(k * units, units)], sems.at[steps, k])
        for k, w in enumerate((d_own, d_oth))
    ]
    moves = [copies(i) for i in range(steps)]
    for move in moves:
        for copy in move:
            copy.start()
    for copy in down:
        copy.start()
    both = None
    for i in range(steps):
        lo, hi = i * tile, (i + 1) * tile
        if hi <= D // 2:
            far = pieces[4][:, lo:hi]
        else:
            far = pieces[5][:, lo - D // 2 : hi - D // 2]
        near = [p[:, lo:hi] for p in pieces[:4]]
        back = [p[:, lo:hi] for p in pieces[6:]]
        piece = jnp.concatenate(near + [far] + back, axis=0)
        for copy in moves[i]:
            copy.wait()
        term = lax.dot_general(piece, first[:, lo:hi], dims, preferred_element_type=jnp.float32)
        both = term if both is None else both + term
    gate, up = both[:, : 2 * units], both[:, 2 * units :]
    act = (gate / (1.0 + jnp.exp(-gate)) * up).astype(jnp.bfloat16)
    for copy in down:
        copy.wait()
    for i in range(steps):
        at = slice(i * tile, (i + 1) * tile)
        out[:, at] = jnp.dot(act, last[:, at], preferred_element_type=jnp.float32).astype(jnp.bfloat16)


def expert(pieces, weights, tile=896):
    units = weights[0].shape[0]
    whole = pl.BlockSpec(memory_space=pltpu.VMEM)
    return pl.pallas_call(
        functools.partial(expert_kernel, tile),
        out_shape=jax.ShapeDtypeStruct((CHIPS * CAP, D), jnp.bfloat16),
        in_specs=[whole] * len(pieces) + [pl.BlockSpec(memory_space=pl.ANY)] * len(weights),
        out_specs=whole,
        scratch_shapes=[
            pltpu.VMEM((4 * units, D), jnp.bfloat16),
            pltpu.VMEM((2 * units, D), jnp.bfloat16),
            pltpu.SemaphoreType.DMA((D // tile + 1, 4)),
        ],
        compiler_params=pltpu.CompilerParams(vmem_limit_bytes=52 * 1024 * 1024),
        name="expert",
    )(*pieces, *weights)


def slots(routes):
    named = jnp.any(routes == 0, axis=1)
    row = jnp.arange(ROWS)
    before = row[:, None] < row[None, :]
    n_named = jnp.sum(named)
    rank_named = jnp.sum((before & named[:, None]).astype(jnp.int32), axis=0)
    slot = jnp.where(named, rank_named, n_named + row - rank_named)
    return row[:, None] == slot[None, :]


def body(
    queries,
    key_cache,
    value_cache,
    lengths,
    out_proj,
    residual,
    routes,
    route_weight,
    w_gate,
    w_up,
    w_down,
):
    place = jnp.stack([lax.axis_index(a) for a in ("xhi", "z", "core")]).astype(jnp.int32)
    o_oth = swap_cores(out_proj)
    g_oth, u_oth, d_oth = swap_cores(w_gate), swap_cores(w_up), swap_cores(w_down)

    order = slots(routes)
    order16 = order.astype(jnp.bfloat16)
    share = jnp.sum(jnp.where(routes == 0, route_weight, 0.0), axis=1)
    share = jnp.sum(jnp.where(order, share[None, :], 0.0), axis=1)

    res = jnp.dot(order16, residual, preferred_element_type=jnp.float32)
    res_oth = swap_x(res[:CAP].astype(jnp.bfloat16))
    attended = attend(queries, key_cache, value_cache, lengths)
    attended = jnp.dot(order16, attended, preferred_element_type=jnp.float32).astype(jnp.bfloat16)
    by_heads = lax.all_to_all(
        attended.reshape(2, CAP, CHIPS, 2 * HS), RING, split_axis=2, concat_axis=1
    )
    by_heads, o_oth, g_oth, u_oth, d_oth, res_oth = lax.optimization_barrier(
        (by_heads, o_oth, g_oth, u_oth, d_oth, res_oth)
    )
    pair_res = jnp.concatenate([res[:CAP], res_oth.astype(jnp.float32)], axis=0)
    mine = sum_z(cut(project(place, by_heads, out_proj, o_oth)))

    theirs = swap_x(mine[: NX * CAP])
    pair = pair_res + add(mine[: NX * CAP], jnp.concatenate([theirs[CAP:], theirs[:CAP]], axis=0))
    normed = (
        pair * lax.rsqrt(jnp.mean(pair * pair, axis=1, keepdims=True) + 1e-06)
    ).astype(jnp.bfloat16)
    pieces = gather_z(normed)
    rows = expert(pieces, (w_gate, g_oth, w_up, u_oth, w_down, d_oth))
    got = sum_z(cut(rows))
    expert_rows = add(got[:CAP], swap_x(got[CAP:]))
    rest = mine[NX * CAP :]
    others = res[CAP:] + add(rest[:CAP], swap_x(rest[CAP:]))
    done = jnp.concatenate(
        [pair[:CAP] + share[:CAP, None] * expert_rows, others], axis=0
    ).astype(jnp.bfloat16)
    return jnp.dot(order16.T, done, preferred_element_type=jnp.float32).astype(jnp.bfloat16)


def solution(mesh):
    fine = Mesh(mesh.devices.reshape(4, 2, NX, NZ, 2), AXES)
    rows, weights = P(AXES, None), P(("xhi", "z", "core"), None)
    placed = (
        rows,
        P(AXES, None, None),
        P(AXES, None, None),
        P(AXES),
        weights,
        rows,
        rows,
        rows,
        weights,
        weights,
        weights,
    )
    return jax.shard_map(body, mesh=fine, in_specs=placed, out_specs=rows, check_vma=False)
```

time: 225 us -> 182 us (0.81)
  waiting for transfers between devices: 109 us -> 91.4 us
  between operations: 13.8 us -> 0.4 us
  local copies, waits for them, and re-layouts: 14.1 us -> 5.35 us
  starting transfers between devices: 54.1 us -> 61.5 us
  Pallas kernels: 19.8 us -> 12.9 us
  matrix products: 6.72 us -> 3.98 us
    reduce_scatter x1 -> x0, waiting for transfers between devices: 22.2 us -> none  [body(): lax.psum_scatter(other_part, 'z', scatter_dimension=0, tiled=True)]
    ppermute x24, waiting for transfers between devices: 59.9 us -> 75.6 us  [shift(): return lax.ppermute(a, 'z', [(i, (i + by) % NZ) for i in range(NZ)])]
    pallas_call x2 -> x1, Pallas kernels: 11.8 us -> 4.13 us  [project(): pl.pallas_call(functools.partial(project_kernel, tile), out_shape=jax.Sha...]
    ppermute x4, waiting for transfers between devices: 15.3 us -> 7.77 us  [swap_x(): return lax.ppermute(a, 'xhi', [(0, 1), (1, 0)])]
    ppermute x4, starting transfers between devices: 3.73 us -> 10.8 us  [swap_x(): return lax.ppermute(a, 'xhi', [(0, 1), (1, 0)])]
    unnamed x34 -> x14, local copies, waits for them, and re-layouts: 9.98 us -> 3.21 us
    all_to_all x1, waiting for transfers between devices: 11.7 us -> 8.08 us  [body(): lax.all_to_all(attended.reshape(2, CAP, CHIPS, 2 * HS), RING, split_axis=...]
  transfers between devices with their start and end apart: 34 -> 33, of which waited for: 17 -> 20; matrix products, arithmetic and copies ran while one was open for 7% -> 4% of each run, Pallas kernels for 3% -> 0%
where the time goes in v1:
time: 182 us; the launch traced here: 181 us
  waiting for transfers between devices  91.4 us (50%)
  starting transfers between devices  61.5 us (34%)
  Pallas kernels  12.9 us (7%)
  local copies, waits for them, and re-layouts  5.35 us (3%)
  other arithmetic  5.16 us (3%)
  matrix products  3.98 us (2%)
    ppermute x24, waiting for transfers between devices, shift(): return lax.ppermute(a, 'z', [(i, (i + by) % NZ) for i in range(NZ)])  75.6 us
    ppermute x24, starting transfers between devices, shift(): return lax.ppermute(a, 'z', [(i, (i + by) % NZ) for i in range(NZ)])  38.6 us
    all_to_all x1, starting transfers between devices, body(): lax.all_to_all(attended.reshape(2, CAP, CHIPS, 2 * HS), RING, split_axis=...  11 us
    ppermute x4, starting transfers between devices, swap_x(): return lax.ppermute(a, 'xhi', [(0, 1), (1, 0)])  10.8 us
    pallas_call x1, Pallas kernels, expert(): pl.pallas_call(functools.partial(expert_kernel, tile), out_shape=jax.Shap...  8.74 us
    all_to_all x1, waiting for transfers between devices, body(): lax.all_to_all(attended.reshape(2, CAP, CHIPS, 2 * HS), RING, split_axis=...  8.08 us
    ppermute x4, waiting for transfers between devices, swap_x(): return lax.ppermute(a, 'xhi', [(0, 1), (1, 0)])  7.77 us
    pallas_call x1, Pallas kernels, project(): pl.pallas_call(functools.partial(project_kernel, tile), out_shape=jax.Sha...  4.13 us
  transfers between devices with their start and end apart: 33, of which 20 were waited for; matrix products, arithmetic and copies ran while one was open for 4% of the time, Pallas kernels for 0%

profile of v1, /device:TPU:24, one launch (start us, length us, event | category | flops | bytes accessed | tf_op | source)
XLA Modules:
  0.0 180.7 jit_solution(4503681201343604009)
XLA Ops:
  1.1 1.0 copy.16
  2.1 0.7 iota_compare_fusion
  2.9 1.7 fusion.3
  4.8 0.9 convolution_convert_fusion.2
  7.6 0.7 copy.14
  8.3 11.0 %all-to-all-start = ((bf16[2,1,8,16,512]{4,2,0,1,3:T(8,128)(2,1)}), bf16[2,1,8,16,512]{4,2,0,1,3:T(8,128)(2,1)S(1)}, u32[]{:S(2)}, u32[]{:S(2)}) async-start(bf16[2,1,8,16,512]{4,2,0,1,3:T(8,128)(2,1)} %copy.14), calls=%async_computation | async-start | bytes 524288 | tf_op jit(solution)/shard_map/all_to_all | solution.py:228
  19.6 3.5 %collective-permute-start.4 = (bf16[8,7168]{1,0:T(8,128)(2,1)S(1)}, bf16[8,7168]{1,0:T(8,128)(2,1)S(1)}, u32[]{:S(2)}, u32[]{:S(2)}) collective-permute-start(bf16[8,7168]{1,0:T(8,128)(2,1)S(1)} %slice.221), channel_id=1, source_target_pairs={{0,16},{16,0},{1,17},{17,1},{2,18},{18,2},{3,19},{19,3},{4,20},{20... | collective-permute-start | bytes 344072 | tf_op jit(solution)/shard_map/ppermute | solution.py:46
  23.2 8.1 %all-to-all-done = bf16[2,1,8,16,512]{4,2,0,1,3:T(8,128)(2,1)S(1)} async-done(((bf16[2,1,8,16,512]{4,2,0,1,3:T(8,128)(2,1)}), bf16[2,1,8,16,512]{4,2,0,1,3:T(8,128)(2,1)S(1)}, u32[]{:S(2)}, u32[]{:S(2)}) %all-to-all-start) | async-done | bytes 262176 | tf_op jit(solution)/shard_map/all_to_all | solution.py:228
  31.3 2.0 %copy-done.1 = bf16[256,7168]{1,0:T(8,128)(2,1)S(1)} copy-done((bf16[256,7168]{1,0:T(8,128)(2,1)S(1)}, bf16[256,7168]{1,0:T(8,128)(2,1)}, u32[]{:S(2)}) %copy-start.1) | copy-done | bytes 3670040
  33.4 4.1 %project.1 = bf16[256,7168]{1,0:T(8,128)(2,1)S(1)} custom-call(s32[3]{0:T(128)S(1)} %pad_add_fusion.place, bf16[2,16,8,512]{3,2,1,0:T(8,128)(2,1)S(1)} %bitcast.23, bf16[256,7168]{1,0:T(8,128)(2,1)S(1)} %copy-done.1, bf16[256,7168]{1,0:T(8,128)(2,1)} %collective-permute-done.w_oth), custom_call_target="tpu_custom_call" | custom-call | tf_op jit(solution)/shard_map/project/pallas_call | solution.py:119
  37.6 1.9 %collective-permute-start.5 = (bf16[32,3584]{1,0:T(8,128)(2,1)S(1)}, bf16[32,3584]{1,0:T(8,128)(2,1)S(1)}, u32[]{:S(2)}, u32[]{:S(2)}) collective-permute-start(bf16[32,3584]{1,0:T(8,128)(2,1)S(1)} %get-tuple-element.25), channel_id=1, source_target_pairs={{0,2},{2,4},{4,6},{6,8},{8,10},{10,12},{12,14},{14,0},{1,3},{3,5},... | collective-permute-start | bytes 688136 | tf_op jit(solution)/shard_map/ppermute | solution.py:50
  39.5 1.4 collective-permute-start.9
  40.9 4.0 %collective-permute-done.5 = bf16[32,3584]{1,0:T(8,128)(2,1)S(1)} collective-permute-done((bf16[32,3584]{1,0:T(8,128)(2,1)S(1)}, bf16[32,3584]{1,0:T(8,128)(2,1)S(1)}, u32[]{:S(2)}, u32[]{:S(2)}) %collective-permute-start.5) | collective-permute-done | bytes 229408 | tf_op jit(solution)/shard_map/ppermute | solution.py:50
  45.7 1.0 collective-permute-start.6
  46.7 2.4 %collective-permute-start.10 = (bf16[32,7168]{1,0:T(8,128)(2,1)S(1)}, bf16[32,7168]{1,0:T(8,128)(2,1)S(1)}, u32[]{:S(2)}, u32[]{:S(2)}) collective-permute-start(bf16[32,7168]{1,0:T(8,128)(2,1)S(1)} %pad_maximum_fusion.1), channel_id=1, source_target_pairs={{0,14},{2,0},{4,2},{6,4},{8,6},{10,8},{12,10},{14,12},{1,15},{3,1}... | collective-permute-start | bytes 1376264 | tf_op jit(solution)/shard_map/ppermute | solution.py:50
  49.1 7.6 %collective-permute-done.6 = bf16[32,7168]{1,0:T(8,128)(2,1)S(1)} collective-permute-done((bf16[32,7168]{1,0:T(8,128)(2,1)S(1)}, bf16[32,7168]{1,0:T(8,128)(2,1)S(1)}, u32[]{:S(2)}, u32[]{:S(2)}) %collective-permute-start.6) | collective-permute-done | bytes 458784 | tf_op jit(solution)/shard_map/ppermute | solution.py:50
  56.9 10.1 %collective-permute-done.7 = bf16[32,7168]{1,0:T(8,128)(2,1)S(1)} collective-permute-done((bf16[32,7168]{1,0:T(8,128)(2,1)S(1)}, bf16[32,7168]{1,0:T(8,128)(2,1)S(1)}, u32[]{:S(2)}, u32[]{:S(2)}) %collective-permute-start.7) | collective-permute-done | bytes 458784 | tf_op jit(solution)/shard_map/ppermute | solution.py:50
  67.3 2.1 %collective-permute-start.11 = (bf16[32,7168]{1,0:T(8,128)(2,1)S(1)}, bf16[32,7168]{1,0:T(8,128)(2,1)S(1)}, u32[]{:S(2)}, u32[]{:S(2)}) collective-permute-start(bf16[32,7168]{1,0:T(8,128)(2,1)S(1)} %get-tuple-element.22), channel_id=1, source_target_pairs={{0,14},{2,0},{4,2},{6,4},{8,6},{10,8},{12,10},{14,12},{1,15},{3,1}... | collective-permute-start | bytes 1376264 | tf_op jit(solution)/shard_map/ppermute | solution.py:50
  69.4 9.4 %collective-permute-done.11 = bf16[32,7168]{1,0:T(8,128)(2,1)S(1)} collective-permute-done((bf16[32,7168]{1,0:T(8,128)(2,1)S(1)}, bf16[32,7168]{1,0:T(8,128)(2,1)S(1)}, u32[]{:S(2)}, u32[]{:S(2)}) %collective-permute-start.11) | collective-permute-done | bytes 458784 | tf_op jit(solution)/shard_map/ppermute | solution.py:50
  78.9 3.8 %collective-permute-start.12 = (bf16[32,7168]{1,0:T(8,128)(2,1)S(1)}, bf16[32,7168]{1,0:T(8,128)(2,1)S(1)}, u32[]{:S(2)}, u32[]{:S(2)}) collective-permute-start(bf16[32,7168]{1,0:T(8,128)(2,1)S(1)} %add_convert_fusion.1), channel_id=1, source_target_pairs={{0,14},{2,0},{4,2},{6,4},{8,6},{10,8},{12,10},{14,12},{1,15},{3,1}... | collective-permute-start | bytes 1376264 | tf_op jit(solution)/shard_map/ppermute | solution.py:50
  82.6 6.0 %collective-permute-done.12 = bf16[32,7168]{1,0:T(8,128)(2,1)S(1)} collective-permute-done((bf16[32,7168]{1,0:T(8,128)(2,1)S(1)}, bf16[32,7168]{1,0:T(8,128)(2,1)S(1)}, u32[]{:S(2)}, u32[]{:S(2)}) %collective-permute-start.12) | collective-permute-done | bytes 458784 | tf_op jit(solution)/shard_map/ppermute | solution.py:50
  89.6 3.0 %collective-permute-start.13 = (bf16[16,7168]{1,0:T(8,128)(2,1)S(1)}, bf16[16,7168]{1,0:T(8,128)(2,1)S(1)}, u32[]{:S(2)}, u32[]{:S(2)}) collective-permute-start(bf16[16,7168]{1,0:T(8,128)(2,1)S(1)} %slice.175), channel_id=1, source_target_pairs={{0,16},{16,0},{1,17},{17,1},{2,18},{18,2},{3,19},{19,3},{4,20},{20... | collective-permute-start | bytes 688136 | tf_op jit(solution)/shard_map/ppermute | solution.py:46
  92.6 2.6 %collective-permute-done.31 = bf16[8,7168]{1,0:T(8,128)(2,1)S(1)} collective-permute-done((bf16[8,7168]{1,0:T(8,128)(2,1)S(1)}, bf16[8,7168]{1,0:T(8,128)(2,1)S(1)}, u32[]{:S(2)}, u32[]{:S(2)}) %collective-permute-start.31) | collective-permute-done | bytes 114720 | tf_op jit(solution)/shard_map/ppermute | solution.py:46
  95.2 2.4 %collective-permute-done.13 = bf16[16,7168]{1,0:T(8,128)(2,1)S(1)} collective-permute-done((bf16[16,7168]{1,0:T(8,128)(2,1)S(1)}, bf16[16,7168]{1,0:T(8,128)(2,1)S(1)}, u32[]{:S(2)}, u32[]{:S(2)}) %collective-permute-start.13) | collective-permute-done | bytes 229408 | tf_op jit(solution)/shard_map/ppermute | solution.py:46
  98.1 3.8 %collective-permute-start.14 = (bf16[16,7168]{1,0:T(8,128)(2,1)S(1)}, bf16[16,7168]{1,0:T(8,128)(2,1)S(1)}, u32[]{:S(2)}, u32[]{:S(2)}) collective-permute-start(bf16[16,7168]{1,0:T(8,128)(2,1)S(1)} %multiply_convert_fusion.refs_0_), channel_id=1, source_target_pairs={{0,14},{2,0},{4,2},{6,4},{8,6},{10,8},{12,10},{14,12},{1,15},{3,1}... | collective-permute-start | bytes 688136 | tf_op jit(solution)/shard_map/ppermute | solution.py:50
  101.9 3.9 %collective-permute-done.17.refs_8_ = bf16[16,7168]{1,0:T(8,128)(2,1)S(1)} collective-permute-done((bf16[16,7168]{1,0:T(8,128)(2,1)S(1)}, bf16[16,7168]{1,0:T(8,128)(2,1)S(1)}, u32[]{:S(2)}, u32[]{:S(2)}) %collective-permute-start.17) | collective-permute-done | bytes 229408 | tf_op jit(solution)/shard_map/ppermute | solution.py:50
  105.8 4.0 %collective-permute-start.15 = (bf16[16,7168]{1,0:T(8,128)(2,1)S(1)}, bf16[16,7168]{1,0:T(8,128)(2,1)S(1)}, u32[]{:S(2)}, u32[]{:S(2)}) collective-permute-start(bf16[16,7168]{1,0:T(8,128)(2,1)S(1)} %collective-permute-done.14.refs_1_), channel_id=1, source_target_pairs={{0,14},{2,0},{4,2},{6,4},{8,6},{10,8},{12,10},{14,12},{1,15},{3,1}... | collective-permute-start | bytes 688136 | tf_op jit(solution)/shard_map/ppermute | solution.py:50
  109.7 5.2 %collective-permute-done.18.refs_7_ = bf16[16,7168]{1,0:T(8,128)(2,1)S(1)} collective-permute-done((bf16[16,7168]{1,0:T(8,128)(2,1)S(1)}, bf16[16,7168]{1,0:T(8,128)(2,1)S(1)}, u32[]{:S(2)}, u32[]{:S(2)}) %collective-permute-start.18) | collective-permute-done | bytes 229408 | tf_op jit(solution)/shard_map/ppermute | solution.py:50
  114.9 3.2 %collective-permute-start.16 = (bf16[16,7168]{1,0:T(8,128)(2,1)S(1)}, bf16[16,7168]{1,0:T(8,128)(2,1)S(1)}, u32[]{:S(2)}, u32[]{:S(2)}) collective-permute-start(bf16[16,7168]{1,0:T(8,128)(2,1)S(1)} %collective-permute-done.15.refs_2_), channel_id=1, source_target_pairs={{0,14},{2,0},{4,2},{6,4},{8,6},{10,8},{12,10},{14,12},{1,15},{3,1}... | collective-permute-start | bytes 688136 | tf_op jit(solution)/shard_map/ppermute | solution.py:50
  118.2 4.0 %collective-permute-done.19.refs_6_ = bf16[16,7168]{1,0:T(8,128)(2,1)S(1)} collective-permute-done((bf16[16,7168]{1,0:T(8,128)(2,1)S(1)}, bf16[16,7168]{1,0:T(8,128)(2,1)S(1)}, u32[]{:S(2)}, u32[]{:S(2)}) %collective-permute-start.19) | collective-permute-done | bytes 229408 | tf_op jit(solution)/shard_map/ppermute | solution.py:50
  122.3 3.5 %collective-permute-start.21 = (bf16[16,3584]{1,0:T(8,128)(2,1)S(1)}, bf16[16,3584]{1,0:T(8,128)(2,1)S(1)}, u32[]{:S(2)}, u32[]{:S(2)}) collective-permute-start(bf16[16,3584]{1,0:T(8,128)(2,1)S(1)} %slice.180), channel_id=1, source_target_pairs={{0,14},{2,0},{4,2},{6,4},{8,6},{10,8},{12,10},{14,12},{1,15},{3,1}... | collective-permute-start | bytes 344072 | tf_op jit(solution)/shard_map/ppermute | solution.py:50
  125.8 2.5 %collective-permute-done.20.refs_4_ = bf16[16,3584]{1,0:T(8,128)(2,1)S(1)} collective-permute-done((bf16[16,3584]{1,0:T(8,128)(2,1)S(1)}, bf16[16,3584]{1,0:T(8,128)(2,1)S(1)}, u32[]{:S(2)}, u32[]{:S(2)}) %collective-permute-start.20) | collective-permute-done | bytes 114720 | tf_op jit(solution)/shard_map/ppermute | solution.py:50
  128.3 8.7 %expert.1 = bf16[128,7168]{1,0:T(8,128)(2,1)} custom-call(bf16[16,7168]{1,0:T(8,128)(2,1)S(1)} %multiply_convert_fusion.refs_0_, bf16[16,7168]{1,0:T(8,128)(2,1)S(1)} %collective-permute-done.14.refs_1_, bf16[16,7168]{1,0:T(8,128)(2,1)S(1)} %collective-permute-done.15.refs_2_, bf16[16,7168]{1,0:T(8,128)(2,1)S(1)} %collective-permute-done.16.refs_3_, ...), custom_call_target="tpu_custom_call" | custom-call | tf_op jit(solution)/shard_map/expert/pallas_call | solution.py:177
  137.0 1.2 fusion.18
  138.4 3.6 %collective-permute-start.26 = (bf16[16,3584]{1,0:T(8,128)(2,1)S(1)}, bf16[16,3584]{1,0:T(8,128)(2,1)S(1)}, u32[]{:S(2)}, u32[]{:S(2)}) collective-permute-start(bf16[16,3584]{1,0:T(8,128)(2,1)S(1)} %get-tuple-element.34), channel_id=1, source_target_pairs={{0,14},{2,0},{4,2},{6,4},{8,6},{10,8},{12,10},{14,12},{1,15},{3,1}... | collective-permute-start | bytes 344072 | tf_op jit(solution)/shard_map/ppermute | solution.py:50
  142.0 3.1 %collective-permute-done.22 = bf16[16,3584]{1,0:T(8,128)(2,1)S(1)} collective-permute-done((bf16[16,3584]{1,0:T(8,128)(2,1)S(1)}, bf16[16,3584]{1,0:T(8,128)(2,1)S(1)}, u32[]{:S(2)}, u32[]{:S(2)}) %collective-permute-start.22) | collective-permute-done | bytes 114720 | tf_op jit(solution)/shard_map/ppermute | solution.py:50
  145.1 1.0 add_convert_fusion.13
  146.2 3.3 %collective-permute-start.27 = (bf16[16,7168]{1,0:T(8,128)(2,1)S(1)}, bf16[16,7168]{1,0:T(8,128)(2,1)S(1)}, u32[]{:S(2)}, u32[]{:S(2)}) collective-permute-start(bf16[16,7168]{1,0:T(8,128)(2,1)S(1)} %pad_maximum_fusion.3), channel_id=1, source_target_pairs={{0,14},{2,0},{4,2},{6,4},{8,6},{10,8},{12,10},{14,12},{1,15},{3,1}... | collective-permute-start | bytes 688136 | tf_op jit(solution)/shard_map/ppermute | solution.py:50
  149.5 3.9 %collective-permute-done.23 = bf16[16,7168]{1,0:T(8,128)(2,1)S(1)} collective-permute-done((bf16[16,7168]{1,0:T(8,128)(2,1)S(1)}, bf16[16,7168]{1,0:T(8,128)(2,1)S(1)}, u32[]{:S(2)}, u32[]{:S(2)}) %collective-permute-start.23) | collective-permute-done | bytes 229408 | tf_op jit(solution)/shard_map/ppermute | solution.py:50
  153.9 1.1 collective-permute-done.27
  155.1 5.7 %collective-permute-done.24 = bf16[16,7168]{1,0:T(8,128)(2,1)S(1)} collective-permute-done((bf16[16,7168]{1,0:T(8,128)(2,1)S(1)}, bf16[16,7168]{1,0:T(8,128)(2,1)S(1)}, u32[]{:S(2)}, u32[]{:S(2)}) %collective-permute-start.24) | collective-permute-done | bytes 229408 | tf_op jit(solution)/shard_map/ppermute | solution.py:50
  161.5 1.6 collective-permute-start.25
  163.0 4.0 %collective-permute-done.28 = bf16[16,7168]{1,0:T(8,128)(2,1)S(1)} collective-permute-done((bf16[16,7168]{1,0:T(8,128)(2,1)S(1)}, bf16[16,7168]{1,0:T(8,128)(2,1)S(1)}, u32[]{:S(2)}, u32[]{:S(2)}) %collective-permute-start.28) | collective-permute-done | bytes 229408 | tf_op jit(solution)/shard_map/ppermute | solution.py:50
  167.1 1.7 collective-permute-start.29
  168.8 4.3 %collective-permute-done.29 = bf16[16,7168]{1,0:T(8,128)(2,1)S(1)} collective-permute-done((bf16[16,7168]{1,0:T(8,128)(2,1)S(1)}, bf16[16,7168]{1,0:T(8,128)(2,1)S(1)}, u32[]{:S(2)}, u32[]{:S(2)}) %collective-permute-start.29) | collective-permute-done | bytes 229408 | tf_op jit(solution)/shard_map/ppermute | solution.py:50
  173.3 3.5 %collective-permute-start.30 = (bf16[8,7168]{1,0:T(8,128)(2,1)S(1)}, bf16[8,7168]{1,0:T(8,128)(2,1)S(1)}, u32[]{:S(2)}, u32[]{:S(2)}) collective-permute-start(bf16[8,7168]{1,0:T(8,128)(2,1)S(1)} %slice.193), channel_id=1, source_target_pairs={{0,16},{16,0},{1,17},{17,1},{2,18},{18,2},{3,19},{19,3},{4,20},{20... | collective-permute-start | bytes 344072 | tf_op jit(solution)/shard_map/ppermute | solution.py:46
  176.9 2.7 %collective-permute-done.30 = bf16[8,7168]{1,0:T(8,128)(2,1)S(1)} collective-permute-done((bf16[8,7168]{1,0:T(8,128)(2,1)S(1)}, bf16[8,7168]{1,0:T(8,128)(2,1)S(1)}, u32[]{:S(2)}, u32[]{:S(2)}) %collective-permute-start.30) | collective-permute-done | bytes 114720 | tf_op jit(solution)/shard_map/ppermute | solution.py:46
  179.8 1.0 convolution_convert_fusion.1
  (79 shorter events, 8.0 us)
Async XLA Ops:
  0.0 4.8 %copy-start = (bf16[16,128,256]{2,1,0:T(8,128)(2,1)S(1)}, bf16[16,128,256]{2,1,0:T(8,128)(2,1)}, u32[]{:S(2)}) copy-start(bf16[16,128,256]{2,1,0:T(8,128)(2,1)} %param.13) | copy-start | bytes 3145732
  0.0 5.9 %copy-start.5 = (s32[16,3]{0,1:T(4,128)S(1)}, s32[16,3]{0,1:T(4,128)}, u32[]{:S(2)}) copy-start(s32[16,3]{0,1:T(4,128)} %param.17) | copy-start | bytes 580
  0.0 5.9 %copy-start.4 = (f32[16,3]{0,1:T(4,128)S(1)}, f32[16,3]{0,1:T(4,128)}, u32[]{:S(2)}) copy-start(f32[16,3]{0,1:T(4,128)} %param.18) | copy-start | bytes 580
  0.0 31.3 %collective-permute-start = (bf16[256,7168]{1,0:T(8,128)(2,1)}, bf16[256,7168]{1,0:T(8,128)(2,1)}, u32[]{:S(2)}, u32[]{:S(2)}) collective-permute-start(bf16[256,7168]{1,0:T(8,128)(2,1)} %w_own.1), channel_id=1, source_target_pairs={{0,1},{1,0},{2,3},{3,2},{4,5},{5,4},{6,7},{7,6},{8,9},{9,8},{10,11... | collective-permute-start | bytes 11010056 | tf_op jit(solution)/shard_map/ppermute | solution.py:42
  0.1 31.2 %collective-permute-start.1 = (bf16[160,7168]{1,0:T(8,128)(2,1)}, bf16[160,7168]{1,0:T(8,128)(2,1)}, u32[]{:S(2)}, u32[]{:S(2)}) collective-permute-start(bf16[160,7168]{1,0:T(8,128)(2,1)} %refs_9_.1), channel_id=1, source_target_pairs={{0,1},{1,0},{2,3},{3,2},{4,5},{5,4},{6,7},{7,6},{8,9},{9,8},{10,11... | collective-permute-start | bytes 6881288 | tf_op jit(solution)/shard_map/ppermute | solution.py:42
  0.6 30.7 %collective-permute-start.2 = (bf16[160,7168]{1,0:T(8,128)(2,1)}, bf16[160,7168]{1,0:T(8,128)(2,1)}, u32[]{:S(2)}, u32[]{:S(2)}) collective-permute-start(bf16[160,7168]{1,0:T(8,128)(2,1)} %refs_11_.1), channel_id=1, source_target_pairs={{0,1},{1,0},{2,3},{3,2},{4,5},{5,4},{6,7},{7,6},{8,9},{9,8},{10,11... | collective-permute-start | bytes 6881288 | tf_op jit(solution)/shard_map/ppermute | solution.py:42
  0.7 30.6 %collective-permute-start.3 = (bf16[160,7168]{1,0:T(8,128)(2,1)}, bf16[160,7168]{1,0:T(8,128)(2,1)}, u32[]{:S(2)}, u32[]{:S(2)}) collective-permute-start(bf16[160,7168]{1,0:T(8,128)(2,1)} %refs_13_.1), channel_id=1, source_target_pairs={{0,1},{1,0},{2,3},{3,2},{4,5},{5,4},{6,7},{7,6},{8,9},{9,8},{10,11... | collective-permute-start | bytes 6881288 | tf_op jit(solution)/shard_map/ppermute | solution.py:42
  4.5 14.8 %copy-start.3 = (bf16[16,7168]{1,0:T(8,128)(2,1)S(1)}, bf16[16,7168]{1,0:T(8,128)(2,1)}, u32[]{:S(2)}) copy-start(bf16[16,7168]{1,0:T(8,128)(2,1)} %param.16) | copy-start | bytes 688132
  8.3 22.9 %all-to-all-start = ((bf16[2,1,8,16,512]{4,2,0,1,3:T(8,128)(2,1)}), bf16[2,1,8,16,512]{4,2,0,1,3:T(8,128)(2,1)S(1)}, u32[]{:S(2)}, u32[]{:S(2)}) async-start(bf16[2,1,8,16,512]{4,2,0,1,3:T(8,128)(2,1)} %copy.14), calls=%async_computation | async-start | bytes 524288 | tf_op jit(solution)/shard_map/all_to_all | solution.py:228
  19.6 11.7 %collective-permute-start.4 = (bf16[8,7168]{1,0:T(8,128)(2,1)S(1)}, bf16[8,7168]{1,0:T(8,128)(2,1)S(1)}, u32[]{:S(2)}, u32[]{:S(2)}) collective-permute-start(bf16[8,7168]{1,0:T(8,128)(2,1)S(1)} %slice.221), channel_id=1, source_target_pairs={{0,16},{16,0},{1,17},{17,1},{2,18},{18,2},{3,19},{19,3},{4,20},{20... | collective-permute-start | bytes 344072 | tf_op jit(solution)/shard_map/ppermute | solution.py:46
  31.3 2.0 %copy-start.1 = (bf16[256,7168]{1,0:T(8,128)(2,1)S(1)}, bf16[256,7168]{1,0:T(8,128)(2,1)}, u32[]{:S(2)}) copy-start(bf16[256,7168]{1,0:T(8,128)(2,1)} %w_own.1) | copy-start | bytes 11010052
  37.6 7.3 %collective-permute-start.5 = (bf16[32,3584]{1,0:T(8,128)(2,1)S(1)}, bf16[32,3584]{1,0:T(8,128)(2,1)S(1)}, u32[]{:S(2)}, u32[]{:S(2)}) collective-permute-start(bf16[32,3584]{1,0:T(8,128)(2,1)S(1)} %get-tuple-element.25), channel_id=1, source_target_pairs={{0,2},{2,4},{4,6},{6,8},{8,10},{10,12},{12,14},{14,0},{1,3},{3,5},... | collective-permute-start | bytes 688136 | tf_op jit(solution)/shard_map/ppermute | solution.py:50
  39.5 6.0 %collective-permute-start.9 = (bf16[32,3584]{1,0:T(8,128)(2,1)S(1)}, bf16[32,3584]{1,0:T(8,128)(2,1)S(1)}, u32[]{:S(2)}, u32[]{:S(2)}) collective-permute-start(bf16[32,3584]{1,0:T(8,128)(2,1)S(1)} %get-tuple-element.26), channel_id=1, source_target_pairs={{0,14},{2,0},{4,2},{6,4},{8,6},{10,8},{12,10},{14,12},{1,15},{3,1}... | collective-permute-start | bytes 688136 | tf_op jit(solution)/shard_map/ppermute | solution.py:50
  45.7 11.1 %collective-permute-start.6 = (bf16[32,7168]{1,0:T(8,128)(2,1)S(1)}, bf16[32,7168]{1,0:T(8,128)(2,1)S(1)}, u32[]{:S(2)}, u32[]{:S(2)}) collective-permute-start(bf16[32,7168]{1,0:T(8,128)(2,1)S(1)} %pad_maximum_fusion), channel_id=1, source_target_pairs={{0,2},{2,4},{4,6},{6,8},{8,10},{10,12},{12,14},{14,0},{1,3},{3,5},... | collective-permute-start | bytes 1376264 | tf_op jit(solution)/shard_map/ppermute | solution.py:50
  46.7 10.2 %collective-permute-start.10 = (bf16[32,7168]{1,0:T(8,128)(2,1)S(1)}, bf16[32,7168]{1,0:T(8,128)(2,1)S(1)}, u32[]{:S(2)}, u32[]{:S(2)}) collective-permute-start(bf16[32,7168]{1,0:T(8,128)(2,1)S(1)} %pad_maximum_fusion.1), channel_id=1, source_target_pairs={{0,14},{2,0},{4,2},{6,4},{8,6},{10,8},{12,10},{14,12},{1,15},{3,1}... | collective-permute-start | bytes 1376264 | tf_op jit(solution)/shard_map/ppermute | solution.py:50
  56.8 10.2 %collective-permute-start.7 = (bf16[32,7168]{1,0:T(8,128)(2,1)S(1)}, bf16[32,7168]{1,0:T(8,128)(2,1)S(1)}, u32[]{:S(2)}, u32[]{:S(2)}) collective-permute-start(bf16[32,7168]{1,0:T(8,128)(2,1)S(1)} %add_convert_fusion.4), channel_id=1, source_target_pairs={{0,2},{2,4},{4,6},{6,8},{8,10},{10,12},{12,14},{14,0},{1,3},{3,5},... | collective-permute-start | bytes 1376264 | tf_op jit(solution)/shard_map/ppermute | solution.py:50
  67.3 11.5 %collective-permute-start.11 = (bf16[32,7168]{1,0:T(8,128)(2,1)S(1)}, bf16[32,7168]{1,0:T(8,128)(2,1)S(1)}, u32[]{:S(2)}, u32[]{:S(2)}) collective-permute-start(bf16[32,7168]{1,0:T(8,128)(2,1)S(1)} %get-tuple-element.22), channel_id=1, source_target_pairs={{0,14},{2,0},{4,2},{6,4},{8,6},{10,8},{12,10},{14,12},{1,15},{3,1}... | collective-permute-start | bytes 1376264 | tf_op jit(solution)/shard_map/ppermute | solution.py:50
  69.4 13.3 %collective-permute-start.8 = (bf16[32,7168]{1,0:T(8,128)(2,1)S(1)}, bf16[32,7168]{1,0:T(8,128)(2,1)S(1)}, u32[]{:S(2)}, u32[]{:S(2)}) collective-permute-start(bf16[32,7168]{1,0:T(8,128)(2,1)S(1)} %get-tuple-element.21), channel_id=1, source_target_pairs={{0,2},{2,4},{4,6},{6,8},{8,10},{10,12},{12,14},{14,0},{1,3},{3,5},... | collective-permute-start | bytes 1376264 | tf_op jit(solution)/shard_map/ppermute | solution.py:50
  78.9 9.8 %collective-permute-start.12 = (bf16[32,7168]{1,0:T(8,128)(2,1)S(1)}, bf16[32,7168]{1,0:T(8,128)(2,1)S(1)}, u32[]{:S(2)}, u32[]{:S(2)}) collective-permute-start(bf16[32,7168]{1,0:T(8,128)(2,1)S(1)} %add_convert_fusion.1), channel_id=1, source_target_pairs={{0,14},{2,0},{4,2},{6,4},{8,6},{10,8},{12,10},{14,12},{1,15},{3,1}... | collective-permute-start | bytes 1376264 | tf_op jit(solution)/shard_map/ppermute | solution.py:50
  88.8 6.4 %collective-permute-start.31 = (bf16[8,7168]{1,0:T(8,128)(2,1)S(1)}, bf16[8,7168]{1,0:T(8,128)(2,1)S(1)}, u32[]{:S(2)}, u32[]{:S(2)}) collective-permute-start(bf16[8,7168]{1,0:T(8,128)(2,1)S(1)} %slice.196), channel_id=1, source_target_pairs={{0,16},{16,0},{1,17},{17,1},{2,18},{18,2},{3,19},{19,3},{4,20},{20... | collective-permute-start | bytes 344072 | tf_op jit(solution)/shard_map/ppermute | solution.py:46
  89.6 8.1 %collective-permute-start.13 = (bf16[16,7168]{1,0:T(8,128)(2,1)S(1)}, bf16[16,7168]{1,0:T(8,128)(2,1)S(1)}, u32[]{:S(2)}, u32[]{:S(2)}) collective-permute-start(bf16[16,7168]{1,0:T(8,128)(2,1)S(1)} %slice.175), channel_id=1, source_target_pairs={{0,16},{16,0},{1,17},{17,1},{2,18},{18,2},{3,19},{19,3},{4,20},{20... | collective-permute-start | bytes 688136 | tf_op jit(solution)/shard_map/ppermute | solution.py:46
  98.0 7.8 %collective-permute-start.17 = (bf16[16,7168]{1,0:T(8,128)(2,1)S(1)}, bf16[16,7168]{1,0:T(8,128)(2,1)S(1)}, u32[]{:S(2)}, u32[]{:S(2)}) collective-permute-start(bf16[16,7168]{1,0:T(8,128)(2,1)S(1)} %multiply_convert_fusion.refs_0_), channel_id=1, source_target_pairs={{0,2},{2,4},{4,6},{6,8},{8,10},{10,12},{12,14},{14,0},{1,3},{3,5},... | collective-permute-start | bytes 688136 | tf_op jit(solution)/shard_map/ppermute | solution.py:50
  98.1 7.7 %collective-permute-start.14 = (bf16[16,7168]{1,0:T(8,128)(2,1)S(1)}, bf16[16,7168]{1,0:T(8,128)(2,1)S(1)}, u32[]{:S(2)}, u32[]{:S(2)}) collective-permute-start(bf16[16,7168]{1,0:T(8,128)(2,1)S(1)} %multiply_convert_fusion.refs_0_), channel_id=1, source_target_pairs={{0,14},{2,0},{4,2},{6,4},{8,6},{10,8},{12,10},{14,12},{1,15},{3,1}... | collective-permute-start | bytes 688136 | tf_op jit(solution)/shard_map/ppermute | solution.py:50
  105.8 9.2 %collective-permute-start.18 = (bf16[16,7168]{1,0:T(8,128)(2,1)S(1)}, bf16[16,7168]{1,0:T(8,128)(2,1)S(1)}, u32[]{:S(2)}, u32[]{:S(2)}) collective-permute-start(bf16[16,7168]{1,0:T(8,128)(2,1)S(1)} %collective-permute-done.17.refs_8_), channel_id=1, source_target_pairs={{0,2},{2,4},{4,6},{6,8},{8,10},{10,12},{12,14},{14,0},{1,3},{3,5},... | collective-permute-start | bytes 688136 | tf_op jit(solution)/shard_map/ppermute | solution.py:50
  105.8 9.2 %collective-permute-start.15 = (bf16[16,7168]{1,0:T(8,128)(2,1)S(1)}, bf16[16,7168]{1,0:T(8,128)(2,1)S(1)}, u32[]{:S(2)}, u32[]{:S(2)}) collective-permute-start(bf16[16,7168]{1,0:T(8,128)(2,1)S(1)} %collective-permute-done.14.refs_1_), channel_id=1, source_target_pairs={{0,14},{2,0},{4,2},{6,4},{8,6},{10,8},{12,10},{14,12},{1,15},{3,1}... | collective-permute-start | bytes 688136 | tf_op jit(solution)/shard_map/ppermute | solution.py:50
  114.9 7.2 %collective-permute-start.19 = (bf16[16,7168]{1,0:T(8,128)(2,1)S(1)}, bf16[16,7168]{1,0:T(8,128)(2,1)S(1)}, u32[]{:S(2)}, u32[]{:S(2)}) collective-permute-start(bf16[16,7168]{1,0:T(8,128)(2,1)S(1)} %collective-permute-done.18.refs_7_), channel_id=1, source_target_pairs={{0,2},{2,4},{4,6},{6,8},{8,10},{10,12},{12,14},{14,0},{1,3},{3,5},... | collective-permute-start | bytes 688136 | tf_op jit(solution)/shard_map/ppermute | solution.py:50
  114.9 7.3 %collective-permute-start.16 = (bf16[16,7168]{1,0:T(8,128)(2,1)S(1)}, bf16[16,7168]{1,0:T(8,128)(2,1)S(1)}, u32[]{:S(2)}, u32[]{:S(2)}) collective-permute-start(bf16[16,7168]{1,0:T(8,128)(2,1)S(1)} %collective-permute-done.15.refs_2_), channel_id=1, source_target_pairs={{0,14},{2,0},{4,2},{6,4},{8,6},{10,8},{12,10},{14,12},{1,15},{3,1}... | collective-permute-start | bytes 688136 | tf_op jit(solution)/shard_map/ppermute | solution.py:50
  122.2 6.1 %collective-permute-start.20 = (bf16[16,3584]{1,0:T(8,128)(2,1)S(1)}, bf16[16,3584]{1,0:T(8,128)(2,1)S(1)}, u32[]{:S(2)}, u32[]{:S(2)}) collective-permute-start(bf16[16,3584]{1,0:T(8,128)(2,1)S(1)} %slice.179), channel_id=1, source_target_pairs={{0,2},{2,4},{4,6},{6,8},{8,10},{10,12},{12,14},{14,0},{1,3},{3,5},... | collective-permute-start | bytes 344072 | tf_op jit(solution)/shard_map/ppermute | solution.py:50
  122.3 6.0 %collective-permute-start.21 = (bf16[16,3584]{1,0:T(8,128)(2,1)S(1)}, bf16[16,3584]{1,0:T(8,128)(2,1)S(1)}, u32[]{:S(2)}, u32[]{:S(2)}) collective-permute-start(bf16[16,3584]{1,0:T(8,128)(2,1)S(1)} %slice.180), channel_id=1, source_target_pairs={{0,14},{2,0},{4,2},{6,4},{8,6},{10,8},{12,10},{14,12},{1,15},{3,1}... | collective-permute-start | bytes 344072 | tf_op jit(solution)/shard_map/ppermute | solution.py:50
  137.0 16.4 %copy-start.2 = (bf16[128,7168]{1,0:T(8,128)(2,1)S(1)}, bf16[128,7168]{1,0:T(8,128)(2,1)}, u32[]{:S(2)}) copy-start(bf16[128,7168]{1,0:T(8,128)(2,1)} %expert.1) | copy-start | bytes 5505028
  138.3 6.8 %collective-permute-start.22 = (bf16[16,3584]{1,0:T(8,128)(2,1)S(1)}, bf16[16,3584]{1,0:T(8,128)(2,1)S(1)}, u32[]{:S(2)}, u32[]{:S(2)}) collective-permute-start(bf16[16,3584]{1,0:T(8,128)(2,1)S(1)} %get-tuple-element.33), channel_id=1, source_target_pairs={{0,2},{2,4},{4,6},{6,8},{8,10},{10,12},{12,14},{14,0},{1,3},{3,5},... | collective-permute-start | bytes 344072 | tf_op jit(solution)/shard_map/ppermute | solution.py:50
  138.4 6.7 %collective-permute-start.26 = (bf16[16,3584]{1,0:T(8,128)(2,1)S(1)}, bf16[16,3584]{1,0:T(8,128)(2,1)S(1)}, u32[]{:S(2)}, u32[]{:S(2)}) collective-permute-start(bf16[16,3584]{1,0:T(8,128)(2,1)S(1)} %get-tuple-element.34), channel_id=1, source_target_pairs={{0,14},{2,0},{4,2},{6,4},{8,6},{10,8},{12,10},{14,12},{1,15},{3,1}... | collective-permute-start | bytes 344072 | tf_op jit(solution)/shard_map/ppermute | solution.py:50
  146.1 7.3 %collective-permute-start.23 = (bf16[16,7168]{1,0:T(8,128)(2,1)S(1)}, bf16[16,7168]{1,0:T(8,128)(2,1)S(1)}, u32[]{:S(2)}, u32[]{:S(2)}) collective-permute-start(bf16[16,7168]{1,0:T(8,128)(2,1)S(1)} %pad_maximum_fusion.2), channel_id=1, source_target_pairs={{0,2},{2,4},{4,6},{6,8},{8,10},{10,12},{12,14},{14,0},{1,3},{3,5},... | collective-permute-start | bytes 688136 | tf_op jit(solution)/shard_map/ppermute | solution.py:50
  146.2 8.8 %collective-permute-start.27 = (bf16[16,7168]{1,0:T(8,128)(2,1)S(1)}, bf16[16,7168]{1,0:T(8,128)(2,1)S(1)}, u32[]{:S(2)}, u32[]{:S(2)}) collective-permute-start(bf16[16,7168]{1,0:T(8,128)(2,1)S(1)} %pad_maximum_fusion.3), channel_id=1, source_target_pairs={{0,14},{2,0},{4,2},{6,4},{8,6},{10,8},{12,10},{14,12},{1,15},{3,1}... | collective-permute-start | bytes 688136 | tf_op jit(solution)/shard_map/ppermute | solution.py:50
  153.5 7.3 %collective-permute-start.24 = (bf16[16,7168]{1,0:T(8,128)(2,1)S(1)}, bf16[16,7168]{1,0:T(8,128)(2,1)S(1)}, u32[]{:S(2)}, u32[]{:S(2)}) collective-permute-start(bf16[16,7168]{1,0:T(8,128)(2,1)S(1)} %add_convert_fusion.9), channel_id=1, source_target_pairs={{0,2},{2,4},{4,6},{6,8},{8,10},{10,12},{12,14},{14,0},{1,3},{3,5},... | collective-permute-start | bytes 688136 | tf_op jit(solution)/shard_map/ppermute | solution.py:50
  160.9 6.1 %collective-permute-start.28 = (bf16[16,7168]{1,0:T(8,128)(2,1)S(1)}, bf16[16,7168]{1,0:T(8,128)(2,1)S(1)}, u32[]{:S(2)}, u32[]{:S(2)}) collective-permute-start(bf16[16,7168]{1,0:T(8,128)(2,1)S(1)} %get-tuple-element.30), channel_id=1, source_target_pairs={{0,14},{2,0},{4,2},{6,4},{8,6},{10,8},{12,10},{14,12},{1,15},{3,1}... | collective-permute-start | bytes 688136 | tf_op jit(solution)/shard_map/ppermute | solution.py:50
  161.5 7.4 %collective-permute-start.25 = (bf16[16,7168]{1,0:T(8,128)(2,1)S(1)}, bf16[16,7168]{1,0:T(8,128)(2,1)S(1)}, u32[]{:S(2)}, u32[]{:S(2)}) collective-permute-start(bf16[16,7168]{1,0:T(8,128)(2,1)S(1)} %get-tuple-element.29), channel_id=1, source_target_pairs={{0,2},{2,4},{4,6},{6,8},{8,10},{10,12},{12,14},{14,0},{1,3},{3,5},... | collective-permute-start | bytes 688136 | tf_op jit(solution)/shard_map/ppermute | solution.py:50
  167.1 6.1 %collective-permute-start.29 = (bf16[16,7168]{1,0:T(8,128)(2,1)S(1)}, bf16[16,7168]{1,0:T(8,128)(2,1)S(1)}, u32[]{:S(2)}, u32[]{:S(2)}) collective-permute-start(bf16[16,7168]{1,0:T(8,128)(2,1)S(1)} %add_convert_fusion.6), channel_id=1, source_target_pairs={{0,14},{2,0},{4,2},{6,4},{8,6},{10,8},{12,10},{14,12},{1,15},{3,1}... | collective-permute-start | bytes 688136 | tf_op jit(solution)/shard_map/ppermute | solution.py:50
  173.3 6.4 %collective-permute-start.30 = (bf16[8,7168]{1,0:T(8,128)(2,1)S(1)}, bf16[8,7168]{1,0:T(8,128)(2,1)S(1)}, u32[]{:S(2)}, u32[]{:S(2)}) collective-permute-start(bf16[8,7168]{1,0:T(8,128)(2,1)S(1)} %slice.193), channel_id=1, source_target_pairs={{0,16},{16,0},{1,17},{17,1},{2,18},{18,2},{3,19},{19,3},{4,20},{20... | collective-permute-start | bytes 344072 | tf_op jit(solution)/shard_map/ppermute | solution.py:46

commit v2 on v1

--- a/solution.py
+++ b/solution.py
@@ -17,7 +17,10 @@
 CHIPS = NX * NZ
 ROWS = 16
 AXES = ("y", "xlo", "xhi", "z", "core")
-RING = ("xhi", "z")
+RING = ("xhi", "z", "core")
+TEAMS = [
+    [(x * NZ + z) * 2 + (z + odd) % 2 for x in range(NX) for z in range(NZ)] for odd in range(2)
+]
 
 
 def attend(queries, key_cache, value_cache, lengths):
@@ -47,7 +50,12 @@
 
 
 def shift(a, by):
-    return lax.ppermute(a, "z", [(i, (i + by) % NZ) for i in range(NZ)])
+    moves = [
+        (2 * z + core, 2 * ((z + by) % NZ) + (core + by) % 2)
+        for z in range(NZ)
+        for core in range(2)
+    ]
+    return lax.ppermute(a, ("z", "core"), moves)
 
 
 def add(*terms):
@@ -93,7 +101,18 @@
     return [mine, b1, b2, b3, a4, b4, a3, a2, a1]
 
 
-def project_kernel(tile, place, a, w_own, w_oth, out):
+def project_kernel(tile, place, a, w_own, w_oth, out, held, sems):
+    steps, depth = D // tile, w_own.shape[0]
+    moves = [
+        [
+            pltpu.make_async_copy(w.at[:, pl.ds(i * tile, tile)], held.at[k, i], sems.at[k, i])
+            for k, w in enumerate((w_own, w_oth))
+        ]
+        for i in range(steps)
+    ]
+    for move in moves:
+        for copy in move:
+            copy.start()
     blocks = []
     for rz in range(NZ):
         for kind in range(a.shape[0]):
@@ -102,52 +121,39 @@
                 z = lax.rem(place[1] + rz, NZ)
                 blocks.append(a[kind, x * NZ + z].astype(jnp.float32))
     rows = jnp.concatenate(blocks, axis=0)
-    depth = w_own.shape[0]
     first = place[2] == 0
     own = jnp.where(first, rows[:, :depth], rows[:, depth:]).astype(jnp.bfloat16)
     oth = jnp.where(first, rows[:, depth:], rows[:, :depth]).astype(jnp.bfloat16)
-    for i in range(D // tile):
-        at = slice(i * tile, (i + 1) * tile)
-        total = jnp.dot(own, w_own[:, at], preferred_element_type=jnp.float32)
-        total += jnp.dot(oth, w_oth[:, at], preferred_element_type=jnp.float32)
-        out[:, at] = total.astype(jnp.bfloat16)
+    for i in range(steps):
+        for copy in moves[i]:
+            copy.wait()
+        total = jnp.dot(own, held[0, i], preferred_element_type=jnp.float32)
+        total += jnp.dot(oth, held[1, i], preferred_element_type=jnp.float32)
+        out[:, i * tile : (i + 1) * tile] = total.astype(jnp.bfloat16)
 
 
 def project(place, attended, w_own, w_oth, tile=1024):
-    rows = math.prod(attended.shape[:3])
+    rows, depth = math.prod(attended.shape[:3]), w_own.shape[0]
     whole = pl.BlockSpec(memory_space=pltpu.VMEM)
+    anywhere = pl.BlockSpec(memory_space=pl.ANY)
     return pl.pallas_call(
         functools.partial(project_kernel, tile),
         out_shape=jax.ShapeDtypeStruct((rows, D), jnp.bfloat16),
-        in_specs=[pl.BlockSpec(memory_space=pltpu.SMEM)] + [whole] * 3,
+        in_specs=[pl.BlockSpec(memory_space=pltpu.SMEM), whole, anywhere, anywhere],
         out_specs=whole,
-        compiler_params=pltpu.CompilerParams(vmem_limit_bytes=16 * 1024 * 1024),
+        scratch_shapes=[
+            pltpu.VMEM((2, D // tile, depth, tile), jnp.bfloat16),
+            pltpu.SemaphoreType.DMA((2, D // tile)),
+        ],
+        compiler_params=pltpu.CompilerParams(vmem_limit_bytes=32 * 1024 * 1024),
         name="project",
     )(place, attended, w_own, w_oth)
 
 
 def expert_kernel(tile, *refs):
-    pieces, (g_own, g_oth, u_own, u_oth, d_own, d_oth, out, first, last, sems) = refs[:9], refs[9:]
-    steps, units = D // tile, g_own.shape[0]
+    pieces, first, (d_own, d_oth, out) = refs[:9], refs[9:13], refs[13:]
+    steps, units = D // tile, d_own.shape[0]
     dims = (((1,), (1,)), ((), ()))
-
-    def copies(i):
-        at = pl.ds(i * tile, tile)
-        return [
-            pltpu.make_async_copy(w.at[:, at], first.at[pl.ds(k * units, units), at], sems.at[i, k])
-            for k, w in enumerate((g_own, g_oth, u_own, u_oth))
-        ]
-
-    down = [
-        pltpu.make_async_copy(w, last.at[pl.ds(k * units, units)], sems.at[steps, k])
-        for k, w in enumerate((d_own, d_oth))
-    ]
-    moves = [copies(i) for i in range(steps)]
-    for move in moves:
-        for copy in move:
-            copy.start()
-    for copy in down:
-        copy.start()
     both = None
     for i in range(steps):
         lo, hi = i * tile, (i + 1) * tile
@@ -158,33 +164,25 @@
         near = [p[:, lo:hi] for p in pieces[:4]]
         back = [p[:, lo:hi] for p in pieces[6:]]
         piece = jnp.concatenate(near + [far] + back, axis=0)
-        for copy in moves[i]:
-            copy.wait()
-        term = lax.dot_general(piece, first[:, lo:hi], dims, preferred_element_type=jnp.float32)
+        weights = jnp.concatenate([w[:, lo:hi] for w in first], axis=0)
+        term = lax.dot_general(piece, weights, dims, preferred_element_type=jnp.float32)
         both = term if both is None else both + term
     gate, up = both[:, : 2 * units], both[:, 2 * units :]
     act = (gate / (1.0 + jnp.exp(-gate)) * up).astype(jnp.bfloat16)
-    for copy in down:
-        copy.wait()
     for i in range(steps):
         at = slice(i * tile, (i + 1) * tile)
-        out[:, at] = jnp.dot(act, last[:, at], preferred_element_type=jnp.float32).astype(jnp.bfloat16)
+        last = jnp.concatenate([d_own[:, at], d_oth[:, at]], axis=0)
+        out[:, at] = jnp.dot(act, last, preferred_element_type=jnp.float32).astype(jnp.bfloat16)
 
 
 def expert(pieces, weights, tile=896):
-    units = weights[0].shape[0]
     whole = pl.BlockSpec(memory_space=pltpu.VMEM)
     return pl.pallas_call(
         functools.partial(expert_kernel, tile),
         out_shape=jax.ShapeDtypeStruct((CHIPS * CAP, D), jnp.bfloat16),
-        in_specs=[whole] * len(pieces) + [pl.BlockSpec(memory_space=pl.ANY)] * len(weights),
+        in_specs=[whole] * (len(pieces) + len(weights)),
         out_specs=whole,
-        scratch_shapes=[
-            pltpu.VMEM((4 * units, D), jnp.bfloat16),
-            pltpu.VMEM((2 * units, D), jnp.bfloat16),
-            pltpu.SemaphoreType.DMA((D // tile + 1, 4)),
-        ],
-        compiler_params=pltpu.CompilerParams(vmem_limit_bytes=52 * 1024 * 1024),
+        compiler_params=pltpu.CompilerParams(vmem_limit_bytes=16 * 1024 * 1024),
         name="expert",
     )(*pieces, *weights)
 
@@ -214,7 +212,6 @@
 ):
     place = jnp.stack([lax.axis_index(a) for a in ("xhi", "z", "core")]).astype(jnp.int32)
     o_oth = swap_cores(out_proj)
-    g_oth, u_oth, d_oth = swap_cores(w_gate), swap_cores(w_up), swap_cores(w_down)
 
     order = slots(routes)
     order16 = order.astype(jnp.bfloat16)
@@ -226,11 +223,13 @@
     attended = attend(queries, key_cache, value_cache, lengths)
     attended = jnp.dot(order16, attended, preferred_element_type=jnp.float32).astype(jnp.bfloat16)
     by_heads = lax.all_to_all(
-        attended.reshape(2, CAP, CHIPS, 2 * HS), RING, split_axis=2, concat_axis=1
+        attended.reshape(2, CAP, CHIPS, 2 * HS), RING, split_axis=2, concat_axis=1,
+        axis_index_groups=TEAMS,
     )
-    by_heads, o_oth, g_oth, u_oth, d_oth, res_oth = lax.optimization_barrier(
-        (by_heads, o_oth, g_oth, u_oth, d_oth, res_oth)
+    by_heads, o_oth, res_oth, w_gate, w_up, w_down = lax.optimization_barrier(
+        (by_heads, o_oth, res_oth, w_gate, w_up, w_down)
     )
+    g_oth, u_oth, d_oth = swap_cores(w_gate), swap_cores(w_up), swap_cores(w_down)
     pair_res = jnp.concatenate([res[:CAP], res_oth.astype(jnp.float32)], axis=0)
     mine = sum_z(cut(project(place, by_heads, out_proj, o_oth)))
 

time: 182 us -> 199 us (1.093)
  waiting for transfers between devices: 91.4 us -> 123 us
  starting transfers between devices: 61.5 us -> 52.6 us
  Pallas kernels: 12.9 us -> 9.07 us
    ppermute x24, waiting for transfers between devices: 75.6 us -> 103 us  [shift(): return lax.ppermute(a, ('z', 'core'), moves)]
    ppermute x24, starting transfers between devices: 38.6 us -> 31.2 us  [shift(): return lax.ppermute(a, ('z', 'core'), moves)]
    pallas_call x1, Pallas kernels: 8.74 us -> 4.22 us  [expert(): pl.pallas_call(functools.partial(expert_kernel, tile), out_shape=jax.Shap...]
    ppermute x4, waiting for transfers between devices: 7.77 us -> 12 us  [swap_x(): return lax.ppermute(a, 'xhi', [(0, 1), (1, 0)])]
where the time goes in v2:
time: 199 us; the launch traced here: 198 us
  waiting for transfers between devices  123 us (62%)
  starting transfers between devices  52.6 us (26%)
  Pallas kernels  9.07 us (5%)
  local copies, waits for them, and re-layouts  4.2 us (2%)
  other arithmetic  4.2 us (2%)
  matrix products  3.98 us (2%)
    ppermute x24, waiting for transfers between devices, shift(): return lax.ppermute(a, ('z', 'core'), moves)  103 us
    ppermute x24, starting transfers between devices, shift(): return lax.ppermute(a, ('z', 'core'), moves)  31.2 us
    ppermute x4, waiting for transfers between devices, swap_x(): return lax.ppermute(a, 'xhi', [(0, 1), (1, 0)])  12 us
    all_to_all x1, starting transfers between devices, body(): lax.all_to_all(attended.reshape(2, CAP, CHIPS, 2 * HS), RING, split_axis=...  11 us
    ppermute x4, starting transfers between devices, swap_x(): return lax.ppermute(a, 'xhi', [(0, 1), (1, 0)])  9.5 us
    all_to_all x1, waiting for transfers between devices, body(): lax.all_to_all(attended.reshape(2, CAP, CHIPS, 2 * HS), RING, split_axis=...  8.11 us
    pallas_call x1, Pallas kernels, project(): pl.pallas_call(functools.partial(project_kernel, tile), out_shape=jax.Sha...  4.85 us
    pallas_call x1, Pallas kernels, expert(): pl.pallas_call(functools.partial(expert_kernel, tile), out_shape=jax.Shap...  4.22 us
  transfers between devices with their start and end apart: 33, of which 20 were waited for; matrix products, arithmetic and copies ran while one was open for 4% of the time, Pallas kernels for 0%

profile of v2, /device:TPU:24, one launch (start us, length us, event | category | flops | bytes accessed | tf_op | source)
XLA Modules:
  0.0 197.8 jit_solution(14633632995555827673)
XLA Ops:
  0.1 1.1 copy.16
  1.2 0.7 iota_compare_fusion
  1.9 1.7 fusion.3
  3.9 0.9 convolution_convert_fusion.2
  5.0 0.6 convert_reduce_fusion.1
  5.8 0.6 subtract_select_fusion
  6.6 0.7 copy.14
  7.3 11.0 %all-to-all-start = ((bf16[2,1,8,16,512]{4,2,0,1,3:T(8,128)(2,1)}), bf16[2,1,8,16,512]{4,2,0,1,3:T(8,128)(2,1)S(1)}, u32[]{:S(2)}, u32[]{:S(2)}) async-start(bf16[2,1,8,16,512]{4,2,0,1,3:T(8,128)(2,1)} %copy.14), calls=%async_computation | async-start | bytes 524288 | tf_op jit(solution)/shard_map/all_to_all | solution.py:225
  18.6 3.5 %collective-permute-start.1 = (bf16[8,7168]{1,0:T(8,128)(2,1)S(1)}, bf16[8,7168]{1,0:T(8,128)(2,1)S(1)}, u32[]{:S(2)}, u32[]{:S(2)}) collective-permute-start(bf16[8,7168]{1,0:T(8,128)(2,1)S(1)} %slice.221), channel_id=1, source_target_pairs={{0,16},{16,0},{1,17},{17,1},{2,18},{18,2},{3,19},{19,3},{4,20},{20... | collective-permute-start | bytes 344072 | tf_op jit(solution)/shard_map/ppermute | solution.py:49
  22.2 8.1 %all-to-all-done = bf16[2,1,8,16,512]{4,2,0,1,3:T(8,128)(2,1)S(1)} async-done(((bf16[2,1,8,16,512]{4,2,0,1,3:T(8,128)(2,1)}), bf16[2,1,8,16,512]{4,2,0,1,3:T(8,128)(2,1)S(1)}, u32[]{:S(2)}, u32[]{:S(2)}) %all-to-all-start) | async-done | bytes 262176 | tf_op jit(solution)/shard_map/all_to_all | solution.py:225
  30.4 2.0 %copy-done.1 = bf16[256,7168]{1,0:T(8,128)(2,1)S(1)} copy-done((bf16[256,7168]{1,0:T(8,128)(2,1)S(1)}, bf16[256,7168]{1,0:T(8,128)(2,1)}, u32[]{:S(2)}) %copy-start.1) | copy-done | bytes 3670040
  32.4 4.8 %project.1 = bf16[256,7168]{1,0:T(8,128)(2,1)S(1)} custom-call(s32[3]{0:T(128)S(1)} %pad_add_fusion.place, bf16[2,16,8,512]{3,2,1,0:T(8,128)(2,1)S(1)} %bitcast.23, bf16[256,7168]{1,0:T(8,128)(2,1)S(1)} %copy-done.1, bf16[256,7168]{1,0:T(8,128)(2,1)} %collective-permute-done.w_oth), custom_call_target="tpu_custom_call" | custom-call | tf_op jit(solution)/shard_map/project/pallas_call | solution.py:139
  37.3 1.8 collective-permute-start.2
  39.1 1.3 collective-permute-start.6
  40.4 6.1 %collective-permute-done.2 = bf16[32,3584]{1,0:T(8,128)(2,1)S(1)} collective-permute-done((bf16[32,3584]{1,0:T(8,128)(2,1)S(1)}, bf16[32,3584]{1,0:T(8,128)(2,1)S(1)}, u32[]{:S(2)}, u32[]{:S(2)}) %collective-permute-start.2) | collective-permute-done | bytes 229408 | tf_op jit(solution)/shard_map/ppermute | solution.py:58
  47.0 3.0 %collective-permute-start.7 = (bf16[32,7168]{1,0:T(8,128)(2,1)S(1)}, bf16[32,7168]{1,0:T(8,128)(2,1)S(1)}, u32[]{:S(2)}, u32[]{:S(2)}) collective-permute-start(bf16[32,7168]{1,0:T(8,128)(2,1)S(1)} %pad_maximum_fusion.1), channel_id=1, source_target_pairs={{0,15},{1,14},{2,1},{3,0},{4,3},{5,2},{6,5},{7,4},{8,7},{9,6},{10,... | collective-permute-start | bytes 1376264 | tf_op jit(solution)/shard_map/ppermute | solution.py:58
  50.1 10.6 %collective-permute-done.3 = bf16[32,7168]{1,0:T(8,128)(2,1)S(1)} collective-permute-done((bf16[32,7168]{1,0:T(8,128)(2,1)S(1)}, bf16[32,7168]{1,0:T(8,128)(2,1)S(1)}, u32[]{:S(2)}, u32[]{:S(2)}) %collective-permute-start.3) | collective-permute-done | bytes 458784 | tf_op jit(solution)/shard_map/ppermute | solution.py:58
  60.9 13.7 %collective-permute-done.4 = bf16[32,7168]{1,0:T(8,128)(2,1)S(1)} collective-permute-done((bf16[32,7168]{1,0:T(8,128)(2,1)S(1)}, bf16[32,7168]{1,0:T(8,128)(2,1)S(1)}, u32[]{:S(2)}, u32[]{:S(2)}) %collective-permute-start.4) | collective-permute-done | bytes 458784 | tf_op jit(solution)/shard_map/ppermute | solution.py:58
  75.0 1.7 collective-permute-start.5
  76.7 10.8 %collective-permute-done.8 = bf16[32,7168]{1,0:T(8,128)(2,1)S(1)} collective-permute-done((bf16[32,7168]{1,0:T(8,128)(2,1)S(1)}, bf16[32,7168]{1,0:T(8,128)(2,1)S(1)}, u32[]{:S(2)}, u32[]{:S(2)}) %collective-permute-start.8) | collective-permute-done | bytes 458784 | tf_op jit(solution)/shard_map/ppermute | solution.py:58
  87.6 1.2 collective-permute-start.9
  88.8 11.3 %collective-permute-done.9 = bf16[32,7168]{1,0:T(8,128)(2,1)S(1)} collective-permute-done((bf16[32,7168]{1,0:T(8,128)(2,1)S(1)}, bf16[32,7168]{1,0:T(8,128)(2,1)S(1)}, u32[]{:S(2)}, u32[]{:S(2)}) %collective-permute-start.9) | collective-permute-done | bytes 458784 | tf_op jit(solution)/shard_map/ppermute | solution.py:58
  100.3 1.6 collective-permute-start.31
  102.7 2.1 %collective-permute-start.10 = (bf16[16,7168]{1,0:T(8,128)(2,1)S(1)}, bf16[16,7168]{1,0:T(8,128)(2,1)S(1)}, u32[]{:S(2)}, u32[]{:S(2)}) collective-permute-start(bf16[16,7168]{1,0:T(8,128)(2,1)S(1)} %slice.175), channel_id=1, source_target_pairs={{0,16},{16,0},{1,17},{17,1},{2,18},{18,2},{3,19},{19,3},{4,20},{20... | collective-permute-start | bytes 688136 | tf_op jit(solution)/shard_map/ppermute | solution.py:49
  104.8 2.5 %collective-permute-done.31 = bf16[8,7168]{1,0:T(8,128)(2,1)S(1)} collective-permute-done((bf16[8,7168]{1,0:T(8,128)(2,1)S(1)}, bf16[8,7168]{1,0:T(8,128)(2,1)S(1)}, u32[]{:S(2)}, u32[]{:S(2)}) %collective-permute-start.31) | collective-permute-done | bytes 114720 | tf_op jit(solution)/shard_map/ppermute | solution.py:49
  107.4 4.9 %collective-permute-done.10 = bf16[16,7168]{1,0:T(8,128)(2,1)S(1)} collective-permute-done((bf16[16,7168]{1,0:T(8,128)(2,1)S(1)}, bf16[16,7168]{1,0:T(8,128)(2,1)S(1)}, u32[]{:S(2)}, u32[]{:S(2)}) %collective-permute-start.10) | collective-permute-done | bytes 229408 | tf_op jit(solution)/shard_map/ppermute | solution.py:49
  112.7 2.9 %collective-permute-start.11 = (bf16[16,7168]{1,0:T(8,128)(2,1)S(1)}, bf16[16,7168]{1,0:T(8,128)(2,1)S(1)}, u32[]{:S(2)}, u32[]{:S(2)}) collective-permute-start(bf16[16,7168]{1,0:T(8,128)(2,1)S(1)} %multiply_convert_fusion.refs_0_), channel_id=1, source_target_pairs={{0,15},{1,14},{2,1},{3,0},{4,3},{5,2},{6,5},{7,4},{8,7},{9,6},{10,... | collective-permute-start | bytes 688136 | tf_op jit(solution)/shard_map/ppermute | solution.py:58
  115.6 6.0 %collective-permute-done.14.refs_8_ = bf16[16,7168]{1,0:T(8,128)(2,1)S(1)} collective-permute-done((bf16[16,7168]{1,0:T(8,128)(2,1)S(1)}, bf16[16,7168]{1,0:T(8,128)(2,1)S(1)}, u32[]{:S(2)}, u32[]{:S(2)}) %collective-permute-start.14) | collective-permute-done | bytes 229408 | tf_op jit(solution)/shard_map/ppermute | solution.py:58
  121.6 3.0 %collective-permute-start.12 = (bf16[16,7168]{1,0:T(8,128)(2,1)S(1)}, bf16[16,7168]{1,0:T(8,128)(2,1)S(1)}, u32[]{:S(2)}, u32[]{:S(2)}) collective-permute-start(bf16[16,7168]{1,0:T(8,128)(2,1)S(1)} %collective-permute-done.11.refs_1_), channel_id=1, source_target_pairs={{0,15},{1,14},{2,1},{3,0},{4,3},{5,2},{6,5},{7,4},{8,7},{9,6},{10,... | collective-permute-start | bytes 688136 | tf_op jit(solution)/shard_map/ppermute | solution.py:58
  124.6 5.8 %collective-permute-done.15.refs_7_ = bf16[16,7168]{1,0:T(8,128)(2,1)S(1)} collective-permute-done((bf16[16,7168]{1,0:T(8,128)(2,1)S(1)}, bf16[16,7168]{1,0:T(8,128)(2,1)S(1)}, u32[]{:S(2)}, u32[]{:S(2)}) %collective-permute-start.15) | collective-permute-done | bytes 229408 | tf_op jit(solution)/shard_map/ppermute | solution.py:58
  130.4 3.0 %collective-permute-start.13 = (bf16[16,7168]{1,0:T(8,128)(2,1)S(1)}, bf16[16,7168]{1,0:T(8,128)(2,1)S(1)}, u32[]{:S(2)}, u32[]{:S(2)}) collective-permute-start(bf16[16,7168]{1,0:T(8,128)(2,1)S(1)} %collective-permute-done.12.refs_2_), channel_id=1, source_target_pairs={{0,15},{1,14},{2,1},{3,0},{4,3},{5,2},{6,5},{7,4},{8,7},{9,6},{10,... | collective-permute-start | bytes 688136 | tf_op jit(solution)/shard_map/ppermute | solution.py:58
  133.4 5.9 %collective-permute-done.16.refs_6_ = bf16[16,7168]{1,0:T(8,128)(2,1)S(1)} collective-permute-done((bf16[16,7168]{1,0:T(8,128)(2,1)S(1)}, bf16[16,7168]{1,0:T(8,128)(2,1)S(1)}, u32[]{:S(2)}, u32[]{:S(2)}) %collective-permute-start.16) | collective-permute-done | bytes 229408 | tf_op jit(solution)/shard_map/ppermute | solution.py:58
  139.3 3.2 %collective-permute-start.18 = (bf16[16,3584]{1,0:T(8,128)(2,1)S(1)}, bf16[16,3584]{1,0:T(8,128)(2,1)S(1)}, u32[]{:S(2)}, u32[]{:S(2)}) collective-permute-start(bf16[16,3584]{1,0:T(8,128)(2,1)S(1)} %slice.180), channel_id=1, source_target_pairs={{0,15},{1,14},{2,1},{3,0},{4,3},{5,2},{6,5},{7,4},{8,7},{9,6},{10,... | collective-permute-start | bytes 344072 | tf_op jit(solution)/shard_map/ppermute | solution.py:58
  142.6 3.1 %collective-permute-done.17.refs_4_ = bf16[16,3584]{1,0:T(8,128)(2,1)S(1)} collective-permute-done((bf16[16,3584]{1,0:T(8,128)(2,1)S(1)}, bf16[16,3584]{1,0:T(8,128)(2,1)S(1)}, u32[]{:S(2)}, u32[]{:S(2)}) %collective-permute-start.17) | collective-permute-done | bytes 114720 | tf_op jit(solution)/shard_map/ppermute | solution.py:58
  145.7 4.2 %expert.1 = bf16[128,7168]{1,0:T(8,128)(2,1)S(1)} custom-call(bf16[16,7168]{1,0:T(8,128)(2,1)S(1)} %multiply_convert_fusion.refs_0_, bf16[16,7168]{1,0:T(8,128)(2,1)S(1)} %collective-permute-done.11.refs_1_, bf16[16,7168]{1,0:T(8,128)(2,1)S(1)} %collective-permute-done.12.refs_2_, bf16[16,7168]{1,0:T(8,128)(2,1)S(1)} %collective-permute-done.13.refs_3_, ...), custom_call_target="tpu_custom_call" | custom-call | tf_op jit(solution)/shard_map/expert/pallas_call | solution.py:180
  150.0 3.1 %collective-permute-start.26 = (bf16[16,3584]{1,0:T(8,128)(2,1)S(1)}, bf16[16,3584]{1,0:T(8,128)(2,1)S(1)}, u32[]{:S(2)}, u32[]{:S(2)}) collective-permute-start(bf16[16,3584]{1,0:T(8,128)(2,1)S(1)} %get-tuple-element.34), channel_id=1, source_target_pairs={{0,15},{1,14},{2,1},{3,0},{4,3},{5,2},{6,5},{7,4},{8,7},{9,6},{10,... | collective-permute-start | bytes 344072 | tf_op jit(solution)/shard_map/ppermute | solution.py:58
  153.1 3.3 %collective-permute-done.22 = bf16[16,3584]{1,0:T(8,128)(2,1)S(1)} collective-permute-done((bf16[16,3584]{1,0:T(8,128)(2,1)S(1)}, bf16[16,3584]{1,0:T(8,128)(2,1)S(1)}, u32[]{:S(2)}, u32[]{:S(2)}) %collective-permute-start.22) | collective-permute-done | bytes 114720 | tf_op jit(solution)/shard_map/ppermute | solution.py:58
  156.5 1.3 collective-permute-start.23
  157.8 1.9 collective-permute-start.27
  159.7 5.8 %collective-permute-done.23 = bf16[16,7168]{1,0:T(8,128)(2,1)S(1)} collective-permute-done((bf16[16,7168]{1,0:T(8,128)(2,1)S(1)}, bf16[16,7168]{1,0:T(8,128)(2,1)S(1)}, u32[]{:S(2)}, u32[]{:S(2)}) %collective-permute-start.23) | collective-permute-done | bytes 229408 | tf_op jit(solution)/shard_map/ppermute | solution.py:58
  165.7 8.6 %collective-permute-done.24 = bf16[16,7168]{1,0:T(8,128)(2,1)S(1)} collective-permute-done((bf16[16,7168]{1,0:T(8,128)(2,1)S(1)}, bf16[16,7168]{1,0:T(8,128)(2,1)S(1)}, u32[]{:S(2)}, u32[]{:S(2)}) %collective-permute-start.24) | collective-permute-done | bytes 229408 | tf_op jit(solution)/shard_map/ppermute | solution.py:58
  174.9 1.4 collective-permute-start.25
  176.3 5.9 %collective-permute-done.28 = bf16[16,7168]{1,0:T(8,128)(2,1)S(1)} collective-permute-done((bf16[16,7168]{1,0:T(8,128)(2,1)S(1)}, bf16[16,7168]{1,0:T(8,128)(2,1)S(1)}, u32[]{:S(2)}, u32[]{:S(2)}) %collective-permute-start.28) | collective-permute-done | bytes 229408 | tf_op jit(solution)/shard_map/ppermute | solution.py:58
  182.2 1.3 collective-permute-start.29
  183.8 5.9 %collective-permute-done.29 = bf16[16,7168]{1,0:T(8,128)(2,1)S(1)} collective-permute-done((bf16[16,7168]{1,0:T(8,128)(2,1)S(1)}, bf16[16,7168]{1,0:T(8,128)(2,1)S(1)}, u32[]{:S(2)}, u32[]{:S(2)}) %collective-permute-start.29) | collective-permute-done | bytes 229408 | tf_op jit(solution)/shard_map/ppermute | solution.py:58
  189.8 2.3 %collective-permute-start.30 = (bf16[8,7168]{1,0:T(8,128)(2,1)S(1)}, bf16[8,7168]{1,0:T(8,128)(2,1)S(1)}, u32[]{:S(2)}, u32[]{:S(2)}) collective-permute-start(bf16[8,7168]{1,0:T(8,128)(2,1)S(1)} %slice.193), channel_id=1, source_target_pairs={{0,16},{16,0},{1,17},{17,1},{2,18},{18,2},{3,19},{19,3},{4,20},{20... | collective-permute-start | bytes 344072 | tf_op jit(solution)/shard_map/ppermute | solution.py:49
  192.1 4.6 %collective-permute-done.30 = bf16[8,7168]{1,0:T(8,128)(2,1)S(1)} collective-permute-done((bf16[8,7168]{1,0:T(8,128)(2,1)S(1)}, bf16[8,7168]{1,0:T(8,128)(2,1)S(1)}, u32[]{:S(2)}, u32[]{:S(2)}) %collective-permute-start.30) | collective-permute-done | bytes 114720 | tf_op jit(solution)/shard_map/ppermute | solution.py:49
  196.9 1.0 convolution_convert_fusion.1
  (83 shorter events, 5.4 us)
Async XLA Ops:
  0.0 3.9 %copy-start = (bf16[16,128,256]{2,1,0:T(8,128)(2,1)S(1)}, bf16[16,128,256]{2,1,0:T(8,128)(2,1)}, u32[]{:S(2)}) copy-start(bf16[16,128,256]{2,1,0:T(8,128)(2,1)} %param.13) | copy-start | bytes 3145732
  0.0 5.0 %copy-start.6 = (f32[16,3]{0,1:T(4,128)S(1)}, f32[16,3]{0,1:T(4,128)}, u32[]{:S(2)}) copy-start(f32[16,3]{0,1:T(4,128)} %param.18) | copy-start | bytes 580
  0.0 5.0 %copy-start.7 = (s32[16,3]{0,1:T(4,128)S(1)}, s32[16,3]{0,1:T(4,128)}, u32[]{:S(2)}) copy-start(s32[16,3]{0,1:T(4,128)} %param.17) | copy-start | bytes 580
  0.0 30.3 %collective-permute-start = (bf16[256,7168]{1,0:T(8,128)(2,1)}, bf16[256,7168]{1,0:T(8,128)(2,1)}, u32[]{:S(2)}, u32[]{:S(2)}) collective-permute-start(bf16[256,7168]{1,0:T(8,128)(2,1)} %w_own.1), channel_id=1, source_target_pairs={{0,1},{1,0},{2,3},{3,2},{4,5},{5,4},{6,7},{7,6},{8,9},{9,8},{10,11... | collective-permute-start | bytes 11010056 | tf_op jit(solution)/shard_map/ppermute | solution.py:45
  3.6 14.8 %copy-start.5 = (bf16[16,7168]{1,0:T(8,128)(2,1)S(1)}, bf16[16,7168]{1,0:T(8,128)(2,1)}, u32[]{:S(2)}) copy-start(bf16[16,7168]{1,0:T(8,128)(2,1)} %param.16) | copy-start | bytes 688132
  7.3 23.0 %all-to-all-start = ((bf16[2,1,8,16,512]{4,2,0,1,3:T(8,128)(2,1)}), bf16[2,1,8,16,512]{4,2,0,1,3:T(8,128)(2,1)S(1)}, u32[]{:S(2)}, u32[]{:S(2)}) async-start(bf16[2,1,8,16,512]{4,2,0,1,3:T(8,128)(2,1)} %copy.14), calls=%async_computation | async-start | bytes 524288 | tf_op jit(solution)/shard_map/all_to_all | solution.py:225
  18.6 11.7 %collective-permute-start.1 = (bf16[8,7168]{1,0:T(8,128)(2,1)S(1)}, bf16[8,7168]{1,0:T(8,128)(2,1)S(1)}, u32[]{:S(2)}, u32[]{:S(2)}) collective-permute-start(bf16[8,7168]{1,0:T(8,128)(2,1)S(1)} %slice.221), channel_id=1, source_target_pairs={{0,16},{16,0},{1,17},{17,1},{2,18},{18,2},{3,19},{19,3},{4,20},{20... | collective-permute-start | bytes 344072 | tf_op jit(solution)/shard_map/ppermute | solution.py:49
  30.4 2.0 %copy-start.1 = (bf16[256,7168]{1,0:T(8,128)(2,1)S(1)}, bf16[256,7168]{1,0:T(8,128)(2,1)}, u32[]{:S(2)}) copy-start(bf16[256,7168]{1,0:T(8,128)(2,1)} %w_own.1) | copy-start | bytes 11010052
  37.3 9.2 %collective-permute-start.2 = (bf16[32,3584]{1,0:T(8,128)(2,1)S(1)}, bf16[32,3584]{1,0:T(8,128)(2,1)S(1)}, u32[]{:S(2)}, u32[]{:S(2)}) collective-permute-start(bf16[32,3584]{1,0:T(8,128)(2,1)S(1)} %get-tuple-element.25), channel_id=1, source_target_pairs={{0,3},{1,2},{2,5},{3,4},{4,7},{5,6},{6,9},{7,8},{8,11},{9,10},{10,... | collective-permute-start | bytes 688136 | tf_op jit(solution)/shard_map/ppermute | solution.py:58
  39.1 7.6 %collective-permute-start.6 = (bf16[32,3584]{1,0:T(8,128)(2,1)S(1)}, bf16[32,3584]{1,0:T(8,128)(2,1)S(1)}, u32[]{:S(2)}, u32[]{:S(2)}) collective-permute-start(bf16[32,3584]{1,0:T(8,128)(2,1)S(1)} %get-tuple-element.26), channel_id=1, source_target_pairs={{0,15},{1,14},{2,1},{3,0},{4,3},{5,2},{6,5},{7,4},{8,7},{9,6},{10,... | collective-permute-start | bytes 688136 | tf_op jit(solution)/shard_map/ppermute | solution.py:58
  46.9 13.8 %collective-permute-start.3 = (bf16[32,7168]{1,0:T(8,128)(2,1)S(1)}, bf16[32,7168]{1,0:T(8,128)(2,1)S(1)}, u32[]{:S(2)}, u32[]{:S(2)}) collective-permute-start(bf16[32,7168]{1,0:T(8,128)(2,1)S(1)} %pad_maximum_fusion), channel_id=1, source_target_pairs={{0,3},{1,2},{2,5},{3,4},{4,7},{5,6},{6,9},{7,8},{8,11},{9,10},{10,... | collective-permute-start | bytes 1376264 | tf_op jit(solution)/shard_map/ppermute | solution.py:58
  47.0 13.9 %collective-permute-start.7 = (bf16[32,7168]{1,0:T(8,128)(2,1)S(1)}, bf16[32,7168]{1,0:T(8,128)(2,1)S(1)}, u32[]{:S(2)}, u32[]{:S(2)}) collective-permute-start(bf16[32,7168]{1,0:T(8,128)(2,1)S(1)} %pad_maximum_fusion.1), channel_id=1, source_target_pairs={{0,15},{1,14},{2,1},{3,0},{4,3},{5,2},{6,5},{7,4},{8,7},{9,6},{10,... | collective-permute-start | bytes 1376264 | tf_op jit(solution)/shard_map/ppermute | solution.py:58
  60.7 41.9 %copy-start.4 = (bf16[160,7168]{1,0:T(8,128)(2,1)S(1)}, bf16[160,7168]{1,0:T(8,128)(2,1)}, u32[]{:S(2)}) copy-start(bf16[160,7168]{1,0:T(8,128)(2,1)} %refs_13_) | copy-start | bytes 6881284
  60.8 13.8 %collective-permute-start.4 = (bf16[32,7168]{1,0:T(8,128)(2,1)S(1)}, bf16[32,7168]{1,0:T(8,128)(2,1)S(1)}, u32[]{:S(2)}, u32[]{:S(2)}) collective-permute-start(bf16[32,7168]{1,0:T(8,128)(2,1)S(1)} %add_convert_fusion.4), channel_id=1, source_target_pairs={{0,3},{1,2},{2,5},{3,4},{4,7},{5,6},{6,9},{7,8},{8,11},{9,10},{10,... | collective-permute-start | bytes 1376264 | tf_op jit(solution)/shard_map/ppermute | solution.py:58
  74.6 27.5 %copy-start.3 = (bf16[160,7168]{1,0:T(8,128)(2,1)S(1)}, bf16[160,7168]{1,0:T(8,128)(2,1)}, u32[]{:S(2)}) copy-start(bf16[160,7168]{1,0:T(8,128)(2,1)} %refs_11_) | copy-start | bytes 6881284
  74.9 27.1 %copy-start.2 = (bf16[160,7168]{1,0:T(8,128)(2,1)S(1)}, bf16[160,7168]{1,0:T(8,128)(2,1)}, u32[]{:S(2)}) copy-start(bf16[160,7168]{1,0:T(8,128)(2,1)} %refs_9_) | copy-start | bytes 6881284
  74.9 12.6 %collective-permute-start.8 = (bf16[32,7168]{1,0:T(8,128)(2,1)S(1)}, bf16[32,7168]{1,0:T(8,128)(2,1)S(1)}, u32[]{:S(2)}, u32[]{:S(2)}) collective-permute-start(bf16[32,7168]{1,0:T(8,128)(2,1)S(1)} %get-tuple-element.22), channel_id=1, source_target_pairs={{0,15},{1,14},{2,1},{3,0},{4,3},{5,2},{6,5},{7,4},{8,7},{9,6},{10,... | collective-permute-start | bytes 1376264 | tf_op jit(solution)/shard_map/ppermute | solution.py:58
  75.0 13.8 %collective-permute-start.5 = (bf16[32,7168]{1,0:T(8,128)(2,1)S(1)}, bf16[32,7168]{1,0:T(8,128)(2,1)S(1)}, u32[]{:S(2)}, u32[]{:S(2)}) collective-permute-start(bf16[32,7168]{1,0:T(8,128)(2,1)S(1)} %get-tuple-element.21), channel_id=1, source_target_pairs={{0,3},{1,2},{2,5},{3,4},{4,7},{5,6},{6,9},{7,8},{8,11},{9,10},{10,... | collective-permute-start | bytes 1376264 | tf_op jit(solution)/shard_map/ppermute | solution.py:58
  87.6 12.5 %collective-permute-start.9 = (bf16[32,7168]{1,0:T(8,128)(2,1)S(1)}, bf16[32,7168]{1,0:T(8,128)(2,1)S(1)}, u32[]{:S(2)}, u32[]{:S(2)}) collective-permute-start(bf16[32,7168]{1,0:T(8,128)(2,1)S(1)} %add_convert_fusion.1), channel_id=1, source_target_pairs={{0,15},{1,14},{2,1},{3,0},{4,3},{5,2},{6,5},{7,4},{8,7},{9,6},{10,... | collective-permute-start | bytes 1376264 | tf_op jit(solution)/shard_map/ppermute | solution.py:58
  100.3 7.0 %collective-permute-start.31 = (bf16[8,7168]{1,0:T(8,128)(2,1)S(1)}, bf16[8,7168]{1,0:T(8,128)(2,1)S(1)}, u32[]{:S(2)}, u32[]{:S(2)}) collective-permute-start(bf16[8,7168]{1,0:T(8,128)(2,1)S(1)} %slice.196), channel_id=1, source_target_pairs={{0,16},{16,0},{1,17},{17,1},{2,18},{18,2},{3,19},{19,3},{4,20},{20... | collective-permute-start | bytes 344072 | tf_op jit(solution)/shard_map/ppermute | solution.py:49
  102.0 40.6 %collective-permute-start.19 = (bf16[160,7168]{1,0:T(8,128)(2,1)S(1)}, bf16[160,7168]{1,0:T(8,128)(2,1)S(1)}, u32[]{:S(2)}, u32[]{:S(2)}) collective-permute-start(bf16[160,7168]{1,0:T(8,128)(2,1)S(1)} %copy-done.2), channel_id=1, source_target_pairs={{0,1},{1,0},{2,3},{3,2},{4,5},{5,4},{6,7},{7,6},{8,9},{9,8},{10,11... | collective-permute-start | bytes 6881288 | tf_op jit(solution)/shard_map/ppermute | solution.py:45
  102.1 40.5 %collective-permute-start.20 = (bf16[160,7168]{1,0:T(8,128)(2,1)S(1)}, bf16[160,7168]{1,0:T(8,128)(2,1)S(1)}, u32[]{:S(2)}, u32[]{:S(2)}) collective-permute-start(bf16[160,7168]{1,0:T(8,128)(2,1)S(1)} %copy-done.3), channel_id=1, source_target_pairs={{0,1},{1,0},{2,3},{3,2},{4,5},{5,4},{6,7},{7,6},{8,9},{9,8},{10,11... | collective-permute-start | bytes 6881288 | tf_op jit(solution)/shard_map/ppermute | solution.py:45
  102.6 40.0 %collective-permute-start.21 = (bf16[160,7168]{1,0:T(8,128)(2,1)S(1)}, bf16[160,7168]{1,0:T(8,128)(2,1)S(1)}, u32[]{:S(2)}, u32[]{:S(2)}) collective-permute-start(bf16[160,7168]{1,0:T(8,128)(2,1)S(1)} %copy-done.4), channel_id=1, source_target_pairs={{0,1},{1,0},{2,3},{3,2},{4,5},{5,4},{6,7},{7,6},{8,9},{9,8},{10,11... | collective-permute-start | bytes 6881288 | tf_op jit(solution)/shard_map/ppermute | solution.py:45
  102.7 9.5 %collective-permute-start.10 = (bf16[16,7168]{1,0:T(8,128)(2,1)S(1)}, bf16[16,7168]{1,0:T(8,128)(2,1)S(1)}, u32[]{:S(2)}, u32[]{:S(2)}) collective-permute-start(bf16[16,7168]{1,0:T(8,128)(2,1)S(1)} %slice.175), channel_id=1, source_target_pairs={{0,16},{16,0},{1,17},{17,1},{2,18},{18,2},{3,19},{19,3},{4,20},{20... | collective-permute-start | bytes 688136 | tf_op jit(solution)/shard_map/ppermute | solution.py:49
  112.6 9.0 %collective-permute-start.14 = (bf16[16,7168]{1,0:T(8,128)(2,1)S(1)}, bf16[16,7168]{1,0:T(8,128)(2,1)S(1)}, u32[]{:S(2)}, u32[]{:S(2)}) collective-permute-start(bf16[16,7168]{1,0:T(8,128)(2,1)S(1)} %multiply_convert_fusion.refs_0_), channel_id=1, source_target_pairs={{0,3},{1,2},{2,5},{3,4},{4,7},{5,6},{6,9},{7,8},{8,11},{9,10},{10,... | collective-permute-start | bytes 688136 | tf_op jit(solution)/shard_map/ppermute | solution.py:58
  112.7 8.9 %collective-permute-start.11 = (bf16[16,7168]{1,0:T(8,128)(2,1)S(1)}, bf16[16,7168]{1,0:T(8,128)(2,1)S(1)}, u32[]{:S(2)}, u32[]{:S(2)}) collective-permute-start(bf16[16,7168]{1,0:T(8,128)(2,1)S(1)} %multiply_convert_fusion.refs_0_), channel_id=1, source_target_pairs={{0,15},{1,14},{2,1},{3,0},{4,3},{5,2},{6,5},{7,4},{8,7},{9,6},{10,... | collective-permute-start | bytes 688136 | tf_op jit(solution)/shard_map/ppermute | solution.py:58
  121.6 8.8 %collective-permute-start.15 = (bf16[16,7168]{1,0:T(8,128)(2,1)S(1)}, bf16[16,7168]{1,0:T(8,128)(2,1)S(1)}, u32[]{:S(2)}, u32[]{:S(2)}) collective-permute-start(bf16[16,7168]{1,0:T(8,128)(2,1)S(1)} %collective-permute-done.14.refs_8_), channel_id=1, source_target_pairs={{0,3},{1,2},{2,5},{3,4},{4,7},{5,6},{6,9},{7,8},{8,11},{9,10},{10,... | collective-permute-start | bytes 688136 | tf_op jit(solution)/shard_map/ppermute | solution.py:58
  121.6 8.8 %collective-permute-start.12 = (bf16[16,7168]{1,0:T(8,128)(2,1)S(1)}, bf16[16,7168]{1,0:T(8,128)(2,1)S(1)}, u32[]{:S(2)}, u32[]{:S(2)}) collective-permute-start(bf16[16,7168]{1,0:T(8,128)(2,1)S(1)} %collective-permute-done.11.refs_1_), channel_id=1, source_target_pairs={{0,15},{1,14},{2,1},{3,0},{4,3},{5,2},{6,5},{7,4},{8,7},{9,6},{10,... | collective-permute-start | bytes 688136 | tf_op jit(solution)/shard_map/ppermute | solution.py:58
  130.4 8.8 %collective-permute-start.16 = (bf16[16,7168]{1,0:T(8,128)(2,1)S(1)}, bf16[16,7168]{1,0:T(8,128)(2,1)S(1)}, u32[]{:S(2)}, u32[]{:S(2)}) collective-permute-start(bf16[16,7168]{1,0:T(8,128)(2,1)S(1)} %collective-permute-done.15.refs_7_), channel_id=1, source_target_pairs={{0,3},{1,2},{2,5},{3,4},{4,7},{5,6},{6,9},{7,8},{8,11},{9,10},{10,... | collective-permute-start | bytes 688136 | tf_op jit(solution)/shard_map/ppermute | solution.py:58
  130.4 8.9 %collective-permute-start.13 = (bf16[16,7168]{1,0:T(8,128)(2,1)S(1)}, bf16[16,7168]{1,0:T(8,128)(2,1)S(1)}, u32[]{:S(2)}, u32[]{:S(2)}) collective-permute-start(bf16[16,7168]{1,0:T(8,128)(2,1)S(1)} %collective-permute-done.12.refs_2_), channel_id=1, source_target_pairs={{0,15},{1,14},{2,1},{3,0},{4,3},{5,2},{6,5},{7,4},{8,7},{9,6},{10,... | collective-permute-start | bytes 688136 | tf_op jit(solution)/shard_map/ppermute | solution.py:58
  139.2 6.4 %collective-permute-start.17 = (bf16[16,3584]{1,0:T(8,128)(2,1)S(1)}, bf16[16,3584]{1,0:T(8,128)(2,1)S(1)}, u32[]{:S(2)}, u32[]{:S(2)}) collective-permute-start(bf16[16,3584]{1,0:T(8,128)(2,1)S(1)} %slice.179), channel_id=1, source_target_pairs={{0,3},{1,2},{2,5},{3,4},{4,7},{5,6},{6,9},{7,8},{8,11},{9,10},{10,... | collective-permute-start | bytes 344072 | tf_op jit(solution)/shard_map/ppermute | solution.py:58
  139.3 6.3 %collective-permute-start.18 = (bf16[16,3584]{1,0:T(8,128)(2,1)S(1)}, bf16[16,3584]{1,0:T(8,128)(2,1)S(1)}, u32[]{:S(2)}, u32[]{:S(2)}) collective-permute-start(bf16[16,3584]{1,0:T(8,128)(2,1)S(1)} %slice.180), channel_id=1, source_target_pairs={{0,15},{1,14},{2,1},{3,0},{4,3},{5,2},{6,5},{7,4},{8,7},{9,6},{10,... | collective-permute-start | bytes 344072 | tf_op jit(solution)/shard_map/ppermute | solution.py:58
  149.9 6.5 %collective-permute-start.22 = (bf16[16,3584]{1,0:T(8,128)(2,1)S(1)}, bf16[16,3584]{1,0:T(8,128)(2,1)S(1)}, u32[]{:S(2)}, u32[]{:S(2)}) collective-permute-start(bf16[16,3584]{1,0:T(8,128)(2,1)S(1)} %get-tuple-element.33), channel_id=1, source_target_pairs={{0,3},{1,2},{2,5},{3,4},{4,7},{5,6},{6,9},{7,8},{8,11},{9,10},{10,... | collective-permute-start | bytes 344072 | tf_op jit(solution)/shard_map/ppermute | solution.py:58
  150.0 6.4 %collective-permute-start.26 = (bf16[16,3584]{1,0:T(8,128)(2,1)S(1)}, bf16[16,3584]{1,0:T(8,128)(2,1)S(1)}, u32[]{:S(2)}, u32[]{:S(2)}) collective-permute-start(bf16[16,3584]{1,0:T(8,128)(2,1)S(1)} %get-tuple-element.34), channel_id=1, source_target_pairs={{0,15},{1,14},{2,1},{3,0},{4,3},{5,2},{6,5},{7,4},{8,7},{9,6},{10,... | collective-permute-start | bytes 344072 | tf_op jit(solution)/shard_map/ppermute | solution.py:58
  156.5 8.9 %collective-permute-start.23 = (bf16[16,7168]{1,0:T(8,128)(2,1)S(1)}, bf16[16,7168]{1,0:T(8,128)(2,1)S(1)}, u32[]{:S(2)}, u32[]{:S(2)}) collective-permute-start(bf16[16,7168]{1,0:T(8,128)(2,1)S(1)} %pad_maximum_fusion.2), channel_id=1, source_target_pairs={{0,3},{1,2},{2,5},{3,4},{4,7},{5,6},{6,9},{7,8},{8,11},{9,10},{10,... | collective-permute-start | bytes 688136 | tf_op jit(solution)/shard_map/ppermute | solution.py:58
  157.8 7.9 %collective-permute-start.27 = (bf16[16,7168]{1,0:T(8,128)(2,1)S(1)}, bf16[16,7168]{1,0:T(8,128)(2,1)S(1)}, u32[]{:S(2)}, u32[]{:S(2)}) collective-permute-start(bf16[16,7168]{1,0:T(8,128)(2,1)S(1)} %pad_maximum_fusion.3), channel_id=1, source_target_pairs={{0,15},{1,14},{2,1},{3,0},{4,3},{5,2},{6,5},{7,4},{8,7},{9,6},{10,... | collective-permute-start | bytes 688136 | tf_op jit(solution)/shard_map/ppermute | solution.py:58
  165.5 8.9 %collective-permute-start.24 = (bf16[16,7168]{1,0:T(8,128)(2,1)S(1)}, bf16[16,7168]{1,0:T(8,128)(2,1)S(1)}, u32[]{:S(2)}, u32[]{:S(2)}) collective-permute-start(bf16[16,7168]{1,0:T(8,128)(2,1)S(1)} %add_convert_fusion.9), channel_id=1, source_target_pairs={{0,3},{1,2},{2,5},{3,4},{4,7},{5,6},{6,9},{7,8},{8,11},{9,10},{10,... | collective-permute-start | bytes 688136 | tf_op jit(solution)/shard_map/ppermute | solution.py:58
  174.5 7.7 %collective-permute-start.28 = (bf16[16,7168]{1,0:T(8,128)(2,1)S(1)}, bf16[16,7168]{1,0:T(8,128)(2,1)S(1)}, u32[]{:S(2)}, u32[]{:S(2)}) collective-permute-start(bf16[16,7168]{1,0:T(8,128)(2,1)S(1)} %get-tuple-element.30), channel_id=1, source_target_pairs={{0,15},{1,14},{2,1},{3,0},{4,3},{5,2},{6,5},{7,4},{8,7},{9,6},{10,... | collective-permute-start | bytes 688136 | tf_op jit(solution)/shard_map/ppermute | solution.py:58
  174.9 8.9 %collective-permute-start.25 = (bf16[16,7168]{1,0:T(8,128)(2,1)S(1)}, bf16[16,7168]{1,0:T(8,128)(2,1)S(1)}, u32[]{:S(2)}, u32[]{:S(2)}) collective-permute-start(bf16[16,7168]{1,0:T(8,128)(2,1)S(1)} %get-tuple-element.29), channel_id=1, source_target_pairs={{0,3},{1,2},{2,5},{3,4},{4,7},{5,6},{6,9},{7,8},{8,11},{9,10},{10,... | collective-permute-start | bytes 688136 | tf_op jit(solution)/shard_map/ppermute | solution.py:58
  182.2 7.4 %collective-permute-start.29 = (bf16[16,7168]{1,0:T(8,128)(2,1)S(1)}, bf16[16,7168]{1,0:T(8,128)(2,1)S(1)}, u32[]{:S(2)}, u32[]{:S(2)}) collective-permute-start(bf16[16,7168]{1,0:T(8,128)(2,1)S(1)} %add_convert_fusion.6), channel_id=1, source_target_pairs={{0,15},{1,14},{2,1},{3,0},{4,3},{5,2},{6,5},{7,4},{8,7},{9,6},{10,... | collective-permute-start | bytes 688136 | tf_op jit(solution)/shard_map/ppermute | solution.py:58
  189.8 7.0 %collective-permute-start.30 = (bf16[8,7168]{1,0:T(8,128)(2,1)S(1)}, bf16[8,7168]{1,0:T(8,128)(2,1)S(1)}, u32[]{:S(2)}, u32[]{:S(2)}) collective-permute-start(bf16[8,7168]{1,0:T(8,128)(2,1)S(1)} %slice.193), channel_id=1, source_target_pairs={{0,16},{16,0},{1,17},{17,1},{2,18},{18,2},{3,19},{19,3},{4,20},{20... | collective-permute-start | bytes 344072 | tf_op jit(solution)/shard_map/ppermute | solution.py:49

commit v3 on v2

--- a/solution.py
+++ b/solution.py
@@ -17,10 +17,7 @@
 CHIPS = NX * NZ
 ROWS = 16
 AXES = ("y", "xlo", "xhi", "z", "core")
-RING = ("xhi", "z", "core")
-TEAMS = [
-    [(x * NZ + z) * 2 + (z + odd) % 2 for x in range(NX) for z in range(NZ)] for odd in range(2)
-]
+RING = ("xhi", "z")
 
 
 def attend(queries, key_cache, value_cache, lengths):
@@ -50,12 +47,7 @@
 
 
 def shift(a, by):
-    moves = [
-        (2 * z + core, 2 * ((z + by) % NZ) + (core + by) % 2)
-        for z in range(NZ)
-        for core in range(2)
-    ]
-    return lax.ppermute(a, ("z", "core"), moves)
+    return lax.ppermute(a, "z", [(i, (i + by) % NZ) for i in range(NZ)])
 
 
 def add(*terms):
@@ -69,16 +61,18 @@
     return add(*terms).astype(jnp.bfloat16)
 
 
-def sum_z(part):
+def sum_z(part, beside=None):
     half = part[0].shape[-1] // 2
     up, down = shift(part[4][:, :half], 1), shift(part[4][:, half:], -1)
     up = shift(add_part(part[3], up, 0), 1)
     down = shift(add_part(part[5], down, half), -1)
     up = shift(add16(part[2], up), 1)
     down = shift(add16(part[6], down), -1)
+    if beside is not None:
+        up, down, beside = lax.optimization_barrier((up, down, beside))
     up = shift(add16(part[1], up), 1)
     down = shift(add16(part[7], down), -1)
-    return add16(part[0], up, down)
+    return add16(part[0], up, down), beside
 
 
 def add_part(whole, piece, at):
@@ -101,7 +95,7 @@
     return [mine, b1, b2, b3, a4, b4, a3, a2, a1]
 
 
-def project_kernel(tile, place, a, w_own, w_oth, out, held, sems):
+def project_kernel(tile, place, a, w_own, w_oth, out, near, far, held, sems):
     steps, depth = D // tile, w_own.shape[0]
     moves = [
         [
@@ -113,13 +107,13 @@
     for move in moves:
         for copy in move:
             copy.start()
+    pairs = [(rx, rz) for rx in range(NX) for rz in range(NZ)]
     blocks = []
-    for rz in range(NZ):
-        for kind in range(a.shape[0]):
-            for rx in range(NX):
-                x = lax.rem(place[0] + rx, NX)
-                z = lax.rem(place[1] + rz, NZ)
-                blocks.append(a[kind, x * NZ + z].astype(jnp.float32))
+    for kind, order in enumerate((sorted(pairs, key=lambda p: p[1]), pairs)):
+        for rx, rz in order:
+            x = lax.rem(place[0] + rx, NX)
+            z = lax.rem(place[1] + rz, NZ)
+            blocks.append(a[kind, x * NZ + z].astype(jnp.float32))
     rows = jnp.concatenate(blocks, axis=0)
     first = place[2] == 0
     own = jnp.where(first, rows[:, :depth], rows[:, depth:]).astype(jnp.bfloat16)
@@ -129,23 +123,28 @@
             copy.wait()
         total = jnp.dot(own, held[0, i], preferred_element_type=jnp.float32)
         total += jnp.dot(oth, held[1, i], preferred_element_type=jnp.float32)
-        out[:, i * tile : (i + 1) * tile] = total.astype(jnp.bfloat16)
+        total = total.astype(jnp.bfloat16)
+        at = slice(i * tile, (i + 1) * tile)
+        top, middle = out.shape[0], out.shape[0] + near.shape[0]
+        out[:, at], near[:, at], far[:, at] = total[:top], total[top:middle], total[middle:]
 
 
 def project(place, attended, w_own, w_oth, tile=1024):
-    rows, depth = math.prod(attended.shape[:3]), w_own.shape[0]
+    rows, depth = CHIPS * attended.shape[2], w_own.shape[0]
     whole = pl.BlockSpec(memory_space=pltpu.VMEM)
     anywhere = pl.BlockSpec(memory_space=pl.ANY)
     return pl.pallas_call(
         functools.partial(project_kernel, tile),
-        out_shape=jax.ShapeDtypeStruct((rows, D), jnp.bfloat16),
+        out_shape=[
+            jax.ShapeDtypeStruct((n, D), jnp.bfloat16) for n in (rows, rows // NX, rows // NX)
+        ],
         in_specs=[pl.BlockSpec(memory_space=pltpu.SMEM), whole, anywhere, anywhere],
-        out_specs=whole,
+        out_specs=[whole] * 3,
         scratch_shapes=[
             pltpu.VMEM((2, D // tile, depth, tile), jnp.bfloat16),
             pltpu.SemaphoreType.DMA((2, D // tile)),
         ],
-        compiler_params=pltpu.CompilerParams(vmem_limit_bytes=32 * 1024 * 1024),
+        compiler_params=pltpu.CompilerParams(vmem_limit_bytes=58 * 1024 * 1024),
         name="project",
     )(place, attended, w_own, w_oth)
 
@@ -219,33 +218,35 @@
     share = jnp.sum(jnp.where(order, share[None, :], 0.0), axis=1)
 
     res = jnp.dot(order16, residual, preferred_element_type=jnp.float32)
-    res_oth = swap_x(res[:CAP].astype(jnp.bfloat16))
     attended = attend(queries, key_cache, value_cache, lengths)
     attended = jnp.dot(order16, attended, preferred_element_type=jnp.float32).astype(jnp.bfloat16)
     by_heads = lax.all_to_all(
-        attended.reshape(2, CAP, CHIPS, 2 * HS), RING, split_axis=2, concat_axis=1,
-        axis_index_groups=TEAMS,
+        attended.reshape(2, CAP, CHIPS, 2 * HS), RING, split_axis=2, concat_axis=1
     )
-    by_heads, o_oth, res_oth, w_gate, w_up, w_down = lax.optimization_barrier(
-        (by_heads, o_oth, res_oth, w_gate, w_up, w_down)
+    by_heads, o_oth, w_gate, w_up, w_down = lax.optimization_barrier(
+        (by_heads, o_oth, w_gate, w_up, w_down)
     )
     g_oth, u_oth, d_oth = swap_cores(w_gate), swap_cores(w_up), swap_cores(w_down)
-    pair_res = jnp.concatenate([res[:CAP], res_oth.astype(jnp.float32)], axis=0)
-    mine = sum_z(cut(project(place, by_heads, out_proj, o_oth)))
-
-    theirs = swap_x(mine[: NX * CAP])
-    pair = pair_res + add(mine[: NX * CAP], jnp.concatenate([theirs[CAP:], theirs[:CAP]], axis=0))
+    parts, near, far = project(place, by_heads, out_proj, o_oth)
+    mine, far = sum_z(cut(parts), swap_x(far))
+    rest = add16(near, far)
+
+    chosen = add(res[:CAP], mine[:CAP])
+    mine = jnp.concatenate([chosen.astype(jnp.bfloat16), mine[CAP:]], axis=0)
+    theirs = swap_x(mine)
+    chosen = add(chosen, theirs[CAP:])
+    pair = add(mine, jnp.concatenate([theirs[CAP:], theirs[:CAP]], axis=0))
     normed = (
         pair * lax.rsqrt(jnp.mean(pair * pair, axis=1, keepdims=True) + 1e-06)
     ).astype(jnp.bfloat16)
     pieces = gather_z(normed)
     rows = expert(pieces, (w_gate, g_oth, w_up, u_oth, w_down, d_oth))
-    got = sum_z(cut(rows))
-    expert_rows = add(got[:CAP], swap_x(got[CAP:]))
-    rest = mine[NX * CAP :]
-    others = res[CAP:] + add(rest[:CAP], swap_x(rest[CAP:]))
+    both = [jnp.concatenate(p, axis=0) for p in zip(cut(rows), cut(rest))]
+    got, _ = sum_z(both)
+    expert_rows = add(got[:CAP], swap_x(got[CAP : NX * CAP]))
+    others = add(res[CAP:], got[NX * CAP :])
     done = jnp.concatenate(
-        [pair[:CAP] + share[:CAP, None] * expert_rows, others], axis=0
+        [chosen + share[:CAP, None] * expert_rows, others], axis=0
     ).astype(jnp.bfloat16)
     return jnp.dot(order16.T, done, preferred_element_type=jnp.float32).astype(jnp.bfloat16)
 

time: 199 us -> 175 us (0.88)
  waiting for transfers between devices: 123 us -> 92.9 us
  starting transfers between devices: 52.6 us -> 56.2 us
  Pallas kernels: 9.07 us -> 11.5 us
    ppermute x24, waiting for transfers between devices: 103 us -> 64 us  [shift(): return lax.ppermute(a, 'z', [(i, (i + by) % NZ) for i in range(NZ)])]
    ppermute x24, starting transfers between devices: 31.2 us -> 42.2 us  [shift(): return lax.ppermute(a, 'z', [(i, (i + by) % NZ) for i in range(NZ)])]
    ppermute x4 -> x3, starting transfers between devices: 9.5 us -> 2.3 us  [swap_x(): return lax.ppermute(a, 'xhi', [(0, 1), (1, 0)])]
    ppermute x4 -> x3, waiting for transfers between devices: 12 us -> 17.5 us  [swap_x(): return lax.ppermute(a, 'xhi', [(0, 1), (1, 0)])]
    all_to_all x1, waiting for transfers between devices: 8.11 us -> 11.5 us  [body(): lax.all_to_all(attended.reshape(2, CAP, CHIPS, 2 * HS), RING, split_axis=...]
    pallas_call x1, Pallas kernels: 4.85 us -> 7.22 us  [project(): pl.pallas_call(functools.partial(project_kernel, tile), out_shape=[jax.Sh...]
    unnamed x18 -> x20, local copies, waits for them, and re-layouts: 3.28 us -> 1.28 us
  transfers between devices with their start and end apart: 33 -> 32, of which waited for: 20 -> 20; matrix products, arithmetic and copies ran while one was open for 4% -> 6% of each run, Pallas kernels for 0% -> 0%
where the time goes in v3:
time: 175 us
  waiting for transfers between devices  92.9 us (53%)
  starting transfers between devices  56.2 us (32%)
  Pallas kernels  11.5 us (7%)
  other arithmetic  5.79 us (3%)
  local copies, waits for them, and re-layouts  4.19 us (2%)
  matrix products  4.01 us (2%)
    ppermute x24, waiting for transfers between devices, shift(): return lax.ppermute(a, 'z', [(i, (i + by) % NZ) for i in range(NZ)])  64 us
    ppermute x24, starting transfers between devices, shift(): return lax.ppermute(a, 'z', [(i, (i + by) % NZ) for i in range(NZ)])  42.2 us
    ppermute x3, waiting for transfers between devices, swap_x(): return lax.ppermute(a, 'xhi', [(0, 1), (1, 0)])  17.5 us
    all_to_all x1, waiting for transfers between devices, body(): lax.all_to_all(attended.reshape(2, CAP, CHIPS, 2 * HS), RING, split_axis=...  11.5 us
    all_to_all x1, starting transfers between devices, body(): lax.all_to_all(attended.reshape(2, CAP, CHIPS, 2 * HS), RING, split_axis=...  11 us
    pallas_call x1, Pallas kernels, project(): pl.pallas_call(functools.partial(project_kernel, tile), out_shape=[jax.Sh...  7.22 us
    pallas_call x1, Pallas kernels, expert(): pl.pallas_call(functools.partial(expert_kernel, tile), out_shape=jax.Shap...  4.23 us
  transfers between devices with their start and end apart: 32, of which 20 were waited for; matrix products, arithmetic and copies ran while one was open for 6% of the time, Pallas kernels for 0%

profile of v3, /device:TPU:24, one launch (start us, length us, event | category | flops | bytes accessed | tf_op | source)
XLA Modules:
  0.0 175.0 jit_solution(10945708508393902800)
XLA Ops:
  0.0 1.1 copy.16
  1.1 0.7 iota_compare_fusion.1
  1.8 1.7 fusion.3
  3.8 0.9 convolution_convert_fusion.2
  5.0 0.6 convert_reduce_fusion.1
  5.7 0.6 subtract_select_fusion
  6.6 0.7 copy.14
  7.3 11.0 %all-to-all-start = ((bf16[2,1,8,16,512]{4,2,0,1,3:T(8,128)(2,1)}), bf16[2,1,8,16,512]{4,2,0,1,3:T(8,128)(2,1)S(1)}, u32[]{:S(2)}, u32[]{:S(2)}) async-start(bf16[2,1,8,16,512]{4,2,0,1,3:T(8,128)(2,1)} %copy.14), calls=%async_computation | async-start | bytes 524288 | tf_op jit(solution)/shard_map/all_to_all | solution.py:223
  18.3 0.7 pad_add_fusion.place
  19.0 11.5 %all-to-all-done = bf16[2,1,8,16,512]{4,2,0,1,3:T(8,128)(2,1)S(1)} async-done(((bf16[2,1,8,16,512]{4,2,0,1,3:T(8,128)(2,1)}), bf16[2,1,8,16,512]{4,2,0,1,3:T(8,128)(2,1)S(1)}, u32[]{:S(2)}, u32[]{:S(2)}) %all-to-all-start) | async-done | bytes 262176 | tf_op jit(solution)/shard_map/all_to_all | solution.py:223
  30.5 0.7 copy.19
  31.2 7.2 %project.1 = (bf16[128,7168]{1,0:T(8,128)(2,1)}, bf16[64,7168]{1,0:T(8,128)(2,1)}, bf16[64,7168]{1,0:T(8,128)(2,1)}) custom-call(s32[3]{0:T(128)} %pad_add_fusion.place, bf16[2,16,8,512]{3,2,1,0:T(8,128)(2,1)} %bitcast.23, bf16[256,7168]{1,0:T(8,128)(2,1)} %w_own.1, bf16[256,7168]{1,0:T(8,128)(2,1)} %collective-permute-done.w_oth), custom_call_target="tpu_custom_call" | custom-call | tf_op jit(solution)/shard_map/project/pallas_call | solution.py:136
  38.4 1.2 fusion.25
  39.7 3.1 %collective-permute-start.4 = (bf16[16,3584]{1,0:T(8,128)(2,1)S(1)}, bf16[16,3584]{1,0:T(8,128)(2,1)S(1)}, u32[]{:S(2)}, u32[]{:S(2)}) collective-permute-start(bf16[16,3584]{1,0:T(8,128)(2,1)S(1)} %get-tuple-element.42), channel_id=1, source_target_pairs={{0,14},{2,0},{4,2},{6,4},{8,6},{10,8},{12,10},{14,12},{1,15},{3,1}... | collective-permute-start | bytes 344072 | tf_op jit(solution)/shard_map/ppermute | solution.py:50
  42.8 2.4 %collective-permute-done.4 = bf16[16,3584]{1,0:T(8,128)(2,1)S(1)} collective-permute-done((bf16[16,3584]{1,0:T(8,128)(2,1)S(1)}, bf16[16,3584]{1,0:T(8,128)(2,1)S(1)}, u32[]{:S(2)}, u32[]{:S(2)}) %collective-permute-start.4) | collective-permute-done | bytes 114720 | tf_op jit(solution)/shard_map/ppermute | solution.py:50
  45.1 3.6 %collective-permute-done.1 = bf16[16,3584]{1,0:T(8,128)(2,1)S(1)} collective-permute-done((bf16[16,3584]{1,0:T(8,128)(2,1)S(1)}, bf16[16,3584]{1,0:T(8,128)(2,1)S(1)}, u32[]{:S(2)}, u32[]{:S(2)}) %collective-permute-start.1) | collective-permute-done | bytes 114720 | tf_op jit(solution)/shard_map/ppermute | solution.py:50
  48.8 1.0 add_convert_fusion.14
  49.9 3.3 %collective-permute-start.5 = (bf16[16,7168]{1,0:T(8,128)(2,1)S(1)}, bf16[16,7168]{1,0:T(8,128)(2,1)S(1)}, u32[]{:S(2)}, u32[]{:S(2)}) collective-permute-start(bf16[16,7168]{1,0:T(8,128)(2,1)S(1)} %pad_maximum_fusion.2), channel_id=1, source_target_pairs={{0,14},{2,0},{4,2},{6,4},{8,6},{10,8},{12,10},{14,12},{1,15},{3,1}... | collective-permute-start | bytes 688136 | tf_op jit(solution)/shard_map/ppermute | solution.py:50
  53.8 3.3 %collective-permute-done.2 = bf16[16,7168]{1,0:T(8,128)(2,1)S(1)} collective-permute-done((bf16[16,7168]{1,0:T(8,128)(2,1)S(1)}, bf16[16,7168]{1,0:T(8,128)(2,1)S(1)}, u32[]{:S(2)}, u32[]{:S(2)}) %collective-permute-start.2) | collective-permute-done | bytes 229408 | tf_op jit(solution)/shard_map/ppermute | solution.py:50
  57.4 3.8 %collective-permute-start.6 = (bf16[16,7168]{1,0:T(8,128)(2,1)S(1)}, bf16[16,7168]{1,0:T(8,128)(2,1)S(1)}, u32[]{:S(2)}, u32[]{:S(2)}) collective-permute-start(bf16[16,7168]{1,0:T(8,128)(2,1)S(1)} %get-tuple-element.39), channel_id=1, source_target_pairs={{0,14},{2,0},{4,2},{6,4},{8,6},{10,8},{12,10},{14,12},{1,15},{3,1}... | collective-permute-start | bytes 688136 | tf_op jit(solution)/shard_map/ppermute | solution.py:50
  61.1 3.5 %collective-permute-done.6 = bf16[16,7168]{1,0:T(8,128)(2,1)S(1)} collective-permute-done((bf16[16,7168]{1,0:T(8,128)(2,1)S(1)}, bf16[16,7168]{1,0:T(8,128)(2,1)S(1)}, u32[]{:S(2)}, u32[]{:S(2)}) %collective-permute-start.6) | collective-permute-done | bytes 229408 | tf_op jit(solution)/shard_map/ppermute | solution.py:50
  64.7 3.7 %collective-permute-done.3 = bf16[16,7168]{1,0:T(8,128)(2,1)S(1)} collective-permute-done((bf16[16,7168]{1,0:T(8,128)(2,1)S(1)}, bf16[16,7168]{1,0:T(8,128)(2,1)S(1)}, u32[]{:S(2)}, u32[]{:S(2)}) %collective-permute-start.3) | collective-permute-done | bytes 229408 | tf_op jit(solution)/shard_map/ppermute | solution.py:50
  68.4 5.2 %collective-permute-done.7 = bf16[64,7168]{1,0:T(8,128)(2,1)S(1)} collective-permute-done((bf16[64,7168]{1,0:T(8,128)(2,1)}, bf16[64,7168]{1,0:T(8,128)(2,1)S(1)}, u32[]{:S(2)}, u32[]{:S(2)}) %collective-permute-start.7) | collective-permute-done | bytes 917536 | tf_op jit(solution)/shard_map/ppermute | solution.py:46
  73.7 3.2 %collective-permute-start.9 = (bf16[16,7168]{1,0:T(8,128)(2,1)S(1)}, bf16[16,7168]{1,0:T(8,128)(2,1)S(1)}, u32[]{:S(2)}, u32[]{:S(2)}) collective-permute-start(bf16[16,7168]{1,0:T(8,128)(2,1)S(1)} %get-tuple-element.38), channel_id=1, source_target_pairs={{0,14},{2,0},{4,2},{6,4},{8,6},{10,8},{12,10},{14,12},{1,15},{3,1}... | collective-permute-start | bytes 688136 | tf_op jit(solution)/shard_map/ppermute | solution.py:50
  77.2 3.8 %collective-permute-done.8 = bf16[16,7168]{1,0:T(8,128)(2,1)S(1)} collective-permute-done((bf16[16,7168]{1,0:T(8,128)(2,1)S(1)}, bf16[16,7168]{1,0:T(8,128)(2,1)S(1)}, u32[]{:S(2)}, u32[]{:S(2)}) %collective-permute-start.8) | collective-permute-done | bytes 229408 | tf_op jit(solution)/shard_map/ppermute | solution.py:50
  81.1 1.0 collective-permute-start.10
  82.1 6.8 %collective-permute-done.10 = bf16[16,7168]{1,0:T(8,128)(2,1)S(1)} collective-permute-done((bf16[16,7168]{1,0:T(8,128)(2,1)S(1)}, bf16[16,7168]{1,0:T(8,128)(2,1)S(1)}, u32[]{:S(2)}, u32[]{:S(2)}) %collective-permute-start.10) | collective-permute-done | bytes 229408 | tf_op jit(solution)/shard_map/ppermute | solution.py:46
  89.3 3.3 %collective-permute-start.11 = (bf16[16,7168]{1,0:T(8,128)(2,1)S(1)}, bf16[16,7168]{1,0:T(8,128)(2,1)S(1)}, u32[]{:S(2)}, u32[]{:S(2)}) collective-permute-start(bf16[16,7168]{1,0:T(8,128)(2,1)S(1)} %multiply_convert_fusion.refs_0_), channel_id=1, source_target_pairs={{0,14},{2,0},{4,2},{6,4},{8,6},{10,8},{12,10},{14,12},{1,15},{3,1}... | collective-permute-start | bytes 688136 | tf_op jit(solution)/shard_map/ppermute | solution.py:50
  92.6 4.9 %collective-permute-done.14.refs_8_ = bf16[16,7168]{1,0:T(8,128)(2,1)S(1)} collective-permute-done((bf16[16,7168]{1,0:T(8,128)(2,1)S(1)}, bf16[16,7168]{1,0:T(8,128)(2,1)S(1)}, u32[]{:S(2)}, u32[]{:S(2)}) %collective-permute-start.14) | collective-permute-done | bytes 229408 | tf_op jit(solution)/shard_map/ppermute | solution.py:50
  97.5 3.2 %collective-permute-start.12 = (bf16[16,7168]{1,0:T(8,128)(2,1)S(1)}, bf16[16,7168]{1,0:T(8,128)(2,1)S(1)}, u32[]{:S(2)}, u32[]{:S(2)}) collective-permute-start(bf16[16,7168]{1,0:T(8,128)(2,1)S(1)} %collective-permute-done.11.refs_1_), channel_id=1, source_target_pairs={{0,14},{2,0},{4,2},{6,4},{8,6},{10,8},{12,10},{14,12},{1,15},{3,1}... | collective-permute-start | bytes 688136 | tf_op jit(solution)/shard_map/ppermute | solution.py:50
  101.4 3.4 %collective-permute-done.15.refs_7_ = bf16[16,7168]{1,0:T(8,128)(2,1)S(1)} collective-permute-done((bf16[16,7168]{1,0:T(8,128)(2,1)S(1)}, bf16[16,7168]{1,0:T(8,128)(2,1)S(1)}, u32[]{:S(2)}, u32[]{:S(2)}) %collective-permute-start.15) | collective-permute-done | bytes 229408 | tf_op jit(solution)/shard_map/ppermute | solution.py:50
  104.8 3.2 %collective-permute-start.13 = (bf16[16,7168]{1,0:T(8,128)(2,1)S(1)}, bf16[16,7168]{1,0:T(8,128)(2,1)S(1)}, u32[]{:S(2)}, u32[]{:S(2)}) collective-permute-start(bf16[16,7168]{1,0:T(8,128)(2,1)S(1)} %collective-permute-done.12.refs_2_), channel_id=1, source_target_pairs={{0,14},{2,0},{4,2},{6,4},{8,6},{10,8},{12,10},{14,12},{1,15},{3,1}... | collective-permute-start | bytes 688136 | tf_op jit(solution)/shard_map/ppermute | solution.py:50
  108.2 3.9 %collective-permute-done.16.refs_6_ = bf16[16,7168]{1,0:T(8,128)(2,1)S(1)} collective-permute-done((bf16[16,7168]{1,0:T(8,128)(2,1)S(1)}, bf16[16,7168]{1,0:T(8,128)(2,1)S(1)}, u32[]{:S(2)}, u32[]{:S(2)}) %collective-permute-start.16) | collective-permute-done | bytes 229408 | tf_op jit(solution)/shard_map/ppermute | solution.py:50
  112.3 3.4 %collective-permute-start.18 = (bf16[16,3584]{1,0:T(8,128)(2,1)S(1)}, bf16[16,3584]{1,0:T(8,128)(2,1)S(1)}, u32[]{:S(2)}, u32[]{:S(2)}) collective-permute-start(bf16[16,3584]{1,0:T(8,128)(2,1)S(1)} %slice.196), channel_id=1, source_target_pairs={{0,14},{2,0},{4,2},{6,4},{8,6},{10,8},{12,10},{14,12},{1,15},{3,1}... | collective-permute-start | bytes 344072 | tf_op jit(solution)/shard_map/ppermute | solution.py:50
  115.7 2.5 %collective-permute-done.17.refs_4_ = bf16[16,3584]{1,0:T(8,128)(2,1)S(1)} collective-permute-done((bf16[16,3584]{1,0:T(8,128)(2,1)S(1)}, bf16[16,3584]{1,0:T(8,128)(2,1)S(1)}, u32[]{:S(2)}, u32[]{:S(2)}) %collective-permute-start.17) | collective-permute-done | bytes 114720 | tf_op jit(solution)/shard_map/ppermute | solution.py:50
  118.2 4.2 %expert.1 = bf16[128,7168]{1,0:T(8,128)(2,1)S(1)} custom-call(bf16[16,7168]{1,0:T(8,128)(2,1)S(1)} %multiply_convert_fusion.refs_0_, bf16[16,7168]{1,0:T(8,128)(2,1)S(1)} %collective-permute-done.11.refs_1_, bf16[16,7168]{1,0:T(8,128)(2,1)S(1)} %collective-permute-done.12.refs_2_, bf16[16,7168]{1,0:T(8,128)(2,1)S(1)} %collective-permute-done.13.refs_3_, ...), custom_call_target="tpu_custom_call" | custom-call | tf_op jit(solution)/shard_map/expert/pallas_call | solution.py:179
  123.0 3.5 %collective-permute-start.26 = (bf16[24,3584]{1,0:T(8,128)(2,1)S(1)}, bf16[24,3584]{1,0:T(8,128)(2,1)S(1)}, u32[]{:S(2)}, u32[]{:S(2)}) collective-permute-start(bf16[24,3584]{1,0:T(8,128)(2,1)S(1)} %get-tuple-element.58), channel_id=1, source_target_pairs={{0,14},{2,0},{4,2},{6,4},{8,6},{10,8},{12,10},{14,12},{1,15},{3,1}... | collective-permute-start | bytes 516104 | tf_op jit(solution)/shard_map/ppermute | solution.py:50
  126.5 4.7 %collective-permute-done.26 = bf16[24,3584]{1,0:T(8,128)(2,1)S(1)} collective-permute-done((bf16[24,3584]{1,0:T(8,128)(2,1)S(1)}, bf16[24,3584]{1,0:T(8,128)(2,1)S(1)}, u32[]{:S(2)}, u32[]{:S(2)}) %collective-permute-start.26) | collective-permute-done | bytes 172064 | tf_op jit(solution)/shard_map/ppermute | solution.py:50
  131.3 3.8 %collective-permute-start.27 = (bf16[24,7168]{1,0:T(8,128)(2,1)S(1)}, bf16[24,7168]{1,0:T(8,128)(2,1)S(1)}, u32[]{:S(2)}, u32[]{:S(2)}) collective-permute-start(bf16[24,7168]{1,0:T(8,128)(2,1)S(1)} %pad_maximum_fusion), channel_id=1, source_target_pairs={{0,14},{2,0},{4,2},{6,4},{8,6},{10,8},{12,10},{14,12},{1,15},{3,1}... | collective-permute-start | bytes 1032200 | tf_op jit(solution)/shard_map/ppermute | solution.py:50
  135.2 8.3 %collective-permute-done.27 = bf16[24,7168]{1,0:T(8,128)(2,1)S(1)} collective-permute-done((bf16[24,7168]{1,0:T(8,128)(2,1)S(1)}, bf16[24,7168]{1,0:T(8,128)(2,1)S(1)}, u32[]{:S(2)}, u32[]{:S(2)}) %collective-permute-start.27) | collective-permute-done | bytes 344096 | tf_op jit(solution)/shard_map/ppermute | solution.py:50
  143.5 3.8 %collective-permute-start.28 = (bf16[24,7168]{1,0:T(8,128)(2,1)S(1)}, bf16[24,7168]{1,0:T(8,128)(2,1)S(1)}, u32[]{:S(2)}, u32[]{:S(2)}) collective-permute-start(bf16[24,7168]{1,0:T(8,128)(2,1)S(1)} %add_convert_fusion.3), channel_id=1, source_target_pairs={{0,14},{2,0},{4,2},{6,4},{8,6},{10,8},{12,10},{14,12},{1,15},{3,1}... | collective-permute-start | bytes 1032200 | tf_op jit(solution)/shard_map/ppermute | solution.py:50
  147.5 7.4 %collective-permute-done.28 = bf16[24,7168]{1,0:T(8,128)(2,1)S(1)} collective-permute-done((bf16[24,7168]{1,0:T(8,128)(2,1)S(1)}, bf16[24,7168]{1,0:T(8,128)(2,1)S(1)}, u32[]{:S(2)}, u32[]{:S(2)}) %collective-permute-start.28) | collective-permute-done | bytes 344096 | tf_op jit(solution)/shard_map/ppermute | solution.py:50
  155.0 3.8 %collective-permute-start.29 = (bf16[24,7168]{1,0:T(8,128)(2,1)S(1)}, bf16[24,7168]{1,0:T(8,128)(2,1)S(1)}, u32[]{:S(2)}, u32[]{:S(2)}) collective-permute-start(bf16[24,7168]{1,0:T(8,128)(2,1)S(1)} %add_convert_fusion.2), channel_id=1, source_target_pairs={{0,14},{2,0},{4,2},{6,4},{8,6},{10,8},{12,10},{14,12},{1,15},{3,1}... | collective-permute-start | bytes 1032200 | tf_op jit(solution)/shard_map/ppermute | solution.py:50
  158.9 4.6 %collective-permute-done.29 = bf16[24,7168]{1,0:T(8,128)(2,1)S(1)} collective-permute-done((bf16[24,7168]{1,0:T(8,128)(2,1)S(1)}, bf16[24,7168]{1,0:T(8,128)(2,1)S(1)}, u32[]{:S(2)}, u32[]{:S(2)}) %collective-permute-start.29) | collective-permute-done | bytes 344096 | tf_op jit(solution)/shard_map/ppermute | solution.py:50
  163.5 3.9 %collective-permute-done.25 = bf16[24,7168]{1,0:T(8,128)(2,1)S(1)} collective-permute-done((bf16[24,7168]{1,0:T(8,128)(2,1)S(1)}, bf16[24,7168]{1,0:T(8,128)(2,1)S(1)}, u32[]{:S(2)}, u32[]{:S(2)}) %collective-permute-start.25) | collective-permute-done | bytes 344096 | tf_op jit(solution)/shard_map/ppermute | solution.py:50
  167.5 0.8 collective-permute-start.30
  168.4 5.5 %collective-permute-done.30 = bf16[8,7168]{1,0:T(8,128)(2,1)S(1)} collective-permute-done((bf16[8,7168]{1,0:T(8,128)(2,1)S(1)}, bf16[8,7168]{1,0:T(8,128)(2,1)S(1)}, u32[]{:S(2)}, u32[]{:S(2)}) %collective-permute-start.30) | collective-permute-done | bytes 114720 | tf_op jit(solution)/shard_map/ppermute | solution.py:46
  174.0 1.0 convolution_convert_fusion.1
  (86 shorter events, 5.2 us)
Async XLA Ops:
  0.0 3.8 %copy-start = (bf16[16,128,256]{2,1,0:T(8,128)(2,1)S(1)}, bf16[16,128,256]{2,1,0:T(8,128)(2,1)}, u32[]{:S(2)}) copy-start(bf16[16,128,256]{2,1,0:T(8,128)(2,1)} %param.13) | copy-start | bytes 3145732
  0.0 31.2 %collective-permute-start = (bf16[256,7168]{1,0:T(8,128)(2,1)}, bf16[256,7168]{1,0:T(8,128)(2,1)}, u32[]{:S(2)}, u32[]{:S(2)}) collective-permute-start(bf16[256,7168]{1,0:T(8,128)(2,1)} %w_own.1), channel_id=1, source_target_pairs={{0,1},{1,0},{2,3},{3,2},{4,5},{5,4},{6,7},{7,6},{8,9},{9,8},{10,11... | collective-permute-start | bytes 11010056 | tf_op jit(solution)/shard_map/ppermute | solution.py:42
  1.8 3.1 %copy-start.7 = (f32[16,3]{0,1:T(4,128)S(1)}, f32[16,3]{0,1:T(4,128)}, u32[]{:S(2)}) copy-start(f32[16,3]{0,1:T(4,128)} %param.18) | copy-start | bytes 580
  1.8 3.1 %copy-start.8 = (s32[16,3]{0,1:T(4,128)S(1)}, s32[16,3]{0,1:T(4,128)}, u32[]{:S(2)}) copy-start(s32[16,3]{0,1:T(4,128)} %param.17) | copy-start | bytes 580
  7.3 23.2 %all-to-all-start = ((bf16[2,1,8,16,512]{4,2,0,1,3:T(8,128)(2,1)}), bf16[2,1,8,16,512]{4,2,0,1,3:T(8,128)(2,1)S(1)}, u32[]{:S(2)}, u32[]{:S(2)}) async-start(bf16[2,1,8,16,512]{4,2,0,1,3:T(8,128)(2,1)} %copy.14), calls=%async_computation | async-start | bytes 524288 | tf_op jit(solution)/shard_map/all_to_all | solution.py:223
  31.2 45.8 %copy-start.6 = (bf16[16,7168]{1,0:T(8,128)(2,1)S(1)}, bf16[16,7168]{1,0:T(8,128)(2,1)}, u32[]{:S(2)}) copy-start(bf16[16,7168]{1,0:T(8,128)(2,1)} %param.16) | copy-start | bytes 688132
  38.4 18.8 %copy-start.4 = (bf16[128,7168]{1,0:T(8,128)(2,1)S(1)}, bf16[128,7168]{1,0:T(8,128)(2,1)}, u32[]{:S(2)}) copy-start(bf16[128,7168]{1,0:T(8,128)(2,1)} %get-tuple-element.18) | copy-start | bytes 5505028
  39.7 5.5 %collective-permute-start.4 = (bf16[16,3584]{1,0:T(8,128)(2,1)S(1)}, bf16[16,3584]{1,0:T(8,128)(2,1)S(1)}, u32[]{:S(2)}, u32[]{:S(2)}) collective-permute-start(bf16[16,3584]{1,0:T(8,128)(2,1)S(1)} %get-tuple-element.42), channel_id=1, source_target_pairs={{0,14},{2,0},{4,2},{6,4},{8,6},{10,8},{12,10},{14,12},{1,15},{3,1}... | collective-permute-start | bytes 344072 | tf_op jit(solution)/shard_map/ppermute | solution.py:50
  42.8 6.0 %collective-permute-start.1 = (bf16[16,3584]{1,0:T(8,128)(2,1)S(1)}, bf16[16,3584]{1,0:T(8,128)(2,1)S(1)}, u32[]{:S(2)}, u32[]{:S(2)}) collective-permute-start(bf16[16,3584]{1,0:T(8,128)(2,1)S(1)} %get-tuple-element.44), channel_id=1, source_target_pairs={{0,2},{2,4},{4,6},{6,8},{8,10},{10,12},{12,14},{14,0},{1,3},{3,5},... | collective-permute-start | bytes 344072 | tf_op jit(solution)/shard_map/ppermute | solution.py:50
  49.8 58.2 %copy-start.5 = (bf16[64,7168]{1,0:T(8,128)(2,1)S(1)}, bf16[64,7168]{1,0:T(8,128)(2,1)}, u32[]{:S(2)}) copy-start(bf16[64,7168]{1,0:T(8,128)(2,1)} %get-tuple-element.25) | copy-start | bytes 2752516
  49.8 7.3 %collective-permute-start.2 = (bf16[16,7168]{1,0:T(8,128)(2,1)S(1)}, bf16[16,7168]{1,0:T(8,128)(2,1)S(1)}, u32[]{:S(2)}, u32[]{:S(2)}) collective-permute-start(bf16[16,7168]{1,0:T(8,128)(2,1)S(1)} %pad_maximum_fusion.1), channel_id=1, source_target_pairs={{0,2},{2,4},{4,6},{6,8},{8,10},{10,12},{12,14},{14,0},{1,3},{3,5},... | collective-permute-start | bytes 688136 | tf_op jit(solution)/shard_map/ppermute | solution.py:50
  49.9 7.3 %collective-permute-start.5 = (bf16[16,7168]{1,0:T(8,128)(2,1)S(1)}, bf16[16,7168]{1,0:T(8,128)(2,1)S(1)}, u32[]{:S(2)}, u32[]{:S(2)}) collective-permute-start(bf16[16,7168]{1,0:T(8,128)(2,1)S(1)} %pad_maximum_fusion.2), channel_id=1, source_target_pairs={{0,14},{2,0},{4,2},{6,4},{8,6},{10,8},{12,10},{14,12},{1,15},{3,1}... | collective-permute-start | bytes 688136 | tf_op jit(solution)/shard_map/ppermute | solution.py:50
  53.2 20.3 %collective-permute-start.7 = (bf16[64,7168]{1,0:T(8,128)(2,1)}, bf16[64,7168]{1,0:T(8,128)(2,1)S(1)}, u32[]{:S(2)}, u32[]{:S(2)}) collective-permute-start(bf16[64,7168]{1,0:T(8,128)(2,1)} %get-tuple-element.19), channel_id=1, source_target_pairs={{0,16},{16,0},{1,17},{17,1},{2,18},{18,2},{3,19},{19,3},{4,20},{20... | collective-permute-start | bytes 2752520 | tf_op jit(solution)/shard_map/ppermute | solution.py:46
  57.3 44.0 %copy-start.3 = (bf16[160,7168]{1,0:T(8,128)(2,1)S(1)}, bf16[160,7168]{1,0:T(8,128)(2,1)}, u32[]{:S(2)}) copy-start(bf16[160,7168]{1,0:T(8,128)(2,1)} %refs_13_) | copy-start | bytes 6881284
  57.4 7.3 %collective-permute-start.6 = (bf16[16,7168]{1,0:T(8,128)(2,1)S(1)}, bf16[16,7168]{1,0:T(8,128)(2,1)S(1)}, u32[]{:S(2)}, u32[]{:S(2)}) collective-permute-start(bf16[16,7168]{1,0:T(8,128)(2,1)S(1)} %get-tuple-element.39), channel_id=1, source_target_pairs={{0,14},{2,0},{4,2},{6,4},{8,6},{10,8},{12,10},{14,12},{1,15},{3,1}... | collective-permute-start | bytes 688136 | tf_op jit(solution)/shard_map/ppermute | solution.py:50
  61.1 7.2 %collective-permute-start.3 = (bf16[16,7168]{1,0:T(8,128)(2,1)S(1)}, bf16[16,7168]{1,0:T(8,128)(2,1)S(1)}, u32[]{:S(2)}, u32[]{:S(2)}) collective-permute-start(bf16[16,7168]{1,0:T(8,128)(2,1)S(1)} %get-tuple-element.40), channel_id=1, source_target_pairs={{0,2},{2,4},{4,6},{6,8},{8,10},{10,12},{12,14},{14,0},{1,3},{3,5},... | collective-permute-start | bytes 688136 | tf_op jit(solution)/shard_map/ppermute | solution.py:50
  73.5 27.2 %copy-start.2 = (bf16[160,7168]{1,0:T(8,128)(2,1)S(1)}, bf16[160,7168]{1,0:T(8,128)(2,1)}, u32[]{:S(2)}) copy-start(bf16[160,7168]{1,0:T(8,128)(2,1)} %refs_11_) | copy-start | bytes 6881284
  73.6 7.3 %collective-permute-start.8 = (bf16[16,7168]{1,0:T(8,128)(2,1)S(1)}, bf16[16,7168]{1,0:T(8,128)(2,1)S(1)}, u32[]{:S(2)}, u32[]{:S(2)}) collective-permute-start(bf16[16,7168]{1,0:T(8,128)(2,1)S(1)} %get-tuple-element.37), channel_id=1, source_target_pairs={{0,2},{2,4},{4,6},{6,8},{8,10},{10,12},{12,14},{14,0},{1,3},{3,5},... | collective-permute-start | bytes 688136 | tf_op jit(solution)/shard_map/ppermute | solution.py:50
  73.7 7.2 %collective-permute-start.9 = (bf16[16,7168]{1,0:T(8,128)(2,1)S(1)}, bf16[16,7168]{1,0:T(8,128)(2,1)S(1)}, u32[]{:S(2)}, u32[]{:S(2)}) collective-permute-start(bf16[16,7168]{1,0:T(8,128)(2,1)S(1)} %get-tuple-element.38), channel_id=1, source_target_pairs={{0,14},{2,0},{4,2},{6,4},{8,6},{10,8},{12,10},{14,12},{1,15},{3,1}... | collective-permute-start | bytes 688136 | tf_op jit(solution)/shard_map/ppermute | solution.py:50
  77.2 23.6 %copy-start.1 = (bf16[160,7168]{1,0:T(8,128)(2,1)S(1)}, bf16[160,7168]{1,0:T(8,128)(2,1)}, u32[]{:S(2)}) copy-start(bf16[160,7168]{1,0:T(8,128)(2,1)} %refs_9_) | copy-start | bytes 6881284
  81.1 7.8 %collective-permute-start.10 = (bf16[16,7168]{1,0:T(8,128)(2,1)S(1)}, bf16[16,7168]{1,0:T(8,128)(2,1)S(1)}, u32[]{:S(2)}, u32[]{:S(2)}) collective-permute-start(bf16[16,7168]{1,0:T(8,128)(2,1)S(1)} %pad_maximum_fusion.3), channel_id=1, source_target_pairs={{0,16},{16,0},{1,17},{17,1},{2,18},{18,2},{3,19},{19,3},{4,20},{20... | collective-permute-start | bytes 688136 | tf_op jit(solution)/shard_map/ppermute | solution.py:46
  89.2 8.3 %collective-permute-start.14 = (bf16[16,7168]{1,0:T(8,128)(2,1)S(1)}, bf16[16,7168]{1,0:T(8,128)(2,1)S(1)}, u32[]{:S(2)}, u32[]{:S(2)}) collective-permute-start(bf16[16,7168]{1,0:T(8,128)(2,1)S(1)} %multiply_convert_fusion.refs_0_), channel_id=1, source_target_pairs={{0,2},{2,4},{4,6},{6,8},{8,10},{10,12},{12,14},{14,0},{1,3},{3,5},... | collective-permute-start | bytes 688136 | tf_op jit(solution)/shard_map/ppermute | solution.py:50
  89.3 8.2 %collective-permute-start.11 = (bf16[16,7168]{1,0:T(8,128)(2,1)S(1)}, bf16[16,7168]{1,0:T(8,128)(2,1)S(1)}, u32[]{:S(2)}, u32[]{:S(2)}) collective-permute-start(bf16[16,7168]{1,0:T(8,128)(2,1)S(1)} %multiply_convert_fusion.refs_0_), channel_id=1, source_target_pairs={{0,14},{2,0},{4,2},{6,4},{8,6},{10,8},{12,10},{14,12},{1,15},{3,1}... | collective-permute-start | bytes 688136 | tf_op jit(solution)/shard_map/ppermute | solution.py:50
  97.5 7.2 %collective-permute-start.15 = (bf16[16,7168]{1,0:T(8,128)(2,1)S(1)}, bf16[16,7168]{1,0:T(8,128)(2,1)S(1)}, u32[]{:S(2)}, u32[]{:S(2)}) collective-permute-start(bf16[16,7168]{1,0:T(8,128)(2,1)S(1)} %collective-permute-done.14.refs_8_), channel_id=1, source_target_pairs={{0,2},{2,4},{4,6},{6,8},{8,10},{10,12},{12,14},{14,0},{1,3},{3,5},... | collective-permute-start | bytes 688136 | tf_op jit(solution)/shard_map/ppermute | solution.py:50
  97.5 7.2 %collective-permute-start.12 = (bf16[16,7168]{1,0:T(8,128)(2,1)S(1)}, bf16[16,7168]{1,0:T(8,128)(2,1)S(1)}, u32[]{:S(2)}, u32[]{:S(2)}) collective-permute-start(bf16[16,7168]{1,0:T(8,128)(2,1)S(1)} %collective-permute-done.11.refs_1_), channel_id=1, source_target_pairs={{0,14},{2,0},{4,2},{6,4},{8,6},{10,8},{12,10},{14,12},{1,15},{3,1}... | collective-permute-start | bytes 688136 | tf_op jit(solution)/shard_map/ppermute | solution.py:50
  100.8 17.5 %collective-permute-start.19 = (bf16[160,7168]{1,0:T(8,128)(2,1)S(1)}, bf16[160,7168]{1,0:T(8,128)(2,1)S(1)}, u32[]{:S(2)}, u32[]{:S(2)}) collective-permute-start(bf16[160,7168]{1,0:T(8,128)(2,1)S(1)} %copy-done.1), channel_id=1, source_target_pairs={{0,1},{1,0},{2,3},{3,2},{4,5},{5,4},{6,7},{7,6},{8,9},{9,8},{10,11... | collective-permute-start | bytes 6881288 | tf_op jit(solution)/shard_map/ppermute | solution.py:42
  100.8 17.5 %collective-permute-start.20 = (bf16[160,7168]{1,0:T(8,128)(2,1)S(1)}, bf16[160,7168]{1,0:T(8,128)(2,1)S(1)}, u32[]{:S(2)}, u32[]{:S(2)}) collective-permute-start(bf16[160,7168]{1,0:T(8,128)(2,1)S(1)} %copy-done.2), channel_id=1, source_target_pairs={{0,1},{1,0},{2,3},{3,2},{4,5},{5,4},{6,7},{7,6},{8,9},{9,8},{10,11... | collective-permute-start | bytes 6881288 | tf_op jit(solution)/shard_map/ppermute | solution.py:42
  101.3 17.0 %collective-permute-start.21 = (bf16[160,7168]{1,0:T(8,128)(2,1)S(1)}, bf16[160,7168]{1,0:T(8,128)(2,1)S(1)}, u32[]{:S(2)}, u32[]{:S(2)}) collective-permute-start(bf16[160,7168]{1,0:T(8,128)(2,1)S(1)} %copy-done.3), channel_id=1, source_target_pairs={{0,1},{1,0},{2,3},{3,2},{4,5},{5,4},{6,7},{7,6},{8,9},{9,8},{10,11... | collective-permute-start | bytes 6881288 | tf_op jit(solution)/shard_map/ppermute | solution.py:42
  104.8 7.4 %collective-permute-start.16 = (bf16[16,7168]{1,0:T(8,128)(2,1)S(1)}, bf16[16,7168]{1,0:T(8,128)(2,1)S(1)}, u32[]{:S(2)}, u32[]{:S(2)}) collective-permute-start(bf16[16,7168]{1,0:T(8,128)(2,1)S(1)} %collective-permute-done.15.refs_7_), channel_id=1, source_target_pairs={{0,2},{2,4},{4,6},{6,8},{8,10},{10,12},{12,14},{14,0},{1,3},{3,5},... | collective-permute-start | bytes 688136 | tf_op jit(solution)/shard_map/ppermute | solution.py:50
  104.8 7.5 %collective-permute-start.13 = (bf16[16,7168]{1,0:T(8,128)(2,1)S(1)}, bf16[16,7168]{1,0:T(8,128)(2,1)S(1)}, u32[]{:S(2)}, u32[]{:S(2)}) collective-permute-start(bf16[16,7168]{1,0:T(8,128)(2,1)S(1)} %collective-permute-done.12.refs_2_), channel_id=1, source_target_pairs={{0,14},{2,0},{4,2},{6,4},{8,6},{10,8},{12,10},{14,12},{1,15},{3,1}... | collective-permute-start | bytes 688136 | tf_op jit(solution)/shard_map/ppermute | solution.py:50
  112.1 6.1 %collective-permute-start.17 = (bf16[16,3584]{1,0:T(8,128)(2,1)S(1)}, bf16[16,3584]{1,0:T(8,128)(2,1)S(1)}, u32[]{:S(2)}, u32[]{:S(2)}) collective-permute-start(bf16[16,3584]{1,0:T(8,128)(2,1)S(1)} %slice.195), channel_id=1, source_target_pairs={{0,2},{2,4},{4,6},{6,8},{8,10},{10,12},{12,14},{14,0},{1,3},{3,5},... | collective-permute-start | bytes 344072 | tf_op jit(solution)/shard_map/ppermute | solution.py:50
  112.3 6.0 %collective-permute-start.18 = (bf16[16,3584]{1,0:T(8,128)(2,1)S(1)}, bf16[16,3584]{1,0:T(8,128)(2,1)S(1)}, u32[]{:S(2)}, u32[]{:S(2)}) collective-permute-start(bf16[16,3584]{1,0:T(8,128)(2,1)S(1)} %slice.196), channel_id=1, source_target_pairs={{0,14},{2,0},{4,2},{6,4},{8,6},{10,8},{12,10},{14,12},{1,15},{3,1}... | collective-permute-start | bytes 344072 | tf_op jit(solution)/shard_map/ppermute | solution.py:50
  122.6 12.4 %collective-permute-start.22 = (bf16[24,3584]{1,0:T(8,128)(2,1)S(1)}, bf16[24,3584]{1,0:T(8,128)(2,1)S(1)}, u32[]{:S(2)}, u32[]{:S(2)}) collective-permute-start(bf16[24,3584]{1,0:T(8,128)(2,1)S(1)} %get-tuple-element.57), channel_id=1, source_target_pairs={{0,2},{2,4},{4,6},{6,8},{8,10},{10,12},{12,14},{14,0},{1,3},{3,5},... | collective-permute-start | bytes 516104 | tf_op jit(solution)/shard_map/ppermute | solution.py:50
  123.0 8.2 %collective-permute-start.26 = (bf16[24,3584]{1,0:T(8,128)(2,1)S(1)}, bf16[24,3584]{1,0:T(8,128)(2,1)S(1)}, u32[]{:S(2)}, u32[]{:S(2)}) collective-permute-start(bf16[24,3584]{1,0:T(8,128)(2,1)S(1)} %get-tuple-element.58), channel_id=1, source_target_pairs={{0,14},{2,0},{4,2},{6,4},{8,6},{10,8},{12,10},{14,12},{1,15},{3,1}... | collective-permute-start | bytes 516104 | tf_op jit(solution)/shard_map/ppermute | solution.py:50
  131.3 12.2 %collective-permute-start.27 = (bf16[24,7168]{1,0:T(8,128)(2,1)S(1)}, bf16[24,7168]{1,0:T(8,128)(2,1)S(1)}, u32[]{:S(2)}, u32[]{:S(2)}) collective-permute-start(bf16[24,7168]{1,0:T(8,128)(2,1)S(1)} %pad_maximum_fusion), channel_id=1, source_target_pairs={{0,14},{2,0},{4,2},{6,4},{8,6},{10,8},{12,10},{14,12},{1,15},{3,1}... | collective-permute-start | bytes 1032200 | tf_op jit(solution)/shard_map/ppermute | solution.py:50
  135.1 12.2 %collective-permute-start.23 = (bf16[24,7168]{1,0:T(8,128)(2,1)S(1)}, bf16[24,7168]{1,0:T(8,128)(2,1)S(1)}, u32[]{:S(2)}, u32[]{:S(2)}) collective-permute-start(bf16[24,7168]{1,0:T(8,128)(2,1)S(1)} %fusion.7), channel_id=1, source_target_pairs={{0,2},{2,4},{4,6},{6,8},{8,10},{10,12},{12,14},{14,0},{1,3},{3,5},... | collective-permute-start | bytes 1032200 | tf_op jit(solution)/shard_map/ppermute | solution.py:50
  143.5 11.4 %collective-permute-start.28 = (bf16[24,7168]{1,0:T(8,128)(2,1)S(1)}, bf16[24,7168]{1,0:T(8,128)(2,1)S(1)}, u32[]{:S(2)}, u32[]{:S(2)}) collective-permute-start(bf16[24,7168]{1,0:T(8,128)(2,1)S(1)} %add_convert_fusion.3), channel_id=1, source_target_pairs={{0,14},{2,0},{4,2},{6,4},{8,6},{10,8},{12,10},{14,12},{1,15},{3,1}... | collective-permute-start | bytes 1032200 | tf_op jit(solution)/shard_map/ppermute | solution.py:50
  147.4 11.4 %collective-permute-start.24 = (bf16[24,7168]{1,0:T(8,128)(2,1)S(1)}, bf16[24,7168]{1,0:T(8,128)(2,1)S(1)}, u32[]{:S(2)}, u32[]{:S(2)}) collective-permute-start(bf16[24,7168]{1,0:T(8,128)(2,1)S(1)} %add_convert_fusion.5), channel_id=1, source_target_pairs={{0,2},{2,4},{4,6},{6,8},{8,10},{10,12},{12,14},{14,0},{1,3},{3,5},... | collective-permute-start | bytes 1032200 | tf_op jit(solution)/shard_map/ppermute | solution.py:50
  155.0 8.5 %collective-permute-start.29 = (bf16[24,7168]{1,0:T(8,128)(2,1)S(1)}, bf16[24,7168]{1,0:T(8,128)(2,1)S(1)}, u32[]{:S(2)}, u32[]{:S(2)}) collective-permute-start(bf16[24,7168]{1,0:T(8,128)(2,1)S(1)} %add_convert_fusion.2), channel_id=1, source_target_pairs={{0,14},{2,0},{4,2},{6,4},{8,6},{10,8},{12,10},{14,12},{1,15},{3,1}... | collective-permute-start | bytes 1032200 | tf_op jit(solution)/shard_map/ppermute | solution.py:50
  158.9 8.5 %collective-permute-start.25 = (bf16[24,7168]{1,0:T(8,128)(2,1)S(1)}, bf16[24,7168]{1,0:T(8,128)(2,1)S(1)}, u32[]{:S(2)}, u32[]{:S(2)}) collective-permute-start(bf16[24,7168]{1,0:T(8,128)(2,1)S(1)} %add_convert_fusion.4), channel_id=1, source_target_pairs={{0,2},{2,4},{4,6},{6,8},{8,10},{10,12},{12,14},{14,0},{1,3},{3,5},... | collective-permute-start | bytes 1032200 | tf_op jit(solution)/shard_map/ppermute | solution.py:50
  167.5 6.4 %collective-permute-start.30 = (bf16[8,7168]{1,0:T(8,128)(2,1)S(1)}, bf16[8,7168]{1,0:T(8,128)(2,1)S(1)}, u32[]{:S(2)}, u32[]{:S(2)}) collective-permute-start(bf16[8,7168]{1,0:T(8,128)(2,1)S(1)} %slice.220), channel_id=1, source_target_pairs={{0,16},{16,0},{1,17},{17,1},{2,18},{18,2},{3,19},{19,3},{4,20},{20... | collective-permute-start | bytes 344072 | tf_op jit(solution)/shard_map/ppermute | solution.py:46

commit v4 on v3

--- a/solution.py
+++ b/solution.py
@@ -61,18 +61,20 @@
     return add(*terms).astype(jnp.bfloat16)
 
 
-def sum_z(part, beside=None):
+def sum_z(part, early=None, late=None):
     half = part[0].shape[-1] // 2
     up, down = shift(part[4][:, :half], 1), shift(part[4][:, half:], -1)
     up = shift(add_part(part[3], up, 0), 1)
     down = shift(add_part(part[5], down, half), -1)
+    if early is not None:
+        up, down, early = lax.optimization_barrier((up, down, early))
     up = shift(add16(part[2], up), 1)
     down = shift(add16(part[6], down), -1)
-    if beside is not None:
-        up, down, beside = lax.optimization_barrier((up, down, beside))
     up = shift(add16(part[1], up), 1)
     down = shift(add16(part[7], down), -1)
-    return add16(part[0], up, down), beside
+    if late is not None:
+        up, down, late = lax.optimization_barrier((up, down, late))
+    return add16(part[0], up, down), early, late
 
 
 def add_part(whole, piece, at):
@@ -113,7 +115,8 @@
         for rx, rz in order:
             x = lax.rem(place[0] + rx, NX)
             z = lax.rem(place[1] + rz, NZ)
-            blocks.append(a[kind, x * NZ + z].astype(jnp.float32))
+            block = a[x * NZ + z].astype(jnp.float32)
+            blocks.append(block[kind * CAP : (kind + 1) * CAP])
     rows = jnp.concatenate(blocks, axis=0)
     first = place[2] == 0
     own = jnp.where(first, rows[:, :depth], rows[:, depth:]).astype(jnp.bfloat16)
@@ -130,7 +133,7 @@
 
 
 def project(place, attended, w_own, w_oth, tile=1024):
-    rows, depth = CHIPS * attended.shape[2], w_own.shape[0]
+    rows, depth = CHIPS * CAP, w_own.shape[0]
     whole = pl.BlockSpec(memory_space=pltpu.VMEM)
     anywhere = pl.BlockSpec(memory_space=pl.ANY)
     return pl.pallas_call(
@@ -144,7 +147,10 @@
             pltpu.VMEM((2, D // tile, depth, tile), jnp.bfloat16),
             pltpu.SemaphoreType.DMA((2, D // tile)),
         ],
-        compiler_params=pltpu.CompilerParams(vmem_limit_bytes=58 * 1024 * 1024),
+        compiler_params=pltpu.CompilerParams(vmem_limit_bytes=50 * 1024 * 1024),
+        cost_estimate=pl.CostEstimate(
+            flops=8 * rows * depth * D, bytes_accessed=6 * depth * D, transcendentals=0
+        ),
         name="project",
     )(place, attended, w_own, w_oth)
 
@@ -221,15 +227,16 @@
     attended = attend(queries, key_cache, value_cache, lengths)
     attended = jnp.dot(order16, attended, preferred_element_type=jnp.float32).astype(jnp.bfloat16)
     by_heads = lax.all_to_all(
-        attended.reshape(2, CAP, CHIPS, 2 * HS), RING, split_axis=2, concat_axis=1
+        attended.reshape(ROWS, CHIPS, 2 * HS), RING, split_axis=1, concat_axis=0
     )
     by_heads, o_oth, w_gate, w_up, w_down = lax.optimization_barrier(
         (by_heads, o_oth, w_gate, w_up, w_down)
     )
     g_oth, u_oth, d_oth = swap_cores(w_gate), swap_cores(w_up), swap_cores(w_down)
     parts, near, far = project(place, by_heads, out_proj, o_oth)
-    mine, far = sum_z(cut(parts), swap_x(far))
-    rest = add16(near, far)
+    half = far.shape[0] // 2
+    mine, first, second = sum_z(cut(parts), swap_x(far[:half]), swap_x(far[half:]))
+    rest = add16(near, jnp.concatenate([first, second], axis=0))
 
     chosen = add(res[:CAP], mine[:CAP])
     mine = jnp.concatenate([chosen.astype(jnp.bfloat16), mine[CAP:]], axis=0)
@@ -242,7 +249,7 @@
     pieces = gather_z(normed)
     rows = expert(pieces, (w_gate, g_oth, w_up, u_oth, w_down, d_oth))
     both = [jnp.concatenate(p, axis=0) for p in zip(cut(rows), cut(rest))]
-    got, _ = sum_z(both)
+    got, _, _ = sum_z(both)
     expert_rows = add(got[:CAP], swap_x(got[CAP : NX * CAP]))
     others = add(res[CAP:], got[NX * CAP :])
     done = jnp.concatenate(

time: 175 us -> 171 us (0.977)
  Pallas kernels: 11.5 us -> 9.23 us
    ppermute x24, waiting for transfers between devices: 64 us -> 68.7 us  [shift(): return lax.ppermute(a, 'z', [(i, (i + by) % NZ) for i in range(NZ)])]
    ppermute x3 -> x4, waiting for transfers between devices: 17.5 us -> 13.7 us  [swap_x(): return lax.ppermute(a, 'xhi', [(0, 1), (1, 0)])]
    pallas_call x1, Pallas kernels: 7.22 us -> 4.97 us  [project(): pl.pallas_call(functools.partial(project_kernel, tile), out_shape=[jax.Sh...]
  transfers between devices with their start and end apart: 32 -> 33, of which waited for: 20 -> 18; matrix products, arithmetic and copies ran while one was open for 6% -> 5% of each run, Pallas kernels for 0% -> 0%
where the time goes in v4:
time: 171 us; the launch traced here: 170 us
  waiting for transfers between devices  94.4 us (55%)
  starting transfers between devices  55.4 us (32%)
  Pallas kernels  9.23 us (5%)
  other arithmetic  4.3 us (3%)
  matrix products  4.01 us (2%)
  local copies, waits for them, and re-layouts  2.53 us (1%)
    ppermute x24, waiting for transfers between devices, shift(): return lax.ppermute(a, 'z', [(i, (i + by) % NZ) for i in range(NZ)])  68.7 us
    ppermute x24, starting transfers between devices, shift(): return lax.ppermute(a, 'z', [(i, (i + by) % NZ) for i in range(NZ)])  42.8 us
    ppermute x4, waiting for transfers between devices, swap_x(): return lax.ppermute(a, 'xhi', [(0, 1), (1, 0)])  13.7 us
    all_to_all x1, waiting for transfers between devices, body(): lax.all_to_all(attended.reshape(ROWS, CHIPS, 2 * HS), RING, split_axis=1,...  12.1 us
    all_to_all x1, starting transfers between devices, body(): lax.all_to_all(attended.reshape(ROWS, CHIPS, 2 * HS), RING, split_axis=1,...  11 us
    pallas_call x1, Pallas kernels, project(): pl.pallas_call(functools.partial(project_kernel, tile), out_shape=[jax.Sh...  4.97 us
    pallas_call x1, Pallas kernels, expert(): pl.pallas_call(functools.partial(expert_kernel, tile), out_shape=jax.Shap...  4.26 us
  transfers between devices with their start and end apart: 33, of which 18 were waited for; matrix products, arithmetic and copies ran while one was open for 5% of the time, Pallas kernels for 0%

profile of v4, /device:TPU:24, one launch (start us, length us, event | category | flops | bytes accessed | tf_op | source)
XLA Modules:
  0.0 170.4 jit_solution(17094862388068843676)
XLA Ops:
  0.0 1.1 copy.15
  1.1 0.7 iota_compare_fusion.1
  1.8 1.7 %fusion.3 = f32[16,32,128]{2,1,0:T(8,128)S(1)} fusion(bf16[16,32,256]{2,1,0:T(8,128)(2,1)S(1)} %bitcast.27, bf16[16,128,256]{2,1,0:T(8,128)(2,1)} %param.12, pred[16,128]{1,0:T(8,128)(4,1)S(1)} %iota_compare_fusion.1), kind=kOutput, calls=%fused_computation.8 | convolution fusion | flops 33685504 | bytes 1574912 | tf_op jit(solution)/shard_map/rhd,rld->rhl/dot_general | solution.py:29
  3.5 0.2 fusion.29
  3.8 0.9 convolution_convert_fusion.2
  5.0 0.6 convert_reduce_fusion.1
  5.7 0.6 subtract_select_fusion
  6.4 0.2 convolution_convert_fusion
  6.7 0.8 copy.14
  7.5 11.0 %all-to-all-start = ((bf16[1,16,16,512]{3,1,0,2:T(8,128)(2,1)}), bf16[1,16,16,512]{3,1,0,2:T(8,128)(2,1)S(1)}, u32[]{:S(2)}, u32[]{:S(2)}) async-start(bf16[1,16,16,512]{3,1,0,2:T(8,128)(2,1)} %copy.14), calls=%async_computation | async-start | bytes 524288 | tf_op jit(solution)/shard_map/all_to_all | solution.py:229
  18.6 12.1 %all-to-all-done = bf16[1,16,16,512]{3,1,0,2:T(8,128)(2,1)S(1)} async-done(((bf16[1,16,16,512]{3,1,0,2:T(8,128)(2,1)}), bf16[1,16,16,512]{3,1,0,2:T(8,128)(2,1)S(1)}, u32[]{:S(2)}, u32[]{:S(2)}) %all-to-all-start) | async-done | bytes 262176 | tf_op jit(solution)/shard_map/all_to_all | solution.py:229
  30.7 5.0 %project.1 = (bf16[128,7168]{1,0:T(8,128)(2,1)S(1)}, bf16[64,7168]{1,0:T(8,128)(2,1)S(1)}, bf16[64,7168]{1,0:T(8,128)(2,1)S(1)}) custom-call(s32[3]{0:T(128)S(1)} %pad_add_fusion.place, bf16[16,16,512]{2,1,0:T(8,128)(2,1)S(1)} %bitcast.23, bf16[256,7168]{1,0:T(8,128)(2,1)} %w_own.1, bf16[256,7168]{1,0:T(8,128)(2,1)} %collective-permute-done.w_oth), custom_call_target="tpu_custom_call" | custom-call | flops 1879048192 | bytes 11010048 | tf_op jit(solution)/shard_map/project/pallas_call | solution.py:139
  35.7 3.1 %collective-permute-start.3 = (bf16[16,3584]{1,0:T(8,128)(2,1)S(1)}, bf16[16,3584]{1,0:T(8,128)(2,1)S(1)}, u32[]{:S(2)}, u32[]{:S(2)}) collective-permute-start(bf16[16,3584]{1,0:T(8,128)(2,1)S(1)} %get-tuple-element.46), channel_id=1, source_target_pairs={{0,14},{2,0},{4,2},{6,4},{8,6},{10,8},{12,10},{14,12},{1,15},{3,1}... | collective-permute-start | bytes 344072 | tf_op jit(solution)/shard_map/ppermute | solution.py:50
  38.9 0.7 collective-permute-start.5
  39.5 1.6 collective-permute-done.3
  41.2 3.6 %collective-permute-done.1 = bf16[16,3584]{1,0:T(8,128)(2,1)S(1)} collective-permute-done((bf16[16,3584]{1,0:T(8,128)(2,1)S(1)}, bf16[16,3584]{1,0:T(8,128)(2,1)S(1)}, u32[]{:S(2)}, u32[]{:S(2)}) %collective-permute-start.1) | collective-permute-done | bytes 114720 | tf_op jit(solution)/shard_map/ppermute | solution.py:50
  45.0 3.3 %collective-permute-start.4 = (bf16[16,7168]{1,0:T(8,128)(2,1)S(1)}, bf16[16,7168]{1,0:T(8,128)(2,1)S(1)}, u32[]{:S(2)}, u32[]{:S(2)}) collective-permute-start(bf16[16,7168]{1,0:T(8,128)(2,1)S(1)} %pad_maximum_fusion.2), channel_id=1, source_target_pairs={{0,14},{2,0},{4,2},{6,4},{8,6},{10,8},{12,10},{14,12},{1,15},{3,1}... | collective-permute-start | bytes 688136 | tf_op jit(solution)/shard_map/ppermute | solution.py:50
  48.3 3.9 %collective-permute-done.2 = bf16[16,7168]{1,0:T(8,128)(2,1)S(1)} collective-permute-done((bf16[16,7168]{1,0:T(8,128)(2,1)S(1)}, bf16[16,7168]{1,0:T(8,128)(2,1)S(1)}, u32[]{:S(2)}, u32[]{:S(2)}) %collective-permute-start.2) | collective-permute-done | bytes 229408 | tf_op jit(solution)/shard_map/ppermute | solution.py:50
  52.3 3.6 %collective-permute-start.8 = (bf16[16,7168]{1,0:T(8,128)(2,1)S(1)}, bf16[16,7168]{1,0:T(8,128)(2,1)S(1)}, u32[]{:S(2)}, u32[]{:S(2)}) collective-permute-start(bf16[16,7168]{1,0:T(8,128)(2,1)S(1)} %add_convert_fusion.8), channel_id=1, source_target_pairs={{0,14},{2,0},{4,2},{6,4},{8,6},{10,8},{12,10},{14,12},{1,15},{3,1}... | collective-permute-start | bytes 688136 | tf_op jit(solution)/shard_map/ppermute | solution.py:50
  55.9 4.4 %collective-permute-done.8 = bf16[16,7168]{1,0:T(8,128)(2,1)S(1)} collective-permute-done((bf16[16,7168]{1,0:T(8,128)(2,1)S(1)}, bf16[16,7168]{1,0:T(8,128)(2,1)S(1)}, u32[]{:S(2)}, u32[]{:S(2)}) %collective-permute-start.8) | collective-permute-done | bytes 229408 | tf_op jit(solution)/shard_map/ppermute | solution.py:50
  60.6 3.8 %collective-permute-start.9 = (bf16[16,7168]{1,0:T(8,128)(2,1)S(1)}, bf16[16,7168]{1,0:T(8,128)(2,1)S(1)}, u32[]{:S(2)}, u32[]{:S(2)}) collective-permute-start(bf16[16,7168]{1,0:T(8,128)(2,1)S(1)} %get-tuple-element.43), channel_id=1, source_target_pairs={{0,14},{2,0},{4,2},{6,4},{8,6},{10,8},{12,10},{14,12},{1,15},{3,1}... | collective-permute-start | bytes 688136 | tf_op jit(solution)/shard_map/ppermute | solution.py:50
  64.4 5.8 %collective-permute-done.6 = bf16[16,7168]{1,0:T(8,128)(2,1)S(1)} collective-permute-done((bf16[16,7168]{1,0:T(8,128)(2,1)S(1)}, bf16[16,7168]{1,0:T(8,128)(2,1)S(1)}, u32[]{:S(2)}, u32[]{:S(2)}) %collective-permute-start.6) | collective-permute-done | bytes 229408 | tf_op jit(solution)/shard_map/ppermute | solution.py:50
  70.2 0.3 collective-permute-start.7
  70.7 7.0 %collective-permute-done.7 = bf16[16,7168]{1,0:T(8,128)(2,1)S(1)} collective-permute-done((bf16[16,7168]{1,0:T(8,128)(2,1)S(1)}, bf16[16,7168]{1,0:T(8,128)(2,1)S(1)}, u32[]{:S(2)}, u32[]{:S(2)}) %collective-permute-start.7) | collective-permute-done | bytes 229408 | tf_op jit(solution)/shard_map/ppermute | solution.py:50
  78.0 7.5 %collective-permute-done.11 = bf16[16,7168]{1,0:T(8,128)(2,1)S(1)} collective-permute-done((bf16[16,7168]{1,0:T(8,128)(2,1)S(1)}, bf16[16,7168]{1,0:T(8,128)(2,1)S(1)}, u32[]{:S(2)}, u32[]{:S(2)}) %collective-permute-start.11) | collective-permute-done | bytes 229408 | tf_op jit(solution)/shard_map/ppermute | solution.py:46
  85.5 0.2 multiply_reduce_fusion
  85.9 3.2 %collective-permute-start.12 = (bf16[16,7168]{1,0:T(8,128)(2,1)S(1)}, bf16[16,7168]{1,0:T(8,128)(2,1)S(1)}, u32[]{:S(2)}, u32[]{:S(2)}) collective-permute-start(bf16[16,7168]{1,0:T(8,128)(2,1)S(1)} %multiply_convert_fusion.refs_0_), channel_id=1, source_target_pairs={{0,14},{2,0},{4,2},{6,4},{8,6},{10,8},{12,10},{14,12},{1,15},{3,1}... | collective-permute-start | bytes 688136 | tf_op jit(solution)/shard_map/ppermute | solution.py:50
  89.2 4.0 %collective-permute-done.15.refs_8_ = bf16[16,7168]{1,0:T(8,128)(2,1)S(1)} collective-permute-done((bf16[16,7168]{1,0:T(8,128)(2,1)S(1)}, bf16[16,7168]{1,0:T(8,128)(2,1)S(1)}, u32[]{:S(2)}, u32[]{:S(2)}) %collective-permute-start.15) | collective-permute-done | bytes 229408 | tf_op jit(solution)/shard_map/ppermute | solution.py:50
  93.2 3.2 %collective-permute-start.13 = (bf16[16,7168]{1,0:T(8,128)(2,1)S(1)}, bf16[16,7168]{1,0:T(8,128)(2,1)S(1)}, u32[]{:S(2)}, u32[]{:S(2)}) collective-permute-start(bf16[16,7168]{1,0:T(8,128)(2,1)S(1)} %collective-permute-done.12.refs_1_), channel_id=1, source_target_pairs={{0,14},{2,0},{4,2},{6,4},{8,6},{10,8},{12,10},{14,12},{1,15},{3,1}... | collective-permute-start | bytes 688136 | tf_op jit(solution)/shard_map/ppermute | solution.py:50
  96.4 0.5 collective-permute-start.21
  97.0 3.4 %collective-permute-done.16.refs_7_ = bf16[16,7168]{1,0:T(8,128)(2,1)S(1)} collective-permute-done((bf16[16,7168]{1,0:T(8,128)(2,1)S(1)}, bf16[16,7168]{1,0:T(8,128)(2,1)S(1)}, u32[]{:S(2)}, u32[]{:S(2)}) %collective-permute-start.16) | collective-permute-done | bytes 229408 | tf_op jit(solution)/shard_map/ppermute | solution.py:50
  100.4 3.2 %collective-permute-start.14 = (bf16[16,7168]{1,0:T(8,128)(2,1)S(1)}, bf16[16,7168]{1,0:T(8,128)(2,1)S(1)}, u32[]{:S(2)}, u32[]{:S(2)}) collective-permute-start(bf16[16,7168]{1,0:T(8,128)(2,1)S(1)} %collective-permute-done.13.refs_2_), channel_id=1, source_target_pairs={{0,14},{2,0},{4,2},{6,4},{8,6},{10,8},{12,10},{14,12},{1,15},{3,1}... | collective-permute-start | bytes 688136 | tf_op jit(solution)/shard_map/ppermute | solution.py:50
  103.6 0.2 add_convert_fusion
  103.8 3.9 %collective-permute-done.17.refs_6_ = bf16[16,7168]{1,0:T(8,128)(2,1)S(1)} collective-permute-done((bf16[16,7168]{1,0:T(8,128)(2,1)S(1)}, bf16[16,7168]{1,0:T(8,128)(2,1)S(1)}, u32[]{:S(2)}, u32[]{:S(2)}) %collective-permute-start.17) | collective-permute-done | bytes 229408 | tf_op jit(solution)/shard_map/ppermute | solution.py:50
  107.9 3.5 %collective-permute-start.19 = (bf16[16,3584]{1,0:T(8,128)(2,1)S(1)}, bf16[16,3584]{1,0:T(8,128)(2,1)S(1)}, u32[]{:S(2)}, u32[]{:S(2)}) collective-permute-start(bf16[16,3584]{1,0:T(8,128)(2,1)S(1)} %slice.204), channel_id=1, source_target_pairs={{0,14},{2,0},{4,2},{6,4},{8,6},{10,8},{12,10},{14,12},{1,15},{3,1}... | collective-permute-start | bytes 344072 | tf_op jit(solution)/shard_map/ppermute | solution.py:50
  111.5 2.4 %collective-permute-done.18.refs_4_ = bf16[16,3584]{1,0:T(8,128)(2,1)S(1)} collective-permute-done((bf16[16,3584]{1,0:T(8,128)(2,1)S(1)}, bf16[16,3584]{1,0:T(8,128)(2,1)S(1)}, u32[]{:S(2)}, u32[]{:S(2)}) %collective-permute-start.18) | collective-permute-done | bytes 114720 | tf_op jit(solution)/shard_map/ppermute | solution.py:50
  113.9 4.3 %expert.1 = bf16[128,7168]{1,0:T(8,128)(2,1)S(1)} custom-call(bf16[16,7168]{1,0:T(8,128)(2,1)S(1)} %multiply_convert_fusion.refs_0_, bf16[16,7168]{1,0:T(8,128)(2,1)S(1)} %collective-permute-done.12.refs_1_, bf16[16,7168]{1,0:T(8,128)(2,1)S(1)} %collective-permute-done.13.refs_2_, bf16[16,7168]{1,0:T(8,128)(2,1)S(1)} %collective-permute-done.14.refs_3_, ...), custom_call_target="tpu_custom_call" | custom-call | tf_op jit(solution)/shard_map/expert/pallas_call | solution.py:185
  118.4 3.6 %collective-permute-start.27 = (bf16[24,3584]{1,0:T(8,128)(2,1)S(1)}, bf16[24,3584]{1,0:T(8,128)(2,1)S(1)}, u32[]{:S(2)}, u32[]{:S(2)}) collective-permute-start(bf16[24,3584]{1,0:T(8,128)(2,1)S(1)} %get-tuple-element.64), channel_id=1, source_target_pairs={{0,14},{2,0},{4,2},{6,4},{8,6},{10,8},{12,10},{14,12},{1,15},{3,1}... | collective-permute-start | bytes 516104 | tf_op jit(solution)/shard_map/ppermute | solution.py:50
  122.0 4.7 %collective-permute-done.27 = bf16[24,3584]{1,0:T(8,128)(2,1)S(1)} collective-permute-done((bf16[24,3584]{1,0:T(8,128)(2,1)S(1)}, bf16[24,3584]{1,0:T(8,128)(2,1)S(1)}, u32[]{:S(2)}, u32[]{:S(2)}) %collective-permute-start.27) | collective-permute-done | bytes 172064 | tf_op jit(solution)/shard_map/ppermute | solution.py:50
  126.8 3.8 %collective-permute-start.28 = (bf16[24,7168]{1,0:T(8,128)(2,1)S(1)}, bf16[24,7168]{1,0:T(8,128)(2,1)S(1)}, u32[]{:S(2)}, u32[]{:S(2)}) collective-permute-start(bf16[24,7168]{1,0:T(8,128)(2,1)S(1)} %pad_maximum_fusion), channel_id=1, source_target_pairs={{0,14},{2,0},{4,2},{6,4},{8,6},{10,8},{12,10},{14,12},{1,15},{3,1}... | collective-permute-start | bytes 1032200 | tf_op jit(solution)/shard_map/ppermute | solution.py:50
  130.8 8.2 %collective-permute-done.28 = bf16[24,7168]{1,0:T(8,128)(2,1)S(1)} collective-permute-done((bf16[24,7168]{1,0:T(8,128)(2,1)S(1)}, bf16[24,7168]{1,0:T(8,128)(2,1)S(1)}, u32[]{:S(2)}, u32[]{:S(2)}) %collective-permute-start.28) | collective-permute-done | bytes 344096 | tf_op jit(solution)/shard_map/ppermute | solution.py:50
  139.0 3.8 %collective-permute-start.29 = (bf16[24,7168]{1,0:T(8,128)(2,1)S(1)}, bf16[24,7168]{1,0:T(8,128)(2,1)S(1)}, u32[]{:S(2)}, u32[]{:S(2)}) collective-permute-start(bf16[24,7168]{1,0:T(8,128)(2,1)S(1)} %add_convert_fusion.3), channel_id=1, source_target_pairs={{0,14},{2,0},{4,2},{6,4},{8,6},{10,8},{12,10},{14,12},{1,15},{3,1}... | collective-permute-start | bytes 1032200 | tf_op jit(solution)/shard_map/ppermute | solution.py:50
  143.0 7.3 %collective-permute-done.29 = bf16[24,7168]{1,0:T(8,128)(2,1)S(1)} collective-permute-done((bf16[24,7168]{1,0:T(8,128)(2,1)S(1)}, bf16[24,7168]{1,0:T(8,128)(2,1)S(1)}, u32[]{:S(2)}, u32[]{:S(2)}) %collective-permute-start.29) | collective-permute-done | bytes 344096 | tf_op jit(solution)/shard_map/ppermute | solution.py:50
  150.4 3.8 %collective-permute-start.30 = (bf16[24,7168]{1,0:T(8,128)(2,1)S(1)}, bf16[24,7168]{1,0:T(8,128)(2,1)S(1)}, u32[]{:S(2)}, u32[]{:S(2)}) collective-permute-start(bf16[24,7168]{1,0:T(8,128)(2,1)S(1)} %add_convert_fusion.2), channel_id=1, source_target_pairs={{0,14},{2,0},{4,2},{6,4},{8,6},{10,8},{12,10},{14,12},{1,15},{3,1}... | collective-permute-start | bytes 1032200 | tf_op jit(solution)/shard_map/ppermute | solution.py:50
  154.3 4.6 %collective-permute-done.30 = bf16[24,7168]{1,0:T(8,128)(2,1)S(1)} collective-permute-done((bf16[24,7168]{1,0:T(8,128)(2,1)S(1)}, bf16[24,7168]{1,0:T(8,128)(2,1)S(1)}, u32[]{:S(2)}, u32[]{:S(2)}) %collective-permute-start.30) | collective-permute-done | bytes 344096 | tf_op jit(solution)/shard_map/ppermute | solution.py:50
  158.9 3.9 %collective-permute-done.26 = bf16[24,7168]{1,0:T(8,128)(2,1)S(1)} collective-permute-done((bf16[24,7168]{1,0:T(8,128)(2,1)S(1)}, bf16[24,7168]{1,0:T(8,128)(2,1)S(1)}, u32[]{:S(2)}, u32[]{:S(2)}) %collective-permute-start.26) | collective-permute-done | bytes 344096 | tf_op jit(solution)/shard_map/ppermute | solution.py:50
  163.1 6.2 %collective-permute-done.31 = bf16[8,7168]{1,0:T(8,128)(2,1)S(1)} collective-permute-done((bf16[8,7168]{1,0:T(8,128)(2,1)S(1)}, bf16[8,7168]{1,0:T(8,128)(2,1)S(1)}, u32[]{:S(2)}, u32[]{:S(2)}) %collective-permute-start.31) | collective-permute-done | bytes 114720 | tf_op jit(solution)/shard_map/ppermute | solution.py:46
  169.4 1.0 convolution_convert_fusion.1
  (86 shorter events, 3.5 us)
Async XLA Ops:
  0.0 3.8 %copy-start = (bf16[16,128,256]{2,1,0:T(8,128)(2,1)S(1)}, bf16[16,128,256]{2,1,0:T(8,128)(2,1)}, u32[]{:S(2)}) copy-start(bf16[16,128,256]{2,1,0:T(8,128)(2,1)} %param.13) | copy-start | bytes 3145732
  0.0 30.7 %collective-permute-start = (bf16[256,7168]{1,0:T(8,128)(2,1)}, bf16[256,7168]{1,0:T(8,128)(2,1)}, u32[]{:S(2)}, u32[]{:S(2)}) collective-permute-start(bf16[256,7168]{1,0:T(8,128)(2,1)} %w_own.1), channel_id=1, source_target_pairs={{0,1},{1,0},{2,3},{3,2},{4,5},{5,4},{6,7},{7,6},{8,9},{9,8},{10,11... | collective-permute-start | bytes 11010056 | tf_op jit(solution)/shard_map/ppermute | solution.py:42
  1.8 3.1 %copy-start.5 = (f32[16,3]{0,1:T(4,128)S(1)}, f32[16,3]{0,1:T(4,128)}, u32[]{:S(2)}) copy-start(f32[16,3]{0,1:T(4,128)} %param.18) | copy-start | bytes 580
  1.8 3.1 %copy-start.6 = (s32[16,3]{0,1:T(4,128)S(1)}, s32[16,3]{0,1:T(4,128)}, u32[]{:S(2)}) copy-start(s32[16,3]{0,1:T(4,128)} %param.17) | copy-start | bytes 580
  7.5 23.2 %all-to-all-start = ((bf16[1,16,16,512]{3,1,0,2:T(8,128)(2,1)}), bf16[1,16,16,512]{3,1,0,2:T(8,128)(2,1)S(1)}, u32[]{:S(2)}, u32[]{:S(2)}) async-start(bf16[1,16,16,512]{3,1,0,2:T(8,128)(2,1)} %copy.14), calls=%async_computation | async-start | bytes 524288 | tf_op jit(solution)/shard_map/all_to_all | solution.py:229
  35.7 5.5 %collective-permute-start.3 = (bf16[16,3584]{1,0:T(8,128)(2,1)S(1)}, bf16[16,3584]{1,0:T(8,128)(2,1)S(1)}, u32[]{:S(2)}, u32[]{:S(2)}) collective-permute-start(bf16[16,3584]{1,0:T(8,128)(2,1)S(1)} %get-tuple-element.46), channel_id=1, source_target_pairs={{0,14},{2,0},{4,2},{6,4},{8,6},{10,8},{12,10},{14,12},{1,15},{3,1}... | collective-permute-start | bytes 344072 | tf_op jit(solution)/shard_map/ppermute | solution.py:50
  38.8 6.0 %collective-permute-start.1 = (bf16[16,3584]{1,0:T(8,128)(2,1)S(1)}, bf16[16,3584]{1,0:T(8,128)(2,1)S(1)}, u32[]{:S(2)}, u32[]{:S(2)}) collective-permute-start(bf16[16,3584]{1,0:T(8,128)(2,1)S(1)} %get-tuple-element.48), channel_id=1, source_target_pairs={{0,2},{2,4},{4,6},{6,8},{8,10},{10,12},{12,14},{14,0},{1,3},{3,5},... | collective-permute-start | bytes 344072 | tf_op jit(solution)/shard_map/ppermute | solution.py:50
  38.9 13.3 %collective-permute-start.5 = (bf16[32,7168]{1,0:T(8,128)(2,1)S(1)}, bf16[32,7168]{1,0:T(8,128)(2,1)S(1)}, u32[]{:S(2)}, u32[]{:S(2)}) collective-permute-start(bf16[32,7168]{1,0:T(8,128)(2,1)S(1)} %get-tuple-element.60), channel_id=1, source_target_pairs={{0,16},{16,0},{1,17},{17,1},{2,18},{18,2},{3,19},{19,3},{4,20},{20... | collective-permute-start | bytes 1376264 | tf_op jit(solution)/shard_map/ppermute | solution.py:46
  44.9 25.7 %copy-start.4 = (bf16[16,7168]{1,0:T(8,128)(2,1)S(1)}, bf16[16,7168]{1,0:T(8,128)(2,1)}, u32[]{:S(2)}) copy-start(bf16[16,7168]{1,0:T(8,128)(2,1)} %param.16) | copy-start | bytes 688132
  44.9 7.3 %collective-permute-start.2 = (bf16[16,7168]{1,0:T(8,128)(2,1)S(1)}, bf16[16,7168]{1,0:T(8,128)(2,1)S(1)}, u32[]{:S(2)}, u32[]{:S(2)}) collective-permute-start(bf16[16,7168]{1,0:T(8,128)(2,1)S(1)} %pad_maximum_fusion.1), channel_id=1, source_target_pairs={{0,2},{2,4},{4,6},{6,8},{8,10},{10,12},{12,14},{14,0},{1,3},{3,5},... | collective-permute-start | bytes 688136 | tf_op jit(solution)/shard_map/ppermute | solution.py:50
  45.0 7.2 %collective-permute-start.4 = (bf16[16,7168]{1,0:T(8,128)(2,1)S(1)}, bf16[16,7168]{1,0:T(8,128)(2,1)S(1)}, u32[]{:S(2)}, u32[]{:S(2)}) collective-permute-start(bf16[16,7168]{1,0:T(8,128)(2,1)S(1)} %pad_maximum_fusion.2), channel_id=1, source_target_pairs={{0,14},{2,0},{4,2},{6,4},{8,6},{10,8},{12,10},{14,12},{1,15},{3,1}... | collective-permute-start | bytes 688136 | tf_op jit(solution)/shard_map/ppermute | solution.py:50
  52.2 44.7 %copy-start.3 = (bf16[160,7168]{1,0:T(8,128)(2,1)S(1)}, bf16[160,7168]{1,0:T(8,128)(2,1)}, u32[]{:S(2)}) copy-start(bf16[160,7168]{1,0:T(8,128)(2,1)} %refs_13_) | copy-start | bytes 6881284
  52.3 8.1 %collective-permute-start.8 = (bf16[16,7168]{1,0:T(8,128)(2,1)S(1)}, bf16[16,7168]{1,0:T(8,128)(2,1)S(1)}, u32[]{:S(2)}, u32[]{:S(2)}) collective-permute-start(bf16[16,7168]{1,0:T(8,128)(2,1)S(1)} %add_convert_fusion.8), channel_id=1, source_target_pairs={{0,14},{2,0},{4,2},{6,4},{8,6},{10,8},{12,10},{14,12},{1,15},{3,1}... | collective-permute-start | bytes 688136 | tf_op jit(solution)/shard_map/ppermute | solution.py:50
  60.4 9.7 %collective-permute-start.6 = (bf16[16,7168]{1,0:T(8,128)(2,1)S(1)}, bf16[16,7168]{1,0:T(8,128)(2,1)S(1)}, u32[]{:S(2)}, u32[]{:S(2)}) collective-permute-start(bf16[16,7168]{1,0:T(8,128)(2,1)S(1)} %get-tuple-element.44), channel_id=1, source_target_pairs={{0,2},{2,4},{4,6},{6,8},{8,10},{10,12},{12,14},{14,0},{1,3},{3,5},... | collective-permute-start | bytes 688136 | tf_op jit(solution)/shard_map/ppermute | solution.py:50
  60.5 10.2 %collective-permute-start.10 = (bf16[32,7168]{1,0:T(8,128)(2,1)S(1)}, bf16[32,7168]{1,0:T(8,128)(2,1)S(1)}, u32[]{:S(2)}, u32[]{:S(2)}) collective-permute-start(bf16[32,7168]{1,0:T(8,128)(2,1)S(1)} %get-tuple-element.59), channel_id=1, source_target_pairs={{0,16},{16,0},{1,17},{17,1},{2,18},{18,2},{3,19},{19,3},{4,20},{20... | collective-permute-start | bytes 1376264 | tf_op jit(solution)/shard_map/ppermute | solution.py:46
  60.6 10.1 %collective-permute-start.9 = (bf16[16,7168]{1,0:T(8,128)(2,1)S(1)}, bf16[16,7168]{1,0:T(8,128)(2,1)S(1)}, u32[]{:S(2)}, u32[]{:S(2)}) collective-permute-start(bf16[16,7168]{1,0:T(8,128)(2,1)S(1)} %get-tuple-element.43), channel_id=1, source_target_pairs={{0,14},{2,0},{4,2},{6,4},{8,6},{10,8},{12,10},{14,12},{1,15},{3,1}... | collective-permute-start | bytes 688136 | tf_op jit(solution)/shard_map/ppermute | solution.py:50
  70.2 26.2 %copy-start.2 = (bf16[160,7168]{1,0:T(8,128)(2,1)S(1)}, bf16[160,7168]{1,0:T(8,128)(2,1)}, u32[]{:S(2)}) copy-start(bf16[160,7168]{1,0:T(8,128)(2,1)} %refs_11_) | copy-start | bytes 6881284
  70.2 7.5 %collective-permute-start.7 = (bf16[16,7168]{1,0:T(8,128)(2,1)S(1)}, bf16[16,7168]{1,0:T(8,128)(2,1)S(1)}, u32[]{:S(2)}, u32[]{:S(2)}) collective-permute-start(bf16[16,7168]{1,0:T(8,128)(2,1)S(1)} %add_convert_fusion.9), channel_id=1, source_target_pairs={{0,2},{2,4},{4,6},{6,8},{8,10},{10,12},{12,14},{14,0},{1,3},{3,5},... | collective-permute-start | bytes 688136 | tf_op jit(solution)/shard_map/ppermute | solution.py:50
  70.7 25.7 %copy-start.1 = (bf16[160,7168]{1,0:T(8,128)(2,1)S(1)}, bf16[160,7168]{1,0:T(8,128)(2,1)}, u32[]{:S(2)}) copy-start(bf16[160,7168]{1,0:T(8,128)(2,1)} %refs_9_) | copy-start | bytes 6881284
  77.9 7.6 %collective-permute-start.11 = (bf16[16,7168]{1,0:T(8,128)(2,1)S(1)}, bf16[16,7168]{1,0:T(8,128)(2,1)S(1)}, u32[]{:S(2)}, u32[]{:S(2)}) collective-permute-start(bf16[16,7168]{1,0:T(8,128)(2,1)S(1)} %pad_maximum_fusion.3), channel_id=1, source_target_pairs={{0,16},{16,0},{1,17},{17,1},{2,18},{18,2},{3,19},{19,3},{4,20},{20... | collective-permute-start | bytes 688136 | tf_op jit(solution)/shard_map/ppermute | solution.py:46
  85.8 7.3 %collective-permute-start.15 = (bf16[16,7168]{1,0:T(8,128)(2,1)S(1)}, bf16[16,7168]{1,0:T(8,128)(2,1)S(1)}, u32[]{:S(2)}, u32[]{:S(2)}) collective-permute-start(bf16[16,7168]{1,0:T(8,128)(2,1)S(1)} %multiply_convert_fusion.refs_0_), channel_id=1, source_target_pairs={{0,2},{2,4},{4,6},{6,8},{8,10},{10,12},{12,14},{14,0},{1,3},{3,5},... | collective-permute-start | bytes 688136 | tf_op jit(solution)/shard_map/ppermute | solution.py:50
  85.9 7.2 %collective-permute-start.12 = (bf16[16,7168]{1,0:T(8,128)(2,1)S(1)}, bf16[16,7168]{1,0:T(8,128)(2,1)S(1)}, u32[]{:S(2)}, u32[]{:S(2)}) collective-permute-start(bf16[16,7168]{1,0:T(8,128)(2,1)S(1)} %multiply_convert_fusion.refs_0_), channel_id=1, source_target_pairs={{0,14},{2,0},{4,2},{6,4},{8,6},{10,8},{12,10},{14,12},{1,15},{3,1}... | collective-permute-start | bytes 688136 | tf_op jit(solution)/shard_map/ppermute | solution.py:50
  93.2 7.2 %collective-permute-start.16 = (bf16[16,7168]{1,0:T(8,128)(2,1)S(1)}, bf16[16,7168]{1,0:T(8,128)(2,1)S(1)}, u32[]{:S(2)}, u32[]{:S(2)}) collective-permute-start(bf16[16,7168]{1,0:T(8,128)(2,1)S(1)} %collective-permute-done.15.refs_8_), channel_id=1, source_target_pairs={{0,2},{2,4},{4,6},{6,8},{8,10},{10,12},{12,14},{14,0},{1,3},{3,5},... | collective-permute-start | bytes 688136 | tf_op jit(solution)/shard_map/ppermute | solution.py:50
  93.2 7.2 %collective-permute-start.13 = (bf16[16,7168]{1,0:T(8,128)(2,1)S(1)}, bf16[16,7168]{1,0:T(8,128)(2,1)S(1)}, u32[]{:S(2)}, u32[]{:S(2)}) collective-permute-start(bf16[16,7168]{1,0:T(8,128)(2,1)S(1)} %collective-permute-done.12.refs_1_), channel_id=1, source_target_pairs={{0,14},{2,0},{4,2},{6,4},{8,6},{10,8},{12,10},{14,12},{1,15},{3,1}... | collective-permute-start | bytes 688136 | tf_op jit(solution)/shard_map/ppermute | solution.py:50
  96.4 17.5 %collective-permute-start.20 = (bf16[160,7168]{1,0:T(8,128)(2,1)S(1)}, bf16[160,7168]{1,0:T(8,128)(2,1)S(1)}, u32[]{:S(2)}, u32[]{:S(2)}) collective-permute-start(bf16[160,7168]{1,0:T(8,128)(2,1)S(1)} %copy-done.1), channel_id=1, source_target_pairs={{0,1},{1,0},{2,3},{3,2},{4,5},{5,4},{6,7},{7,6},{8,9},{9,8},{10,11... | collective-permute-start | bytes 6881288 | tf_op jit(solution)/shard_map/ppermute | solution.py:42
  96.4 17.5 %collective-permute-start.21 = (bf16[160,7168]{1,0:T(8,128)(2,1)S(1)}, bf16[160,7168]{1,0:T(8,128)(2,1)S(1)}, u32[]{:S(2)}, u32[]{:S(2)}) collective-permute-start(bf16[160,7168]{1,0:T(8,128)(2,1)S(1)} %copy-done.2), channel_id=1, source_target_pairs={{0,1},{1,0},{2,3},{3,2},{4,5},{5,4},{6,7},{7,6},{8,9},{9,8},{10,11... | collective-permute-start | bytes 6881288 | tf_op jit(solution)/shard_map/ppermute | solution.py:42
  96.9 17.0 %collective-permute-start.22 = (bf16[160,7168]{1,0:T(8,128)(2,1)S(1)}, bf16[160,7168]{1,0:T(8,128)(2,1)S(1)}, u32[]{:S(2)}, u32[]{:S(2)}) collective-permute-start(bf16[160,7168]{1,0:T(8,128)(2,1)S(1)} %copy-done.3), channel_id=1, source_target_pairs={{0,1},{1,0},{2,3},{3,2},{4,5},{5,4},{6,7},{7,6},{8,9},{9,8},{10,11... | collective-permute-start | bytes 6881288 | tf_op jit(solution)/shard_map/ppermute | solution.py:42
  100.4 7.4 %collective-permute-start.17 = (bf16[16,7168]{1,0:T(8,128)(2,1)S(1)}, bf16[16,7168]{1,0:T(8,128)(2,1)S(1)}, u32[]{:S(2)}, u32[]{:S(2)}) collective-permute-start(bf16[16,7168]{1,0:T(8,128)(2,1)S(1)} %collective-permute-done.16.refs_7_), channel_id=1, source_target_pairs={{0,2},{2,4},{4,6},{6,8},{8,10},{10,12},{12,14},{14,0},{1,3},{3,5},... | collective-permute-start | bytes 688136 | tf_op jit(solution)/shard_map/ppermute | solution.py:50
  100.4 7.5 %collective-permute-start.14 = (bf16[16,7168]{1,0:T(8,128)(2,1)S(1)}, bf16[16,7168]{1,0:T(8,128)(2,1)S(1)}, u32[]{:S(2)}, u32[]{:S(2)}) collective-permute-start(bf16[16,7168]{1,0:T(8,128)(2,1)S(1)} %collective-permute-done.13.refs_2_), channel_id=1, source_target_pairs={{0,14},{2,0},{4,2},{6,4},{8,6},{10,8},{12,10},{14,12},{1,15},{3,1}... | collective-permute-start | bytes 688136 | tf_op jit(solution)/shard_map/ppermute | solution.py:50
  107.8 6.1 %collective-permute-start.18 = (bf16[16,3584]{1,0:T(8,128)(2,1)S(1)}, bf16[16,3584]{1,0:T(8,128)(2,1)S(1)}, u32[]{:S(2)}, u32[]{:S(2)}) collective-permute-start(bf16[16,3584]{1,0:T(8,128)(2,1)S(1)} %slice.203), channel_id=1, source_target_pairs={{0,2},{2,4},{4,6},{6,8},{8,10},{10,12},{12,14},{14,0},{1,3},{3,5},... | collective-permute-start | bytes 344072 | tf_op jit(solution)/shard_map/ppermute | solution.py:50
  107.9 6.0 %collective-permute-start.19 = (bf16[16,3584]{1,0:T(8,128)(2,1)S(1)}, bf16[16,3584]{1,0:T(8,128)(2,1)S(1)}, u32[]{:S(2)}, u32[]{:S(2)}) collective-permute-start(bf16[16,3584]{1,0:T(8,128)(2,1)S(1)} %slice.204), channel_id=1, source_target_pairs={{0,14},{2,0},{4,2},{6,4},{8,6},{10,8},{12,10},{14,12},{1,15},{3,1}... | collective-permute-start | bytes 344072 | tf_op jit(solution)/shard_map/ppermute | solution.py:50
  118.3 12.3 %collective-permute-start.23 = (bf16[24,3584]{1,0:T(8,128)(2,1)S(1)}, bf16[24,3584]{1,0:T(8,128)(2,1)S(1)}, u32[]{:S(2)}, u32[]{:S(2)}) collective-permute-start(bf16[24,3584]{1,0:T(8,128)(2,1)S(1)} %get-tuple-element.63), channel_id=1, source_target_pairs={{0,2},{2,4},{4,6},{6,8},{8,10},{10,12},{12,14},{14,0},{1,3},{3,5},... | collective-permute-start | bytes 516104 | tf_op jit(solution)/shard_map/ppermute | solution.py:50
  118.4 8.4 %collective-permute-start.27 = (bf16[24,3584]{1,0:T(8,128)(2,1)S(1)}, bf16[24,3584]{1,0:T(8,128)(2,1)S(1)}, u32[]{:S(2)}, u32[]{:S(2)}) collective-permute-start(bf16[24,3584]{1,0:T(8,128)(2,1)S(1)} %get-tuple-element.64), channel_id=1, source_target_pairs={{0,14},{2,0},{4,2},{6,4},{8,6},{10,8},{12,10},{14,12},{1,15},{3,1}... | collective-permute-start | bytes 516104 | tf_op jit(solution)/shard_map/ppermute | solution.py:50
  126.8 12.1 %collective-permute-start.28 = (bf16[24,7168]{1,0:T(8,128)(2,1)S(1)}, bf16[24,7168]{1,0:T(8,128)(2,1)S(1)}, u32[]{:S(2)}, u32[]{:S(2)}) collective-permute-start(bf16[24,7168]{1,0:T(8,128)(2,1)S(1)} %pad_maximum_fusion), channel_id=1, source_target_pairs={{0,14},{2,0},{4,2},{6,4},{8,6},{10,8},{12,10},{14,12},{1,15},{3,1}... | collective-permute-start | bytes 1032200 | tf_op jit(solution)/shard_map/ppermute | solution.py:50
  130.7 12.1 %collective-permute-start.24 = (bf16[24,7168]{1,0:T(8,128)(2,1)S(1)}, bf16[24,7168]{1,0:T(8,128)(2,1)S(1)}, u32[]{:S(2)}, u32[]{:S(2)}) collective-permute-start(bf16[24,7168]{1,0:T(8,128)(2,1)S(1)} %fusion.7), channel_id=1, source_target_pairs={{0,2},{2,4},{4,6},{6,8},{8,10},{10,12},{12,14},{14,0},{1,3},{3,5},... | collective-permute-start | bytes 1032200 | tf_op jit(solution)/shard_map/ppermute | solution.py:50
  139.0 11.3 %collective-permute-start.29 = (bf16[24,7168]{1,0:T(8,128)(2,1)S(1)}, bf16[24,7168]{1,0:T(8,128)(2,1)S(1)}, u32[]{:S(2)}, u32[]{:S(2)}) collective-permute-start(bf16[24,7168]{1,0:T(8,128)(2,1)S(1)} %add_convert_fusion.3), channel_id=1, source_target_pairs={{0,14},{2,0},{4,2},{6,4},{8,6},{10,8},{12,10},{14,12},{1,15},{3,1}... | collective-permute-start | bytes 1032200 | tf_op jit(solution)/shard_map/ppermute | solution.py:50
  142.9 11.2 %collective-permute-start.25 = (bf16[24,7168]{1,0:T(8,128)(2,1)S(1)}, bf16[24,7168]{1,0:T(8,128)(2,1)S(1)}, u32[]{:S(2)}, u32[]{:S(2)}) collective-permute-start(bf16[24,7168]{1,0:T(8,128)(2,1)S(1)} %add_convert_fusion.5), channel_id=1, source_target_pairs={{0,2},{2,4},{4,6},{6,8},{8,10},{10,12},{12,14},{14,0},{1,3},{3,5},... | collective-permute-start | bytes 1032200 | tf_op jit(solution)/shard_map/ppermute | solution.py:50
  150.4 8.5 %collective-permute-start.30 = (bf16[24,7168]{1,0:T(8,128)(2,1)S(1)}, bf16[24,7168]{1,0:T(8,128)(2,1)S(1)}, u32[]{:S(2)}, u32[]{:S(2)}) collective-permute-start(bf16[24,7168]{1,0:T(8,128)(2,1)S(1)} %add_convert_fusion.2), channel_id=1, source_target_pairs={{0,14},{2,0},{4,2},{6,4},{8,6},{10,8},{12,10},{14,12},{1,15},{3,1}... | collective-permute-start | bytes 1032200 | tf_op jit(solution)/shard_map/ppermute | solution.py:50
  154.2 8.5 %collective-permute-start.26 = (bf16[24,7168]{1,0:T(8,128)(2,1)S(1)}, bf16[24,7168]{1,0:T(8,128)(2,1)S(1)}, u32[]{:S(2)}, u32[]{:S(2)}) collective-permute-start(bf16[24,7168]{1,0:T(8,128)(2,1)S(1)} %add_convert_fusion.4), channel_id=1, source_target_pairs={{0,2},{2,4},{4,6},{6,8},{8,10},{10,12},{12,14},{14,0},{1,3},{3,5},... | collective-permute-start | bytes 1032200 | tf_op jit(solution)/shard_map/ppermute | solution.py:50
  162.9 6.4 %collective-permute-start.31 = (bf16[8,7168]{1,0:T(8,128)(2,1)S(1)}, bf16[8,7168]{1,0:T(8,128)(2,1)S(1)}, u32[]{:S(2)}, u32[]{:S(2)}) collective-permute-start(bf16[8,7168]{1,0:T(8,128)(2,1)S(1)} %slice.228), channel_id=1, source_target_pairs={{0,16},{16,0},{1,17},{17,1},{2,18},{18,2},{3,19},{19,3},{4,20},{20... | collective-permute-start | bytes 344072 | tf_op jit(solution)/shard_map/ppermute | solution.py:46
